TPU v7x, 128 devices: a whole 4x4x4 slice. The times are simulated.
128 devices in a mesh: comm: 16 (over z, y), inner: 8 (over x, core).
Axes of the slice: x: 4, y: 4, z: 4, core: 2. Of those that a mesh axis runs over, the one named last changes fastest.
Arguments:
- vec_x: bfloat16 [32, 524288], P(None, ('comm', 'inner')), may hold values from -8 to 8
- vec_p: bfloat16 [32, 524288], P(None, ('comm', 'inner')), may hold values from -3 to 3
- diag_shift: float32 [524288], P(('comm', 'inner')), may hold values from 0.5 to 4
- tiles: bfloat16 [24576, 256, 256], P(('comm', 'inner')), may hold values from 0 to 0.125
- tile_row: int32 [24576], P(('comm', 'inner')), may hold values from 0 to 15
- tile_col: int32 [24576], P(('comm', 'inner')), may hold values from 0 to 207
- tile_count: int32 [128], P(('comm', 'inner')), may hold values from 96 to 192, as said below
- send_near: int32 [128, 8, 8], P(('comm', 'inner')), may hold values from 0 to 15
- send_far: int32 [128, 128, 1], P(('comm', 'inner')), may hold values from 0 to 15
Outputs:
- next_x: float32 [32, 524288], P(None, ('comm', 'inner'))
- next_p: float32 [32, 524288], P(None, ('comm', 'inner'))
Inputs may be any that keep to these rules, and one draw needn't show every extreme that they name: `tile_count`: some device has all 192 slots live and some exactly 96.
All inputs are finite; a program needn't handle non-finite values.
Results may differ from a plain program's by a relative error of at most 0.0046.
Values may be sent and summed in bfloat16 or wider, within the bound.
No kernel may reach another device: no remote copies, remote signals or barrier semaphores. Data moves between devices by JAX's collectives and lax.ppermute only.
A program may use at most 128 MiB of HBM per device.

v0:
```python
import jax
import jax.numpy as jnp
from jax import lax
from jax.sharding import PartitionSpec as P

NS = 6


exact_mode = lax.Precision.HIGHEST


def operate(field, degree, selector, tiles, tile_col, send_near, send_far):
    width, columns = field.shape
    tile_size = tiles.shape[1]
    own_count = columns // tile_size
    blocks = field.reshape(width, own_count, tile_size)
    inner_count = send_near.shape[1]
    outgoing = jnp.take(blocks, send_near.reshape(-1), axis=1).reshape(
        width, inner_count, -1, tile_size
    )
    came_near = lax.all_to_all(outgoing, "inner", split_axis=1, concat_axis=1, tiled=True)
    far_out = jnp.take(blocks, send_far.reshape(-1), axis=1)
    direct = far_out.reshape(width, send_far.shape[1], -1, tile_size)
    came_far = lax.all_to_all(direct, ("comm", "inner"), split_axis=1, concat_axis=1, tiled=True)
    pooled = jnp.concatenate(
        [blocks, came_near.reshape(width, -1, tile_size), came_far.reshape(width, -1, tile_size)],
        axis=1,
    )
    picked = jnp.take(pooled, tile_col, axis=1)
    contrib = jnp.einsum("knc,nrc->knr", picked, tiles, preferred_element_type=jnp.float32)
    summed = jnp.einsum("bn,knr->kbr", selector, contrib, precision=exact_mode)
    return degree[None, :] * field.astype(jnp.float32) - summed.reshape(width, columns)


def ritz_solve(gram, proj, width):
    basis_len = gram.shape[0]
    symmetric = 0.5 * (proj + proj.T)
    factor = jnp.linalg.cholesky(gram)
    halfway = jax.scipy.linalg.solve_triangular(factor, symmetric, lower=True)
    reduced = jax.scipy.linalg.solve_triangular(factor, halfway.T, lower=True)
    reduced = 0.5 * (reduced + reduced.T)
    identity_mat = jnp.eye(basis_len, dtype=jnp.float32)
    center = jnp.trace(reduced) / basis_len
    moved = reduced - center * identity_mat
    signum = moved / jnp.sqrt(jnp.sum(moved * moved) + 1e-06)
    for repeat in range(NS):
        square = jnp.dot(signum, signum, precision=exact_mode)
        signum = 1.5 * signum - 0.5 * jnp.dot(square, signum, precision=exact_mode)
    low_proj = 0.5 * (identity_mat - signum)
    target = jnp.dot(low_proj, factor[:width, :].T, precision=exact_mode)
    return jax.scipy.linalg.solve_triangular(factor, target, lower=True, trans=1)


def shards(vec_x, vec_p, diag_shift, tiles, tile_row, tile_col, tile_count, send_near, send_far):
    width = vec_x.shape[0]
    tile_size = tiles.shape[1]
    own_count = diag_shift.shape[0] // tile_size
    slot_ids = jnp.arange(tile_row.shape[0], dtype=jnp.int32)
    living = slot_ids < tile_count[0]
    selector = (
        (tile_row[None, :] == jnp.arange(own_count, dtype=jnp.int32)[:, None]) & living[None, :]
    ).astype(jnp.float32)
    row_totals = jnp.sum(tiles, axis=2, dtype=jnp.float32)
    degree = jnp.dot(selector, row_totals, precision=exact_mode).reshape(-1) + diag_shift
    extras = (tiles, tile_col, send_near, send_far)
    both = jnp.concatenate([vec_x, vec_p], axis=0)
    image = operate(both, degree, selector, *extras)
    image_x = image[:width]
    image_low = image.astype(jnp.bfloat16)
    x_wide = vec_x.astype(jnp.float32)
    numer = jnp.sum(x_wide * image_x, axis=1)
    denom = jnp.sum(x_wide * x_wide, axis=1)
    numer, denom = lax.psum((numer, denom), ("comm", "inner"))
    ratio = numer / (denom + 1e-06)
    search = ((image_x - ratio[:, None] * x_wide) / degree[None, :]).astype(jnp.bfloat16)
    image_w = operate(search, degree, selector, *extras)
    image_w_low = image_w.astype(jnp.bfloat16)
    basis = jnp.concatenate([vec_x, vec_p, search], axis=0)
    applied = jnp.concatenate([image_low, image_w_low], axis=0)
    gram_local = jnp.dot(basis, basis.T, preferred_element_type=jnp.float32)
    proj_local = jnp.dot(basis, applied.T, preferred_element_type=jnp.float32)
    gram, proj = lax.psum((gram_local, proj_local), ("comm", "inner"))
    coeff = ritz_solve(gram, proj, width).astype(jnp.bfloat16)
    next_x = jnp.dot(coeff.T, basis, preferred_element_type=jnp.float32)
    next_p = jnp.dot(coeff[width:].T, basis[width:], preferred_element_type=jnp.float32)
    return (next_x, next_p)


def solution(mesh):
    in_specs = (
        P(None, ("comm", "inner")),
        P(None, ("comm", "inner")),
        P(("comm", "inner")),
        P(("comm", "inner"), None, None),
        P(("comm", "inner")),
        P(("comm", "inner")),
        P(("comm", "inner")),
        P(("comm", "inner"), None, None),
        P(("comm", "inner"), None, None),
    )
    out_specs = (P(None, ("comm", "inner")), P(None, ("comm", "inner")))
    return jax.shard_map(shards, mesh=mesh, in_specs=in_specs, out_specs=out_specs, check_vma=False)
```

profile of v0, /device:TPU:1, one launch (start us, length us, event | category | flops | bytes accessed | tf_op | source)
XLA Modules:
  0.0 478.6 jit_solution(14830785433417722481)
XLA Ops:
  13.6 5.8 %all-to-all-start = ((bf16[64,8,8,256]{3,0,2,1:T(8,128)(2,1)}), bf16[64,8,8,256]{3,0,2,1:T(8,128)(2,1)S(1)}, u32[]{:S(2)}, u32[]{:S(2)}) async-start(bf16[64,8,8,256]{3,0,2,1:T(8,128)(2,1)} %broadcast_select_fusion), calls=%async_computation | async-start | bytes 4194304 | tf_op jit(solution)/shard_map/all_to_all | solution.py:21
  19.4 2.7 gather_fusion.1
  22.1 4.6 fusion.11
  26.7 19.0 %all-to-all-done = bf16[64,8,8,256]{3,0,2,1:T(8,128)(2,1)S(1)} async-done(((bf16[64,8,8,256]{3,0,2,1:T(8,128)(2,1)}), bf16[64,8,8,256]{3,0,2,1:T(8,128)(2,1)S(1)}, u32[]{:S(2)}, u32[]{:S(2)}) %all-to-all-start) | async-done | bytes 2097184 | tf_op jit(solution)/shard_map/all_to_all | solution.py:21
  45.7 9.5 %all-to-all-start.1 = ((bf16[64,128,1,256]{3,0,2,1:T(8,128)(2,1)}), bf16[64,128,1,256]{3,0,2,1:T(8,128)(2,1)}, u32[]{:S(2)}, u32[]{:S(2)}) async-start(bf16[64,128,1,256]{3,0,2,1:T(8,128)(2,1)} %fusion.11), calls=%async_computation.1 | async-start | bytes 8388608 | tf_op jit(solution)/shard_map/all_to_all | solution.py:24
  55.9 10.9 %convert_reduce_fusion = f32[192,256]{1,0:T(8,128)S(1)} fusion(bf16[192,256,256]{2,1,0:T(8,128)(2,1)} %param.14), kind=kLoop, calls=%fused_computation.6 | loop fusion | flops 25116672 | bytes 25362432 | tf_op jit(solution)/shard_map/reduce_sum | solution.py:63
  67.0 40.8 %all-to-all-done.1 = bf16[64,128,1,256]{3,0,2,1:T(8,128)(2,1)} async-done(((bf16[64,128,1,256]{3,0,2,1:T(8,128)(2,1)}), bf16[64,128,1,256]{3,0,2,1:T(8,128)(2,1)}, u32[]{:S(2)}, u32[]{:S(2)}) %all-to-all-start.1) | async-done | bytes 4194336 | tf_op jit(solution)/shard_map/all_to_all | solution.py:24
  107.8 5.7 %pad_maximum_fusion = bf16[64,208,256]{2,0,1:T(8,128)(2,1)} fusion(bf16[64,128,256]{2,0,1:T(8,128)(2,1)} %bitcast.12, bf16[64,64,256]{2,0,1:T(8,128)(2,1)S(1)} %bitcast.140, bf16[64,16,256]{2,0,1:T(8,128)(2,1)S(1)} %bitcast.134), kind=kLoop, calls=%fused_computation.9 | loop fusion | flops 6815744 | bytes 13631488 | tf_op jit(solution)/shard_map/concatenate | solution.py:25
  113.5 10.9 %gather_fusion.2 = bf16[192,64,256]{2,1,0:T(8,128)(2,1)} fusion(bf16[64,208,256]{2,0,1:T(8,128)(2,1)} %pad_maximum_fusion, s32[1024]{0:T(1024)S(1)} %pad_clamp_fusion), kind=kCustom, calls=%fused_computation.2 | custom fusion | bytes 12583680 | tf_op jit(solution)/shard_map/jit(_take)/gather | solution.py:29
  124.4 18.4 %fusion.8 = f32[64,192,256]{2,0,1:T(8,128)} fusion(bf16[192,256,256]{2,1,0:T(8,128)(2,1)} %param.14, bf16[192,64,256]{2,1,0:T(8,128)(2,1)} %gather_fusion.2, pred[192]{0:T(512)(128)(4,1)S(1)} %compare_and_fusion.2), kind=kOutput, calls=%fused_computation.16 | convolution fusion | flops 1613758464 | bytes 44040384 | tf_op jit(solution)/shard_map/knc,nrc->knr/dot_general | solution.py:30
  142.8 15.4 %fusion = f32[64,256,16]{1,2,0:T(8,128)S(1)} fusion(f32[64,192,256]{2,0,1:T(8,128)} %fusion.8, s32[192]{0:T(256)S(1)} %copy-done.7, pred[192]{0:T(512)(128)(4,1)S(1)} %iota_compare_fusion.3), kind=kOutput, calls=%fused_computation.7 | convolution fusion | flops 603985920 | bytes 13632448 | tf_op jit(solution)/shard_map/bn,knr->kbr/dot_general | solution.py:31
  160.0 62.3 %all-reduce.1 = (f32[32]{0:T(128)S(1)}, f32[32]{0:T(128)S(1)}) all-reduce(f32[32]{0:T(128)S(1)} %get-tuple-element.4, f32[32]{0:T(128)S(1)} %get-tuple-element.3), channel_id=1, replica_groups=mesh['comm'=16,'inner'=8] {'comm','inner'}, use_global_device_ids=true, to_apply=%region_2.3 | all-reduce | flops 64 | bytes 512 | tf_op jit(solution)/shard_map/psum | solution.py:73
  225.0 4.4 all-to-all-start.2
  231.7 12.8 %all-to-all-done.2 = bf16[32,8,8,256]{3,0,2,1:T(8,128)(2,1)S(1)} async-done(((bf16[32,8,8,256]{3,0,2,1:T(8,128)(2,1)}), bf16[32,8,8,256]{3,0,2,1:T(8,128)(2,1)S(1)}, u32[]{:S(2)}, u32[]{:S(2)}) %all-to-all-start.2) | async-done | bytes 1048608 | tf_op jit(solution)/shard_map/all_to_all | solution.py:21
  244.5 5.2 %all-to-all-start.3 = ((bf16[32,128,1,256]{3,0,2,1:T(8,128)(2,1)}), bf16[32,128,1,256]{3,0,2,1:T(8,128)(2,1)S(1)}, u32[]{:S(2)}, u32[]{:S(2)}) async-start(bf16[32,128,1,256]{3,0,2,1:T(8,128)(2,1)} %fusion.20), calls=%async_computation.3 | async-start | bytes 4194304 | tf_op jit(solution)/shard_map/all_to_all | solution.py:24
  249.8 2.3 fusion.80
  252.1 28.2 %all-to-all-done.3 = bf16[32,128,1,256]{3,0,2,1:T(8,128)(2,1)S(1)} async-done(((bf16[32,128,1,256]{3,0,2,1:T(8,128)(2,1)}), bf16[32,128,1,256]{3,0,2,1:T(8,128)(2,1)S(1)}, u32[]{:S(2)}, u32[]{:S(2)}) %all-to-all-start.3) | async-done | bytes 2097184 | tf_op jit(solution)/shard_map/all_to_all | solution.py:24
  280.3 2.0 pad_maximum_fusion.1
  282.2 2.8 gather_fusion.5
  285.1 13.7 %fusion.17 = f32[32,192,256]{2,0,1:T(8,128)} fusion(bf16[192,256,256]{2,1,0:T(8,128)(2,1)} %param.14, bf16[192,32,256]{2,1,0:T(8,128)(2,1)S(1)} %gather_fusion.5, pred[192]{0:T(512)(128)(4,1)S(1)} %compare_and_fusion.2), kind=kOutput, calls=%fused_computation.25 | convolution fusion | flops 806879232 | bytes 34603200 | tf_op jit(solution)/shard_map/knc,nrc->knr/dot_general | solution.py:30
  298.8 8.2 %fusion.4 = f32[32,256,16]{1,2,0:T(8,128)S(1)} fusion(f32[32,192,256]{2,0,1:T(8,128)} %fusion.17, s32[192]{0:T(256)S(1)} %copy-done.7, pred[192]{0:T(512)(128)(4,1)S(1)} %iota_compare_fusion.3), kind=kOutput, calls=%fused_computation.12 | convolution fusion | flops 301996032 | bytes 6816704 | tf_op jit(solution)/shard_map/bn,knr->kbr/dot_general | solution.py:31
  308.5 134.4 %all-reduce.4.cloned.1.call-done = (f32[96,96]{0,1:T(8,128)}, f32[96,96]{0,1:T(8,128)}) async-done(((f32[96,96]{0,1:T(8,128)}, f32[96,96]{0,1:T(8,128)}), (f32[96,96]{0,1:T(8,128)}, f32[96,96]{0,1:T(8,128)})) %all-reduce.4.cloned.1.call-update) | async-done | bytes 73744 | tf_op jit(solution)/shard_map/psum | solution.py:82
  444.6 8.8 %cholesky.19 = f32[96,96]{1,0:T(8,128)S(1)} custom-call(f32[96,96]{1,0:T(8,128)S(1)} %fusion.50), custom_call_target="Cholesky" | custom-call | tf_op jit(solution)/shard_map/jit(cholesky)/cholesky | solution.py:38
  454.7 7.4 %custom-call.10 = f32[1,96,96]{1,2,0:T(8,128)S(1)} custom-call(f32[1,96,96]{2,1,0:T(8,128)S(1)} %get-tuple-element.11), custom_call_target="InvertDiagBlocksLowerTriangular" | custom-call | tf_op jit(solution)/shard_map/jit(_solve_triangular)/triangular_solve | solution.py:51
  (80 shorter events, 26.1 us)
Async XLA Ops:
  13.6 32.1 %all-to-all-start = ((bf16[64,8,8,256]{3,0,2,1:T(8,128)(2,1)}), bf16[64,8,8,256]{3,0,2,1:T(8,128)(2,1)S(1)}, u32[]{:S(2)}, u32[]{:S(2)}) async-start(bf16[64,8,8,256]{3,0,2,1:T(8,128)(2,1)} %broadcast_select_fusion), calls=%async_computation | async-start | bytes 4194304 | tf_op jit(solution)/shard_map/all_to_all | solution.py:21
  19.4 2.8 copy-start.9
  45.7 62.1 %all-to-all-start.1 = ((bf16[64,128,1,256]{3,0,2,1:T(8,128)(2,1)}), bf16[64,128,1,256]{3,0,2,1:T(8,128)(2,1)}, u32[]{:S(2)}, u32[]{:S(2)}) async-start(bf16[64,128,1,256]{3,0,2,1:T(8,128)(2,1)} %fusion.11), calls=%async_computation.1 | async-start | bytes 8388608 | tf_op jit(solution)/shard_map/all_to_all | solution.py:24
  55.8 10.9 %copy-start.7 = (s32[192]{0:T(256)S(1)}, s32[192]{0:T(256)}, u32[]{:S(2)}) copy-start(s32[192]{0:T(256)} %param.15) | copy-start | bytes 2308
  55.8 11.1 %copy-start.6 = (f32[4096]{0:T(1024)S(1)}, f32[4096]{0:T(1024)}, u32[]{:S(2)}) copy-start(f32[4096]{0:T(1024)} %param.13) | copy-start | bytes 49156
  55.9 11.1 %copy-start.8 = (s32[192]{0:T(256)S(1)}, s32[192]{0:T(256)}, u32[]{:S(2)}) copy-start(s32[192]{0:T(256)} %param.16) | copy-start | bytes 2308
  158.2 1.6 copy-start.2
  222.5 0.7 copy-start
  225.0 19.5 %all-to-all-start.2 = ((bf16[32,8,8,256]{3,0,2,1:T(8,128)(2,1)}), bf16[32,8,8,256]{3,0,2,1:T(8,128)(2,1)S(1)}, u32[]{:S(2)}, u32[]{:S(2)}) async-start(bf16[32,8,8,256]{3,0,2,1:T(8,128)(2,1)} %broadcast_select_fusion.1), calls=%async_computation.2 | async-start | bytes 2097152 | tf_op jit(solution)/shard_map/all_to_all | solution.py:21
  244.5 35.7 %all-to-all-start.3 = ((bf16[32,128,1,256]{3,0,2,1:T(8,128)(2,1)}), bf16[32,128,1,256]{3,0,2,1:T(8,128)(2,1)S(1)}, u32[]{:S(2)}, u32[]{:S(2)}) async-start(bf16[32,128,1,256]{3,0,2,1:T(8,128)(2,1)} %fusion.20), calls=%async_computation.3 | async-start | bytes 4194304 | tf_op jit(solution)/shard_map/all_to_all | solution.py:24
  249.7 193.2 %all-reduce.4.cloned.1.call-start = ((), (), s32[]{:S(2)}) async-start(), calls=%async_computation.4 | async-start | bytes 196608 | tf_op jit(solution)/shard_map/psum | solution.py:82
  298.8 8.6 %copy-start.1 = (bf16[32,4096]{1,0:T(8,128)(2,1)S(1)}, bf16[32,4096]{1,0:T(8,128)(2,1)}, u32[]{:S(2)}) copy-start(bf16[32,4096]{1,0:T(8,128)(2,1)} %copy-done) | copy-start | bytes 786436
  298.8 8.6 %copy-start.3 = (bf16[32,4096]{1,0:T(8,128)(2,1)S(1)}, bf16[32,4096]{1,0:T(8,128)(2,1)}, u32[]{:S(2)}) copy-start(bf16[32,4096]{1,0:T(8,128)(2,1)} %param.11) | copy-start | bytes 786436
  298.8 8.7 %copy-start.4 = (bf16[32,4096]{1,0:T(8,128)(2,1)S(1)}, bf16[32,4096]{1,0:T(8,128)(2,1)}, u32[]{:S(2)}) copy-start(bf16[32,4096]{1,0:T(8,128)(2,1)} %param.12) | copy-start | bytes 786436
  298.8 8.7 %copy-start.5 = (bf16[64,4096]{1,0:T(8,128)(2,1)S(1)}, bf16[64,4096]{1,0:T(8,128)(2,1)}, u32[]{:S(2)}) copy-start(bf16[64,4096]{1,0:T(8,128)(2,1)} %get-tuple-element.13) | copy-start | bytes 1572868
Sparse Core Ops, SparseCore 0:
  308.6 134.2 all-reduce.3
where the time goes:
time: 480 us; the launch traced here: 479 us
  waiting for transfers between devices  235 us (49%)
  matrix products  65.3 us (14%)
  blocking collectives  62.3 us (13%)
  other arithmetic  49.8 us (10%)
  starting transfers between devices  24.9 us (5%)
  local copies, waits for them, and re-layouts  24.7 us (5%)
  between operations  16.4 us (3%)
    psum x1, waiting for transfers between devices, shards(): gram, proj = lax.psum((gram_local, proj_local), ('comm', 'inner'))  134 us
    all_to_all x2, waiting for transfers between devices, operate(): lax.all_to_all(direct, ('comm', 'inner'), split_axis=1, concat_axis=1, ti...  68.9 us
    psum x1, blocking collectives, shards(): numer, denom = lax.psum((numer, denom), ('comm', 'inner'))  62.3 us
    dot_general x2, matrix products, operate(): jnp.einsum('knc,nrc->knr', picked, tiles, preferred_element_type=jnp.floa...  32 us
    all_to_all x2, waiting for transfers between devices, operate(): lax.all_to_all(outgoing, 'inner', split_axis=1, concat_axis=1, tiled=True)  31.8 us
    dot_general x2, matrix products, operate(): summed = jnp.einsum('bn,knr->kbr', selector, contrib, precision=exact_mode)  23.6 us
    all_to_all x2, starting transfers between devices, operate(): lax.all_to_all(direct, ('comm', 'inner'), split_axis=1, concat_axis=1, ti...  14.7 us
    gather x2, local copies, waits for them, and re-layouts, operate(): picked = jnp.take(pooled, tile_col, axis=1)  13.8 us
  transfers between devices with their start and end apart: 5, of which 5 were waited for; matrix products, arithmetic and copies ran while one was open for 5% of the time, Pallas kernels for 0%

commit v1 on v0

v1 whole, which is shorter than its diff:
```python
import functools
import math

import jax
import jax.numpy as jnp
from jax import lax
from jax.experimental import pallas as pl
from jax.experimental.pallas import tpu as pltpu
from jax.sharding import PartitionSpec as P

NS = 6
CHUNK = 8
BOTH = ("comm", "inner")
MIB = 1 << 20
exact_mode = lax.Precision.HIGHEST
f32, bf16 = jnp.float32, jnp.bfloat16
NT_DIMS = (((1,), (1,)), ((), ()))
VMEM = pl.BlockSpec(memory_space=pltpu.VMEM)
SMEM = pl.BlockSpec(memory_space=pltpu.SMEM)
HBM = pl.BlockSpec(memory_space=pl.ANY)


def nt_dot(a, b):
    return lax.dot_general(a, b, NT_DIMS, preferred_element_type=f32)


def exact_dot(a, b):
    return jnp.dot(a, b, precision=exact_mode, preferred_element_type=f32)


def cost(flops, nbytes):
    return pl.CostEstimate(flops=int(flops), bytes_accessed=int(nbytes), transcendentals=0)


def pack_kernel(per, index_ref, blocks_ref, out_ref):
    step = pl.program_id(0)
    for e in range(per):
        out_ref[e] = blocks_ref[index_ref[step * per + e]]


def pack(index, blocks, per=16):
    count = index.shape[0]
    _, width, size = blocks.shape
    return pl.pallas_call(
        functools.partial(pack_kernel, per),
        grid_spec=pltpu.PrefetchScalarGridSpec(
            num_scalar_prefetch=1,
            grid=(count // per,),
            in_specs=[pl.BlockSpec(blocks.shape, lambda g, s: (0, 0, 0))],
            out_specs=pl.BlockSpec((per, width, size), lambda g, s: (g, 0, 0)),
        ),
        out_shape=jax.ShapeDtypeStruct((count, width, size), blocks.dtype),
        compiler_params=pltpu.CompilerParams(vmem_limit_bytes=32 * MIB),
        cost_estimate=cost(0, 2 * count * width * size * 2),
        name="pack",
    )(index, blocks)


def degree_kernel(row_ref, count_ref, tile_ref, shift_ref, out_ref, acc):
    step = pl.program_id(0)
    own = shift_ref.shape[0]

    @pl.when(step == 0)
    def _():
        acc[...] = jnp.zeros_like(acc)

    ones = jnp.ones((16, tile_ref.shape[2]), bf16)
    for e in range(CHUNK):
        t = step * CHUNK + e
        row = jnp.where(t < count_ref[0], row_ref[t], own)
        acc[row] = acc[row] + nt_dot(ones, tile_ref[e])[:8]

    @pl.when(step == pl.num_programs(0) - 1)
    def _():
        for b in range(own):
            out_ref[b : b + 1, :] = acc[b, 0:1, :] + shift_ref[b : b + 1, :]


def degree_of(tiles, tile_row, tile_count, shift):
    slots, size, _ = tiles.shape
    own = shift.shape[0]
    return pl.pallas_call(
        degree_kernel,
        grid_spec=pltpu.PrefetchScalarGridSpec(
            num_scalar_prefetch=2,
            grid=(slots // CHUNK,),
            in_specs=[
                pl.BlockSpec((CHUNK, size, size), lambda g, r, c: (g, 0, 0)),
                pl.BlockSpec(shift.shape, lambda g, r, c: (0, 0)),
            ],
            out_specs=pl.BlockSpec(shift.shape, lambda g, r, c: (0, 0)),
            scratch_shapes=[pltpu.VMEM((own + 1, 8, size), f32)],
        ),
        out_shape=jax.ShapeDtypeStruct(shift.shape, f32),
        compiler_params=pltpu.CompilerParams(vmem_limit_bytes=32 * MIB),
        cost_estimate=cost(2 * 16 * slots * size * size, slots * size * size * 2),
        name="degree",
    )(tile_row, tile_count, tiles, shift)


def tile_sums(step, row_ref, col_ref, count_ref, table_ref, tile_ref, near_ref, far_ref, pool, acc, sems):
    own = acc.shape[0] - 1
    near = near_ref.shape[0]

    @pl.when(step == 0)
    def _():
        first = pltpu.make_async_copy(near_ref, pool.at[pl.ds(0, near)], sems.at[0])
        second = pltpu.make_async_copy(far_ref, pool.at[pl.ds(near, far_ref.shape[0])], sems.at[1])
        first.start()
        second.start()
        acc[...] = jnp.zeros_like(acc)
        first.wait()
        second.wait()

    for e in range(CHUNK):
        t = step * CHUNK + e
        row = jnp.where(t < count_ref[0], row_ref[t], own)
        picked = pool[table_ref[col_ref[t]]]
        acc[row] = acc[row] + nt_dot(picked, tile_ref[e])


def first_kernel(width, row_ref, col_ref, count_ref, table_ref, tile_ref, near_ref, far_ref, degree_ref,
                 image_ref, low_ref, gram_ref, ratio_ref, pool, acc, sems):
    step = pl.program_id(0)
    own = degree_ref.shape[0]
    tile_sums(step, row_ref, col_ref, count_ref, table_ref, tile_ref, near_ref, far_ref, pool, acc, sems)

    @pl.when(step == pl.num_programs(0) - 1)
    def _():
        start = table_ref[0]
        numer = denom = gram = proj = 0.0
        for b in range(own):
            field = pool[start + b]
            wide = field.astype(f32)
            image = degree_ref[b : b + 1, :] * wide - acc[b]
            low = image.astype(bf16)
            image_ref[b] = image[:width]
            low_ref[b] = low
            numer = numer + wide[:width] * image[:width]
            denom = denom + wide[:width] * wide[:width]
            gram = gram + nt_dot(field, field)
            proj = proj + nt_dot(field, low)
        gram_ref[0] = gram
        gram_ref[1] = proj
        ratio_ref[0] = numer
        ratio_ref[1] = denom


def second_kernel(row_ref, col_ref, count_ref, table_ref, tile_ref, near_ref, far_ref, degree_ref, blocks_ref,
                  proj_ref, pool, acc, sems):
    step = pl.program_id(0)
    own = degree_ref.shape[0]
    tile_sums(step, row_ref, col_ref, count_ref, table_ref, tile_ref, near_ref, far_ref, pool, acc, sems)

    @pl.when(step == pl.num_programs(0) - 1)
    def _():
        start = table_ref[0]
        first = last = 0.0
        for b in range(own):
            field = pool[start + b]
            low = (degree_ref[b : b + 1, :] * field.astype(f32) - acc[b]).astype(bf16)
            first = first + nt_dot(blocks_ref[b], low)
            last = last + nt_dot(field, low)
        proj_ref[0 : first.shape[0]] = first
        proj_ref[first.shape[0] :] = last


def apply_tiles(kernel, out_shape, plan, tiles, near, far, extra, name):
    slots, size, _ = tiles.shape
    width = near.shape[1]
    own = extra[0].shape[0]
    whole = lambda a: pl.BlockSpec(a.shape, lambda g, *_: (0,) * len(a.shape))
    return pl.pallas_call(
        kernel,
        grid_spec=pltpu.PrefetchScalarGridSpec(
            num_scalar_prefetch=4,
            grid=(slots // CHUNK,),
            in_specs=[pl.BlockSpec((CHUNK, size, size), lambda g, *_: (g, 0, 0)), HBM, HBM]
            + [whole(a) for a in extra],
            out_specs=[whole(a) for a in out_shape],
            scratch_shapes=[
                pltpu.VMEM((near.shape[0] + far.shape[0], width, size), bf16),
                pltpu.VMEM((own + 1, width, size), f32),
                pltpu.SemaphoreType.DMA((2,)),
            ],
        ),
        out_shape=out_shape,
        compiler_params=pltpu.CompilerParams(vmem_limit_bytes=48 * MIB),
        cost_estimate=cost(2 * width * slots * size * size, slots * size * size * 2 + 2 * near.size * 2),
        name=name,
    )(*plan, tiles, near, far, *extra)


def search_kernel(ratio_ref, image_ref, blocks_ref, degree_ref, out_ref):
    width = image_ref.shape[1]
    ratio = ratio_ref[...]
    for b in range(image_ref.shape[0]):
        x = blocks_ref[b][:width].astype(f32)
        out_ref[b] = ((image_ref[b] - ratio * x) / degree_ref[b : b + 1, :]).astype(bf16)


def search_of(ratio, image_x, blocks, degree):
    return pl.pallas_call(
        search_kernel,
        in_specs=[VMEM] * 4,
        out_specs=VMEM,
        out_shape=jax.ShapeDtypeStruct(image_x.shape, bf16),
        cost_estimate=cost(0, image_x.size * 8),
        name="search",
    )(ratio, image_x, blocks, degree)


def cross_kernel(blocks_ref, search_ref, low_ref, out_ref):
    upper = lower = proj = 0.0
    for b in range(blocks_ref.shape[0]):
        s = search_ref[b]
        upper = upper + nt_dot(blocks_ref[b], s)
        lower = lower + nt_dot(s, s)
        proj = proj + nt_dot(low_ref[b], s)
    n, m = upper.shape
    out_ref[0, 0:n] = upper
    out_ref[0, n : n + m] = lower
    out_ref[1, 0:n] = proj
    out_ref[1, n : n + m] = jnp.zeros_like(lower)


def cross_of(blocks, search, low):
    n, m = blocks.shape[1], search.shape[1]
    return pl.pallas_call(
        cross_kernel,
        in_specs=[VMEM] * 3,
        out_specs=VMEM,
        out_shape=jax.ShapeDtypeStruct((2, n + m, m), f32),
        cost_estimate=cost(2 * 16 * 96 * 256 * 96, blocks.size * 6),
        name="cross",
    )(blocks, search, low)


def ritz_kernel(width, gram_ref, proj_ref, blocks_ref, search_ref, x_ref, p_ref):
    n = gram_ref.shape[0]
    rows = lax.broadcasted_iota(jnp.int32, (n, n), 0)
    cols = lax.broadcasted_iota(jnp.int32, (n, n), 1)
    eye = (rows == cols).astype(f32)
    a = gram_ref[...]
    for k in range(n):
        inv = 1.0 / a[k : k + 1, k : k + 1]
        line = a[k : k + 1, :]
        side = a[:, k : k + 1] * inv
        scaled = line * inv
        new = a - side * line
        new = jnp.where(rows == k, scaled, new)
        new = jnp.where(cols == k, side, new)
        a = jnp.where((rows == k) & (cols == k), -inv, new)
    proj = proj_ref[...]
    sym = 0.5 * (proj + proj.T)
    reduced = -exact_dot(a, sym)
    center = jnp.sum(reduced * eye) / n
    moved = reduced - center * eye
    signum = moved * lax.rsqrt(jnp.sum(moved * moved.T) + 1e-06)
    for _ in range(NS):
        square = exact_dot(signum, signum)
        signum = 1.5 * signum - 0.5 * exact_dot(square, signum)
    low_proj = 0.5 * (eye - signum)
    coeff = low_proj.T[:width, :]
    lanes = lax.broadcasted_iota(jnp.int32, coeff.shape, 1)
    both = jnp.concatenate([coeff, jnp.where(lanes < width, 0.0, coeff)], axis=0).astype(bf16)
    m = blocks_ref.shape[1]
    size = blocks_ref.shape[2]
    for b in range(blocks_ref.shape[0]):
        basis = jnp.concatenate([blocks_ref[b], search_ref[b]], axis=0)
        out = jnp.dot(both, basis, preferred_element_type=f32)
        x_ref[:, b * size : (b + 1) * size] = out[:width]
        p_ref[:, b * size : (b + 1) * size] = out[width:]


def ritz(gram, proj, blocks, search):
    own, width, size = search.shape
    shape = jax.ShapeDtypeStruct((width, own * size), f32)
    return pl.pallas_call(
        functools.partial(ritz_kernel, width),
        in_specs=[VMEM] * 4,
        out_specs=[VMEM] * 2,
        out_shape=[shape, shape],
        compiler_params=pltpu.CompilerParams(vmem_limit_bytes=32 * MIB),
        cost_estimate=cost(2 * 14 * 6 * 96**3, 2 * MIB),
        name="ritz",
    )(gram, proj, blocks, search)


def exchange(a, axes):
    return lax.all_to_all(a, axes, split_axis=0, concat_axis=0, tiled=True)


def spread(a, axis, count):
    return exchange(jnp.broadcast_to(a[None], (count,) + a.shape), axis)


def total(a, inner, comm):
    part = a.reshape(inner, -1, 128)
    part = jnp.sum(exchange(part, "inner"), axis=0)
    part = jnp.sum(spread(part, "comm", comm), axis=0)
    return spread(part, "inner", inner).reshape(a.shape)


def shards(inner, comm, vec_x, vec_p, diag_shift, tiles, tile_row, tile_col, tile_count, send_near, send_far):
    width = vec_x.shape[0]
    size = tiles.shape[1]
    own = diag_shift.shape[0] // size
    place = lax.axis_index("inner")
    blocks = jnp.concatenate([vec_x, vec_p], axis=0).reshape(2 * width, own, size).transpose(1, 0, 2)
    far_index = send_far.reshape(-1)
    near_sets = lax.all_gather(send_near.reshape(inner, -1), "inner", axis=0)
    near_mine = lax.dynamic_index_in_dim(near_sets, place, axis=1, keepdims=False)
    near_place = near_mine + own * jnp.arange(inner, dtype=jnp.int32)[:, None]
    table = jnp.concatenate([
        place * own + jnp.arange(own, dtype=jnp.int32),
        near_place.reshape(-1),
        inner * own + jnp.arange(far_index.shape[0], dtype=jnp.int32),
    ])
    plan = (tile_row, tile_col, tile_count, table)

    near = lax.all_gather(blocks, "inner", axis=0, tiled=True)
    far = exchange(pack(far_index, blocks), BOTH)
    degree = degree_of(tiles, tile_row, tile_count, diag_shift.reshape(own, size))
    image_x, low, gram_a, sums = apply_tiles(
        functools.partial(first_kernel, width),
        [
            jax.ShapeDtypeStruct((own, width, size), f32),
            jax.ShapeDtypeStruct((own, 2 * width, size), bf16),
            jax.ShapeDtypeStruct((2, 2 * width, 2 * width), f32),
            jax.ShapeDtypeStruct((2, width, size), f32),
        ],
        plan, tiles, near, far, [degree], "first",
    )
    sums = jnp.sum(sums, axis=2).reshape(1, 2 * width)
    sums = jnp.sum(spread(sums, BOTH, inner * comm), axis=(0, 1))
    ratio = (sums[:width] / (sums[width:] + 1e-06)).reshape(width, 1)
    search = search_of(ratio, image_x, blocks, degree)

    near = lax.all_gather(search, "inner", axis=0, tiled=True)
    far = exchange(pack(far_index, search), BOTH)
    cross = cross_of(blocks, search, low)
    (proj_w,) = apply_tiles(
        second_kernel, [jax.ShapeDtypeStruct((3 * width, width), f32)],
        plan, tiles, near, far, [degree, blocks], "second",
    )
    n = 2 * width
    packed = jnp.concatenate([gram_a.reshape(-1), cross.reshape(-1), proj_w.reshape(-1)])
    packed = total(packed, inner, comm)
    a, b, c = jnp.split(packed, [gram_a.size, gram_a.size + cross.size])
    gram_a, cross, proj_w = a.reshape(gram_a.shape), b.reshape(cross.shape), c.reshape(proj_w.shape)
    gram = jnp.concatenate([
        jnp.concatenate([gram_a[0], cross[0, :n]], axis=1),
        jnp.concatenate([cross[0, :n].T, cross[0, n:]], axis=1),
    ], axis=0)
    proj = jnp.concatenate([
        jnp.concatenate([gram_a[1], cross[1, :n].T], axis=0), proj_w], axis=1)
    return tuple(ritz(gram, proj, blocks, search))


def solution(mesh):
    in_specs = (
        P(None, BOTH),
        P(None, BOTH),
        P(BOTH),
        P(BOTH, None, None),
        P(BOTH),
        P(BOTH),
        P(BOTH),
        P(BOTH, None, None),
        P(BOTH, None, None),
    )
    out_specs = (P(None, BOTH), P(None, BOTH))
    run = functools.partial(shards, mesh.shape["inner"], mesh.shape["comm"])
    return jax.shard_map(run, mesh=mesh, in_specs=in_specs, out_specs=out_specs, check_vma=False)
```

time: 480 us -> 290 us (0.60)
  waiting for transfers between devices: 235 us -> 34.3 us
  Pallas kernels: 0 us -> 91.1 us
  matrix products: 65.3 us -> 0 us
  blocking collectives: 62.3 us -> 115 us
  other arithmetic: 49.8 us -> 1.61 us
  local copies, waits for them, and re-layouts: 24.7 us -> 14.9 us
  starting transfers between devices: 24.9 us -> 16.5 us
    psum x1 -> x0, waiting for transfers between devices: 134 us -> none  [shards(): gram, proj = lax.psum((gram_local, proj_local), ('comm', 'inner'))]
    pallas_call x0 -> x8, Pallas kernels: none -> 91.1 us  [the longest x2 47.4 us: apply_tiles(): pl.pallas_call(kernel, grid_spec=pltpu.PrefetchScalarGridSpec(num_scalar_...]
    all_gather x0 -> x1, blocking collectives: none -> 70.3 us  [shards(): near_sets = lax.all_gather(send_near.reshape(inner, -1), 'inner', axis=0)]
    all_to_all x4 -> x2, waiting for transfers between devices: 101 us -> 34.3 us  [exchange(): return lax.all_to_all(a, axes, split_axis=0, concat_axis=0, tiled=True)]
    dot_general x22 -> x0, matrix products: 63.8 us -> none  [the longest x2 32 us: operate(): jnp.einsum('knc,nrc->knr', picked, tiles, preferred_element_type=jnp.floa...]
    psum x1 -> x0, blocking collectives: 62.3 us -> none  [shards(): numer, denom = lax.psum((numer, denom), ('comm', 'inner'))]
    all_to_all x0 -> x4, blocking collectives: none -> 44.3 us  [exchange(): return lax.all_to_all(a, axes, split_axis=0, concat_axis=0, tiled=True)]
    gather x6 -> x0, local copies, waits for them, and re-layouts: 18.5 us -> none  [the longest x2 13.8 us: operate(): picked = jnp.take(pooled, tile_col, axis=1)]
  transfers between devices with their start and end apart: 5 -> 4, of which waited for: 5 -> 1; matrix products, arithmetic and copies ran while one was open for 5% -> 0% of each run, Pallas kernels for 0% -> 9%
where the time goes in v1:
time: 290 us; the launch traced here: 288 us
  blocking collectives  115 us (40%)
  Pallas kernels  91.1 us (31%)
  waiting for transfers between devices  34.3 us (12%)
  starting transfers between devices  16.5 us (6%)
  between operations  15.1 us (5%)
  local copies, waits for them, and re-layouts  14.9 us (5%)
    all_gather x1, blocking collectives, shards(): near_sets = lax.all_gather(send_near.reshape(inner, -1), 'inner', axis=0)  70.3 us
    pallas_call x2, Pallas kernels, apply_tiles(): pl.pallas_call(kernel, grid_spec=pltpu.PrefetchScalarGridSpec(num_scalar_...  47.4 us
    all_to_all x4, blocking collectives, exchange(): return lax.all_to_all(a, axes, split_axis=0, concat_axis=0, tiled=True)  44.3 us
    all_to_all x2, waiting for transfers between devices, exchange(): return lax.all_to_all(a, axes, split_axis=0, concat_axis=0, tiled=True)  34.3 us
    pallas_call x1, Pallas kernels, degree_of(): pl.pallas_call(degree_kernel, grid_spec=pltpu.PrefetchScalarGridSpec(num_...  21.3 us
    all_to_all x2, starting transfers between devices, exchange(): return lax.all_to_all(a, axes, split_axis=0, concat_axis=0, tiled=True)  16.5 us
    pallas_call x1, Pallas kernels, ritz(): pl.pallas_call(functools.partial(ritz_kernel, width), in_specs=[VMEM] * 4...  16.3 us
    unnamed x38, local copies, waits for them, and re-layouts  11.5 us
  transfers between devices with their start and end apart: 4, of which 1 were waited for; matrix products, arithmetic and copies ran while one was open for 0% of the time, Pallas kernels for 9%

profile of v1, /device:TPU:1, one launch (start us, length us, event | category | flops | bytes accessed | tf_op | source)
XLA Modules:
  0.0 288.2 jit_solution(12045099866620205508)
XLA Ops:
  7.2 1.1 pad_maximum_fusion
  8.3 0.8 copy.45
  9.2 1.0 copy-done
  10.8 0.9 pack.2
  11.8 2.0 copy-done.2
  13.8 12.0 %all-to-all-start = ((bf16[128,64,256]{2,1,0:T(8,128)(2,1)}), bf16[128,64,256]{2,1,0:T(8,128)(2,1)}, u32[]{:S(2)}, u32[]{:S(2)}) async-start(bf16[128,64,256]{2,1,0:T(8,128)(2,1)} %copy-done.2), calls=%async_computation | async-start | bytes 8388608 | tf_op jit(solution)/shard_map/all_to_all | solution.py:291
  25.8 70.3 %all_gather.9 = s32[8,8,8]{2,1,0:T(8,128)S(1)} all-gather(s32[1,8,8]{2,1,0:T(8,128)S(1)} %copy-done.17), channel_id=1, replica_groups=mesh['comm'=16,'inner'=8] {'inner'}, dimensions={0}, use_global_device_ids=true | all-gather | bytes 2304 | tf_op jit(solution)/shard_map/all_gather | solution.py:312
  97.1 21.3 %degree.1.degree_ref = f32[16,256]{1,0:T(8,128)S(1)} custom-call(s32[192]{0:T(256)S(1)} %copy-done.12, s32[1]{0:T(128)S(6)} %copy.46.count_ref, bf16[192,256,256]{2,1,0:T(8,128)(2,1)} %tile_ref.5, f32[16,256]{1,0:T(8,128)S(1)} %reshape.63.shift_ref), custom_call_target="tpu_custom_call" | custom-call | flops 402653184 | bytes 25165824 | tf_op jit(solution)/shard_map/degree/pallas_call | solution.py:82
  118.5 2.2 copy-done.6
  120.7 24.9 %first.1 = (f32[16,32,256]{2,1,0:T(8,128)S(1)}, bf16[16,64,256]{2,1,0:T(8,128)(2,1)S(1)}, f32[2,64,64]{2,1,0:T(8,128)S(1)}, f32[2,32,256]{2,1,0:T(8,128)S(1)}) custom-call(s32[192]{0:T(256)S(1)} %copy-done.12, s32[192]{0:T(256)S(1)} %copy-done.13, s32[1]{0:T(128)S(6)} %copy.46.count_ref, s32[208]{0:T(256)S(1)} %pad_add_fusion.table_ref, ...), custom_call_target="tpu_custom_call" | custom-call | flops 1610612736 | bytes 33554432 | tf_op jit(solution)/shard_map/first/pallas_call | solution.py:173
  147.4 17.0 %all_to_all.30 = f32[128,1,64]{2,1,0:T(1,128)S(1)} all-to-all(f32[128,1,64]{2,1,0:T(1,128)S(1)} %broadcast_in_dim.9), channel_id=1, replica_groups=mesh['comm'=16,'inner'=8] {'comm','inner'}, dimensions={0} | all-to-all | bytes 65536 | tf_op jit(solution)/shard_map/all_to_all | solution.py:291
  165.4 2.1 search.1.search_ref.blocks_ref
  167.5 1.0 copy-done.4
  169.3 1.3 copy-done.3
  170.7 4.5 %all-to-all-start.2 = ((bf16[128,32,256]{2,1,0:T(8,128)(2,1)}), bf16[128,32,256]{2,1,0:T(8,128)(2,1)S(1)}, u32[]{:S(2)}, u32[]{:S(2)}) async-start(bf16[128,32,256]{2,1,0:T(8,128)(2,1)} %copy-done.3), calls=%async_computation.2 | async-start | bytes 4194304 | tf_op jit(solution)/shard_map/all_to_all | solution.py:291
  175.2 2.4 cross.1
  177.6 1.0 reshape.66
  178.6 34.3 %all-to-all-done.2.far_ref = bf16[128,32,256]{2,1,0:T(8,128)(2,1)S(1)} async-done(((bf16[128,32,256]{2,1,0:T(8,128)(2,1)}), bf16[128,32,256]{2,1,0:T(8,128)(2,1)S(1)}, u32[]{:S(2)}, u32[]{:S(2)}) %all-to-all-start.2) | async-done | bytes 2097184 | tf_op jit(solution)/shard_map/all_to_all | solution.py:291
  212.9 1.6 copy-done.7
  214.5 22.4 %second.1 = f32[96,32]{1,0:T(8,128)S(1)} custom-call(s32[192]{0:T(256)S(1)} %copy-done.12, s32[192]{0:T(256)S(1)} %copy-done.13, s32[1]{0:T(128)S(6)} %copy.46.count_ref, s32[208]{0:T(256)S(1)} %pad_add_fusion.table_ref, bf16[192,256,256]{2,1,0:T(8,128)(2,1)} %tile_ref.5, bf16[128,32,256]{2,1,0:T(8,128)(2,1)S(1)} %copy-done.7, ...), custom_call_target="tpu_custom_call" | custom-call | flops 805306368 | bytes 29360128 | tf_op jit(solution)/shard_map/second/pallas_call | solution.py:173
  237.1 8.1 %all_to_all.31 = f32[8,17,128]{2,1,0:T(8,128)S(1)} all-to-all(f32[8,17,128]{2,1,0:T(8,128)S(1)} %reshape.68), channel_id=1, replica_groups=mesh['comm'=16,'inner'=8] {'inner'}, dimensions={0} | all-to-all | bytes 139264 | tf_op jit(solution)/shard_map/all_to_all | solution.py:291
  245.2 9.8 %all_to_all.32 = f32[16,17,128]{2,1,0:T(8,128)S(1)} all-to-all(f32[16,17,128]{2,1,0:T(8,128)S(1)} %broadcast_in_dim.10), channel_id=1, replica_groups=mesh['comm'=16,'inner'=8] {'comm'}, dimensions={0} | all-to-all | bytes 278528 | tf_op jit(solution)/shard_map/all_to_all | solution.py:291
  255.0 9.4 %all_to_all.33 = f32[8,17,128]{2,1,0:T(8,128)S(1)} all-to-all(f32[8,17,128]{2,1,0:T(8,128)S(1)} %broadcast_in_dim.11), channel_id=1, replica_groups=mesh['comm'=16,'inner'=8] {'inner'}, dimensions={0} | all-to-all | bytes 139264 | tf_op jit(solution)/shard_map/all_to_all | solution.py:291
  265.0 16.3 %ritz.1 = (f32[32,4096]{1,0:T(8,128)}, f32[32,4096]{1,0:T(8,128)}) custom-call(f32[96,96]{1,0:T(8,128)S(1)} %get-tuple-element.15.gram_ref, f32[96,96]{1,0:T(8,128)S(1)} %get-tuple-element.16.proj_ref, bf16[16,64,256]{2,1,0:T(8,128)(2,1)S(1)} %bitcast.25, bf16[16,32,256]{2,1,0:T(8,128)(2,1)S(1)} %copy-done.5), custom_call_target="tpu_custom_call" | custom-call | flops 148635648 | bytes 2097152 | tf_op jit(solution)/shard_map/ritz/pallas_call | solution.py:279
  (74 shorter events, 5.5 us)
Async XLA Ops:
  7.2 111.3 %all-gather.3.cloned.1.call-start = ((), (), s32[]{:S(2)}) async-start(), calls=%async_computation.6 | async-start | bytes 4718592 | tf_op jit(solution)/shard_map/all_gather | solution.py:322
  9.1 1.0 copy-start
  10.2 0.7 copy-start.14
  11.8 2.0 copy-start.2
  13.8 12.0 %copy-start.17 = (s32[1,8,8]{2,1,0:T(8,128)S(1)}, s32[1,8,8]{2,1,0:T(8,128)}, u32[]{:S(2)}) copy-start(s32[1,8,8]{2,1,0:T(8,128)} %param.16) | copy-start | bytes 772
  13.8 83.2 %copy-start.16 = (f32[4096]{0:T(1024)S(1)}, f32[4096]{0:T(1024)}, u32[]{:S(2)}) copy-start(f32[4096]{0:T(1024)} %param.11) | copy-start | bytes 49156
  13.8 83.3 %copy-start.12 = (s32[192]{0:T(256)S(1)}, s32[192]{0:T(256)}, u32[]{:S(2)}) copy-start(s32[192]{0:T(256)} %row_ref.5) | copy-start | bytes 2308
  13.8 104.7 %all-to-all-start = ((bf16[128,64,256]{2,1,0:T(8,128)(2,1)}), bf16[128,64,256]{2,1,0:T(8,128)(2,1)}, u32[]{:S(2)}, u32[]{:S(2)}) async-start(bf16[128,64,256]{2,1,0:T(8,128)(2,1)} %copy-done.2), calls=%async_computation | async-start | bytes 8388608 | tf_op jit(solution)/shard_map/all_to_all | solution.py:291
  25.7 187.2 %all-gather.5.cloned.1.call-start = ((), (), s32[]{:S(2)}) async-start(), calls=%async_computation.7 | async-start | bytes 2359296 | tf_op jit(solution)/shard_map/all_gather | solution.py:340
  97.0 21.4 %copy-start.13 = (s32[192]{0:T(256)S(1)}, s32[192]{0:T(256)}, u32[]{:S(2)}) copy-start(s32[192]{0:T(256)} %col_ref.3) | copy-start | bytes 2308
  118.3 27.3 %copy-start.10 = (f32[16,256]{1,0:T(8,128)}, f32[16,256]{1,0:T(8,128)S(1)}, u32[]{:S(2)}) copy-start(f32[16,256]{1,0:T(8,128)S(1)} %degree.1.degree_ref) | copy-start | bytes 49156
  118.4 49.1 %copy-start.15 = (s32[1,128,1]{1,2,0:T(1,128)S(1)}, s32[1,128,1]{1,2,0:T(1,128)}, u32[]{:S(2)}) copy-start(s32[1,128,1]{1,2,0:T(1,128)} %param.17) | copy-start | bytes 1540
  118.5 2.2 copy-start.6
  145.6 0.8 copy-start.8
  146.4 0.8 copy-start.9
  167.5 45.5 %copy-start.1 = (bf16[8,16,8,256]{3,2,0,1:T(8,128)(2,1)S(1)}, bf16[8,16,8,256]{3,2,0,1:T(8,128)(2,1)}, u32[]{:S(2)}) copy-start(bf16[8,16,8,256]{3,2,0,1:T(8,128)(2,1)} %copy.45) | copy-start | bytes 1572868
  167.5 1.0 copy-start.4
  168.5 44.4 %copy-start.11 = (f32[16,256]{1,0:T(8,128)S(1)}, f32[16,256]{1,0:T(8,128)}, u32[]{:S(2)}) copy-start(f32[16,256]{1,0:T(8,128)} %copy-done.10) | copy-start | bytes 49156
  169.3 1.3 copy-start.3
  170.7 42.3 %all-to-all-start.2 = ((bf16[128,32,256]{2,1,0:T(8,128)(2,1)}), bf16[128,32,256]{2,1,0:T(8,128)(2,1)S(1)}, u32[]{:S(2)}, u32[]{:S(2)}) async-start(bf16[128,32,256]{2,1,0:T(8,128)(2,1)} %copy-done.3), calls=%async_computation.2 | async-start | bytes 4194304 | tf_op jit(solution)/shard_map/all_to_all | solution.py:291
  178.6 86.4 %copy-start.5 = (bf16[16,32,256]{2,1,0:T(8,128)(2,1)S(1)}, bf16[16,32,256]{2,1,0:T(8,128)(2,1)}, u32[]{:S(2)}) copy-start(bf16[16,32,256]{2,1,0:T(8,128)(2,1)} %search.1.search_ref.blocks_ref) | copy-start | bytes 786436
  212.9 1.6 copy-start.7
Sparse Core Ops, SparseCore 0:
  10.3 67.0 all-gather.2
  167.6 35.4 all-gather.4

commit v2 on v0

v2 whole, which is shorter than its diff:
```python
import functools

import jax
import jax.numpy as jnp
from jax import lax
from jax.experimental import pallas as pl
from jax.experimental.pallas import tpu as pltpu
from jax.sharding import PartitionSpec as P

NS = 6
CHUNK = 24
AHEAD = 2
LIMIT = 60
BOTH = ("comm", "inner")
MIB = 1 << 20
exact_mode = lax.Precision.HIGHEST
f32, bf16, i32 = jnp.float32, jnp.bfloat16, jnp.int32
NT_DIMS = (((1,), (1,)), ((), ()))
VMEM = pl.BlockSpec(memory_space=pltpu.VMEM)
SMEM = pl.BlockSpec(memory_space=pltpu.SMEM)
HBM = pl.BlockSpec(memory_space=pltpu.HBM)


def nt_dot(a, b):
    return lax.dot_general(a, b, NT_DIMS, preferred_element_type=f32)


def exact_dot(a, b):
    return jnp.dot(a, b, precision=exact_mode, preferred_element_type=f32)


def cost(flops, nbytes):
    return pl.CostEstimate(flops=int(flops), bytes_accessed=int(nbytes), transcendentals=0)


def call(kernel, name, specs, out_shape, scratch, flops, nbytes, limit=LIMIT):
    whole = lambda a: pl.BlockSpec(a.shape, lambda g: (0,) * len(a.shape))
    return pl.pallas_call(
        kernel,
        grid=(1,),
        in_specs=[whole(s) if isinstance(s, (jax.Array, jax.core.Tracer)) else s for s in specs],
        out_specs=[whole(a) for a in out_shape],
        out_shape=out_shape,
        scratch_shapes=scratch,
        compiler_params=pltpu.CompilerParams(vmem_limit_bytes=limit * MIB),
        cost_estimate=cost(flops, nbytes),
        name=name,
    )


def stream(tile_ref, held, sems, use):
    slots = sems.shape[0]
    steps = tile_ref.shape[0] // CHUNK
    copy = lambda k: pltpu.make_async_copy(
        tile_ref.at[pl.ds(k * CHUNK, CHUNK)], held.at[pl.ds(k % slots * CHUNK, CHUNK)], sems.at[k % slots])

    @pl.loop(0, steps)
    def _(k):
        copy(k).wait()

        @pl.when(k + AHEAD < steps)
        def _():
            copy(k + AHEAD).start()

        for e in range(CHUNK):
            use(k * CHUNK + e, held.at[k % slots * CHUNK + e])


def stream_start(tile_ref, held, sems):
    for k in range(AHEAD):
        pltpu.make_async_copy(
            tile_ref.at[pl.ds(k * CHUNK, CHUNK)], held.at[pl.ds(k * CHUNK, CHUNK)], sems.at[k]).start()


def stream_scratch(size):
    return [pltpu.VMEM(((AHEAD + 1) * CHUNK, size, size), bf16), pltpu.SemaphoreType.DMA((AHEAD + 1,))]


def degree_kernel(row_ref, count_ref, tile_ref, shift_ref, out_ref, acc, held, sems):
    own, size = shift_ref.shape
    stream_start(tile_ref, held, sems)
    acc[...] = jnp.zeros_like(acc)
    ones = jnp.ones((16, size), bf16)

    def use(t, tile):
        row = jnp.where(t < count_ref[0], row_ref[t], own)
        acc[row] = acc[row] + nt_dot(ones, tile[...])[:8]

    stream(tile_ref, held, sems, use)
    for b in range(own):
        out_ref[b : b + 1, :] = acc[b, 0:1, :] + shift_ref[b : b + 1, :]


def degree_of(tiles, tile_row, tile_count, shift):
    size = tiles.shape[1]
    return call(
        degree_kernel, "degree", [SMEM, SMEM, HBM, shift], [jax.ShapeDtypeStruct(shift.shape, f32)],
        [pltpu.VMEM((shift.shape[0] + 1, 8, size), f32)] + stream_scratch(size), 1.2e10, tiles.size,
    )(tile_row, tile_count, tiles, shift)[0]


def cut_kernel(own, far_index, near_index, place_ref, field_ref, *outs):
    blocks_ref = outs[0]
    size = blocks_ref.shape[2]
    for b in range(own):
        blocks_ref[b] = field_ref[:, b * size : (b + 1) * size]
    nears = outs[1:8]
    pick = nears[0].shape[0]
    for d, near_ref in enumerate(nears, 1):
        mate = (place_ref[0] + d) % (len(nears) + 1)
        for e in range(pick):
            near_ref[e] = blocks_ref[near_index[mate, e]]
    for far_ref in outs[8:]:
        for e in range(far_ref.shape[0]):
            far_ref[e] = blocks_ref[far_index[e]]


def cut(name, own, far_index, near_index, place, field, far):
    width, size = field.shape[0], field.shape[1] // own
    pick = near_index.shape[1]
    shape = lambda n: jax.ShapeDtypeStruct((n, width, size), bf16)
    out = [shape(own)] + [shape(pick)] * 7 + [shape(far_index.shape[0])] * far
    return call(
        functools.partial(cut_kernel, own), name, [SMEM] * 3 + [field], out, [], 0, 8 * field.size,
    )(far_index, near_index, place, field)


def tile_sums(plan, tile_ref, pool, acc, held, sems):
    row_ref, col_ref, count_ref, table_ref = plan
    own = acc.shape[0] - 1

    def use(t, tile):
        row = jnp.where(t < count_ref[0], row_ref[t], own)
        acc[row] = acc[row] + nt_dot(pool[table_ref[col_ref[t]]], tile[...])

    stream(tile_ref, held, sems, use)


def copy_all(pairs, sems):
    copies = [pltpu.make_async_copy(a, b, sems.at[k]) for k, (a, b) in enumerate(pairs)]
    for copy in copies:
        copy.start()
    return copies


def split3(a):
    high = a.astype(bf16)
    rest = a - high.astype(f32)
    mid = rest.astype(bf16)
    return high, mid, (rest - mid.astype(f32)).astype(bf16)


def row_sums(a):
    n = a.shape[0]
    turn = lax.broadcasted_iota(i32, (n, n), 0) == lax.broadcasted_iota(i32, (n, n), 1)
    column = jnp.broadcast_to(jnp.sum(a, axis=1, keepdims=True), (n, n))
    return jnp.sum(jnp.where(turn, column, 0.0), axis=0, keepdims=True)


def first_kernel(*refs):
    plan, far_index, near_index, place_ref = refs[:4], refs[4], refs[5], refs[6]
    tile_ref, own_ref, near_refs, far_ref = refs[7], refs[8], refs[9:16], refs[16]
    degree_ref, p_ref = refs[17:19]
    image_ref, low_ref, send_ref, around_refs = refs[19], refs[20], refs[21], refs[22:29]
    pool, acc, held, sems, pool_sems, ext = refs[29:]
    own, width = own_ref.shape[0], own_ref.shape[1]
    pick = near_refs[0].shape[0]
    pairs = [(own_ref, pool.at[pl.ds(0, own)])]
    pairs += [(ref, pool.at[pl.ds(own + k * pick, pick)]) for k, ref in enumerate(near_refs)]
    pairs += [(far_ref, pool.at[pl.ds(own + 7 * pick, far_ref.shape[0])])]
    copies = copy_all(pairs, pool_sems)
    stream_start(tile_ref, held, sems)
    acc[...] = jnp.zeros_like(acc)
    for copy in copies:
        copy.wait()
    tile_sums(plan, tile_ref, pool, acc, held, sems)
    numer = denom = 0.0
    for b in range(own):
        wide = pool[b].astype(f32)
        image = degree_ref[b : b + 1, :] * wide - acc[b]
        low = image.astype(bf16)
        image_ref[b] = image
        low_ref[b] = low
        ext[b, 0:width] = p_ref[b]
        ext[b, width : 2 * width] = low
        numer = numer + wide * image
        denom = denom + wide * wide
    terms = [jnp.concatenate([u, v], axis=1) for u, v in zip(split3(row_sums(numer)), split3(row_sums(denom)))]
    sums = jnp.concatenate(terms + [jnp.zeros_like(terms[0])], axis=1).astype(f32)
    at = lax.broadcasted_iota(i32, (8, sums.shape[1]), 0)
    for b in range(own):
        degree = degree_ref[b : b + 1, :]
        high = degree.astype(bf16).astype(f32)
        tail = jnp.where(at == 0, high, jnp.where(at == 1, degree - high, jnp.where(at == 2, sums, 0.0)))
        ext[b, 2 * width :] = tail.astype(bf16)
    for e in range(send_ref.shape[0]):
        send_ref[e] = ext[far_index[e]]
    for d, ref in enumerate(around_refs, 1):
        mate = (place_ref[0] + d) % 8
        for e in range(pick):
            ref[e] = ext[near_index[mate, e], width:]


def op_x(plan, far_index, near_index, place, tiles, own_x, nears, far, degree, p):
    own, width, size = own_x.shape
    pick = nears[0].shape[0]
    blocks = own + 7 * pick + far.shape[0]
    out = [
        jax.ShapeDtypeStruct(own_x.shape, f32),
        jax.ShapeDtypeStruct(own_x.shape, bf16),
        jax.ShapeDtypeStruct((far.shape[0], 2 * width + 8, size), bf16),
    ] + [jax.ShapeDtypeStruct((pick, width + 8, size), bf16)] * 7
    return call(
        first_kernel, "op_x", [SMEM] * 7 + [HBM] * 10 + [degree, p], out,
        [pltpu.VMEM((blocks, width, size), bf16), pltpu.VMEM((own + 1, width, size), f32)] + stream_scratch(size)
        + [pltpu.SemaphoreType.DMA((9,)), pltpu.VMEM((own, 2 * width + 8, size), bf16)],
        1.2e10, tiles.size,
    )(*plan, far_index, near_index, place, tiles, own_x, *nears, far, degree, p)


def last_kernel(*refs):
    plan, tile_ref = refs[:4], refs[4]
    near_x, near_p, near_low = refs[5:12], refs[12:19], refs[19:26]
    far_x_ref, far_ref = refs[26:28]
    degree_ref, x_ref, p_ref, image_ref, low_x_ref = refs[28:33]
    search_ref, out_ref = refs[33:35]
    pool, acc, held, sems, pool_sems, xs, lows, fars = refs[35:]
    own, width, size = x_ref.shape
    pick = near_x[0].shape[0]
    near, far = 7 * pick, far_ref.shape[0]
    pairs = [(far_ref, fars), (far_x_ref, xs.at[pl.ds(near, far)])]
    for k in range(7):
        pairs.append((near_x[k], xs.at[pl.ds(k * pick, pick)]))
        pairs.append((near_low[k], lows.at[pl.ds(k * pick, pick)]))
        pairs.append((near_p[k], pool.at[pl.ds(own + k * pick, pick), pl.ds(0, width)]))
    copies = copy_all(pairs, pool_sems)
    stream_start(tile_ref, held, sems)
    acc[...] = jnp.zeros_like(acc)
    copies[0].wait()

    def add(k, total):
        for e in range(8):
            total = total + fars[k * 8 + e, 2 * width :].astype(f32)
        return total

    sums = lax.fori_loop(0, far // 8, add, jnp.zeros((8, size), f32))[2:3, :]
    two = 2 * width
    sums = sums[:, :two] + sums[:, two : 2 * two] + sums[:, 2 * two : 3 * two]
    ratio = sums[:, :width] / (sums[:, width:two] + 1e-06)
    square = (width, width)
    turn = lax.broadcasted_iota(i32, square, 0) == lax.broadcasted_iota(i32, square, 1)
    ratio = jnp.sum(jnp.where(turn, jnp.broadcast_to(ratio, square), 0.0), axis=1, keepdims=True)

    for b in range(own):
        s = ((image_ref[b] - ratio * x_ref[b].astype(f32)) / degree_ref[b : b + 1, :]).astype(bf16)
        search_ref[b] = s
        pool[b, 0:width] = p_ref[b]
        pool[b, width:] = s
    for copy in copies[1:]:
        copy.wait()

    def form(image, x, tail):
        tail = tail.astype(f32)
        inv = 1.0 / (tail[0:1] + tail[1:2])
        return ((image.astype(f32) - ratio * x.astype(f32)) * inv).astype(bf16)

    @pl.loop(0, 7)
    def _(k):
        for e in range(pick):
            m = k * pick + e
            pool[own + m, width:] = form(lows[m, 0:width], xs[m], lows[m, width:])

    @pl.loop(0, far // 8)
    def _(k):
        for e in range(8):
            m = k * 8 + e
            pool[own + near + m, 0:width] = fars[m, 0:width]
            pool[own + near + m, width:] = form(fars[m, width : 2 * width], xs[near + m], fars[m, 2 * width :])

    tile_sums(plan, tile_ref, pool, acc, held, sems)
    total = 0.0
    for b in range(own):
        field = pool[b]
        low = (degree_ref[b : b + 1, :] * field.astype(f32) - acc[b]).astype(bf16)
        basis = jnp.concatenate([x_ref[b], field], axis=0)
        total = total + nt_dot(basis, jnp.concatenate([basis, low_x_ref[b], low], axis=0))
    n = 3 * width
    rest = jnp.concatenate([total[: n // 2, 4 * width :], total[n // 2 :, 4 * width :]], axis=1)
    out_ref[:, 0, :] = jnp.concatenate([total[:, : 4 * width], rest], axis=0).T


def op_ps(plan, tiles, near_x, near_p, near_low, far_x, far, degree, x, p, image, low_x):
    own, width, size = x.shape
    pick = near_x[0].shape[0]
    near, count = 7 * pick, far.shape[0]
    n = 3 * width
    out = [jax.ShapeDtypeStruct(x.shape, bf16), jax.ShapeDtypeStruct((4 * width, 1, n + n // 2), f32)]
    return call(
        last_kernel, "op_ps", [SMEM] * 4 + [HBM] * 24 + [degree, x, p, image, low_x], out,
        [pltpu.VMEM((own + near + count, 2 * width, size), bf16), pltpu.VMEM((own + 1, 2 * width, size), f32)]
        + stream_scratch(size)
        + [
            pltpu.SemaphoreType.DMA((23,)),
            pltpu.VMEM((near + count, width, size), bf16),
            pltpu.VMEM((near, width + 8, size), bf16),
            pltpu.VMEM((count, 2 * width + 8, size), bf16),
        ],
        1.2e10, tiles.size,
    )(*plan, tiles, *near_x, *near_p, *near_low, far_x, far, degree, x, p, image, low_x)


def inverse(gram, eye, guess_ref, image_ref):
    root_row = lax.rsqrt(jnp.sum(gram * eye, axis=0, keepdims=True))
    root_col = lax.rsqrt(jnp.sum(gram * eye, axis=1, keepdims=True))
    scaled = gram * root_row * root_col
    bound = jnp.max(jnp.sum(jnp.abs(scaled), axis=1, keepdims=True))
    guess_ref[...] = eye / bound
    image_ref[...] = scaled / bound

    def improve(state):
        count, _ = state
        image = image_ref[...]
        guess = exact_dot(guess_ref[...], 2.0 * eye - image)
        guess_ref[...] = guess
        image_ref[...] = exact_dot(scaled, guess)
        return count + 1, jnp.max(jnp.abs(eye - image))

    lax.while_loop(lambda state: (state[1] > 3e-4) & (state[0] < 60), improve, (jnp.int32(0), jnp.float32(1.0)))
    return exact_dot(guess_ref[...], 2.0 * eye - image_ref[...]) * root_row * root_col


def ritz_kernel(sums_ref, x_ref, p_ref, s_ref, out_x_ref, out_p_ref, guess_ref, image_ref):
    width = x_ref.shape[1]
    n = 3 * width
    eye = (lax.broadcasted_iota(i32, (n, n), 0) == lax.broadcasted_iota(i32, (n, n), 1)).astype(f32)
    sums = sums_ref[:, 0, :].T
    late = sums[n:]
    late = jnp.concatenate([late[:, : 2 * width], late[:, 2 * width :]], axis=0)
    proj = jnp.concatenate([sums[0:n, n:], late], axis=1)
    sym = 0.5 * (proj + proj.T)
    reduced = exact_dot(inverse(sums[0:n, 0:n], eye, guess_ref, image_ref), sym)
    center = jnp.sum(reduced * eye) / n
    moved = reduced - center * eye
    signum = moved * lax.rsqrt(jnp.sum(moved * moved.T) + 1e-06)
    for _ in range(NS):
        square = exact_dot(signum, signum)
        signum = 1.5 * signum - 0.5 * exact_dot(square, signum)
    low_proj = 0.5 * (eye - signum)
    coeff = low_proj.T[:width, :]
    lanes = lax.broadcasted_iota(i32, coeff.shape, 1)
    both = jnp.concatenate([coeff, jnp.where(lanes < width, 0.0, coeff)], axis=0).astype(bf16)
    size = x_ref.shape[2]
    for b in range(out_x_ref.shape[1] // size):
        basis = jnp.concatenate([x_ref[b], p_ref[b], s_ref[b]], axis=0)
        out = jnp.dot(both, basis, preferred_element_type=f32)
        out_x_ref[:, b * size : (b + 1) * size] = out[:width]
        out_p_ref[:, b * size : (b + 1) * size] = out[width:]


def ritz(sums, x, p, search):
    own, width, size = p.shape
    shape = jax.ShapeDtypeStruct((width, own * size), f32)
    return call(
        ritz_kernel, "ritz", [sums, x, p, search], [shape, shape],
        [pltpu.VMEM((3 * width, 3 * width), f32)] * 2, 4e9, 2 * MIB,
    )(sums, x, p, search)


def exchange(a, axes):
    return lax.all_to_all(a, axes, split_axis=0, concat_axis=0, tiled=True)


def spread(a, axis, count):
    return exchange(jnp.broadcast_to(a[None], (count,) + a.shape), axis)


def total(a, devices):
    part = jnp.sum(exchange(a, BOTH), axis=0)
    return spread(part, BOTH, devices)


def pass_on(parts, inner):
    return [
        lax.ppermute(part, "inner", [(k, (k + d) % inner) for k in range(inner)])
        for d, part in enumerate(parts, 1)
    ]


def shards(inner, comm, vec_x, vec_p, diag_shift, tiles, tile_row, tile_col, tile_count, send_near, send_far):
    width = vec_x.shape[0]
    size = tiles.shape[1]
    own = diag_shift.shape[0] // size
    place = lax.axis_index("inner").astype(i32)
    devices = inner * comm
    pick = send_near.shape[2]
    far_index, near_index = send_far.reshape(-1), send_near[0]

    before = (place - jnp.arange(inner, dtype=i32)) % inner
    near_table = own + (before[:, None] - 1) * pick + jnp.arange(pick, dtype=i32)[None, :]
    mine = lax.dynamic_index_in_dim(send_near[0], place, axis=0, keepdims=True)
    near_table = jnp.where(before[:, None] == 0, mine, near_table)
    table = jnp.concatenate([
        jnp.arange(own, dtype=i32),
        near_table.reshape(-1),
        own + (inner - 1) * pick + jnp.arange(devices, dtype=i32),
    ])
    plan = (tile_row, tile_col, tile_count, table)
    spot = place.reshape(1)

    x, *rest = cut("cut_x", own, far_index, near_index, spot, vec_x, 1)
    far_x = exchange(rest[7], BOTH)
    near_x = pass_on(rest[:7], inner)
    degree = degree_of(tiles, tile_row, tile_count, diag_shift.reshape(own, size))
    p, *near_p = cut("cut_p", own, far_index, near_index, spot, vec_p, 0)
    far_x, p, near_p, degree = lax.optimization_barrier((far_x, p, near_p, degree))
    near_p = pass_on(near_p, inner)

    image, low_x, far, *near_low = op_x(
        plan, far_index, near_index, spot, tiles, x, near_x, far_x, degree, p)
    far, near_p = lax.optimization_barrier((far, near_p))
    far = exchange(far, BOTH)
    near_low = pass_on(near_low, inner)
    search, sums = op_ps(
        plan, tiles, near_x, near_p, near_low, far_x, far, degree, x, p, image, low_x)
    return tuple(ritz(total(sums, devices), x, p, search))


def solution(mesh):
    in_specs = (
        P(None, BOTH),
        P(None, BOTH),
        P(BOTH),
        P(BOTH, None, None),
        P(BOTH),
        P(BOTH),
        P(BOTH),
        P(BOTH, None, None),
        P(BOTH, None, None),
    )
    out_specs = (P(None, BOTH), P(None, BOTH))
    run = functools.partial(shards, mesh.shape["inner"], mesh.shape["comm"])
    return jax.shard_map(run, mesh=mesh, in_specs=in_specs, out_specs=out_specs, check_vma=False)
```

time: 480 us -> 218 us (0.45)
  waiting for transfers between devices: 235 us -> 67.4 us
  matrix products: 65.3 us -> 0 us
  Pallas kernels: 0 us -> 60.2 us
  other arithmetic: 49.8 us -> 0.93 us
  blocking collectives: 62.3 us -> 31.8 us
  starting transfers between devices: 24.9 us -> 51.6 us
  local copies, waits for them, and re-layouts: 24.7 us -> 4.37 us
  between operations: 16.4 us -> 1.6 us
    psum x1 -> x0, waiting for transfers between devices: 134 us -> none  [shards(): gram, proj = lax.psum((gram_local, proj_local), ('comm', 'inner'))]
    all_to_all x4 -> x2, waiting for transfers between devices: 101 us -> 6.42 us  [exchange(): return lax.all_to_all(a, axes, split_axis=0, concat_axis=0, tiled=True)]
    dot_general x22 -> x0, matrix products: 63.8 us -> none  [the longest x2 32 us: operate(): jnp.einsum('knc,nrc->knr', picked, tiles, preferred_element_type=jnp.floa...]
    psum x1 -> x0, blocking collectives: 62.3 us -> none  [shards(): numer, denom = lax.psum((numer, denom), ('comm', 'inner'))]
    ppermute x0 -> x21, waiting for transfers between devices: none -> 61 us  [pass_on(): lax.ppermute(part, 'inner', [(k, (k + d) % inner) for k in range(inner)])]
    pallas_call x0 -> x6, Pallas kernels: none -> 60.2 us  [the longest x1 17.8 us: op_ps(): call(last_kernel, 'op_ps', [SMEM] * 4 + [HBM] * 24 + [degree, x, p, image...]
    all_to_all x0 -> x2, blocking collectives: none -> 31.8 us  [exchange(): return lax.all_to_all(a, axes, split_axis=0, concat_axis=0, tiled=True)]
    ppermute x0 -> x21, starting transfers between devices: none -> 27.4 us  [pass_on(): lax.ppermute(part, 'inner', [(k, (k + d) % inner) for k in range(inner)])]
  transfers between devices with their start and end apart: 5 -> 23, of which waited for: 5 -> 9; matrix products, arithmetic and copies ran while one was open for 5% -> 1% of each run, Pallas kernels for 0% -> 13%
where the time goes in v2:
time: 218 us
  waiting for transfers between devices  67.4 us (31%)
  Pallas kernels  60.2 us (28%)
  starting transfers between devices  51.6 us (24%)
  blocking collectives  31.8 us (15%)
  local copies, waits for them, and re-layouts  4.37 us (2%)
    ppermute x21, waiting for transfers between devices, pass_on(): lax.ppermute(part, 'inner', [(k, (k + d) % inner) for k in range(inner)])  61 us
    all_to_all x2, blocking collectives, exchange(): return lax.all_to_all(a, axes, split_axis=0, concat_axis=0, tiled=True)  31.8 us
    ppermute x21, starting transfers between devices, pass_on(): lax.ppermute(part, 'inner', [(k, (k + d) % inner) for k in range(inner)])  27.4 us
    all_to_all x2, starting transfers between devices, exchange(): return lax.all_to_all(a, axes, split_axis=0, concat_axis=0, tiled=True)  24.2 us
    pallas_call x1, Pallas kernels, op_ps(): call(last_kernel, 'op_ps', [SMEM] * 4 + [HBM] * 24 + [degree, x, p, image...  17.8 us
    pallas_call x1, Pallas kernels, op_x(): call(first_kernel, 'op_x', [SMEM] * 7 + [HBM] * 10 + [degree, p], out, [p...  15.6 us
    pallas_call x1, Pallas kernels, degree_of(): call(degree_kernel, 'degree', [SMEM, SMEM, HBM, shift], [jax.ShapeDtypeSt...  11.6 us
    pallas_call x1, Pallas kernels, ritz(): call(ritz_kernel, 'ritz', [sums, x, p, search], [shape, shape], [pltpu.VM...  10.4 us
  transfers between devices with their start and end apart: 23, of which 9 were waited for; matrix products, arithmetic and copies ran while one was open for 1% of the time, Pallas kernels for 13%

profile of v2, /device:TPU:1, one launch (start us, length us, event | category | flops | bytes accessed | tf_op | source)
XLA Modules:
  0.0 217.9 jit_solution(3796255392117957582)
XLA Ops:
  0.6 2.8 %cut_x.1 = (bf16[16,32,256]{2,1,0:T(8,128)(2,1)}, bf16[8,32,256]{2,1,0:T(8,128)(2,1)}, bf16[8,32,256]{2,1,0:T(8,128)(2,1)}, bf16[8,32,256]{2,1,0:T(8,128)(2,1)},...) custom-call(s32[128]{0:T(128)} %bitcast.8, ...), custom_call_target="tpu_custom_call" | custom-call | bytes 1048576 | tf_op jit(solution)/shard_map/cut_x/pallas_call | solution.py:123
  3.4 11.5 %all-to-all-start = ((bf16[128,32,256]{2,1,0:T(8,128)(2,1)}), bf16[128,32,256]{2,1,0:T(8,128)(2,1)S(1)}, u32[]{:S(2)}, u32[]{:S(2)}) async-start(bf16[128,32,256]{2,1,0:T(8,128)(2,1)} %get-tuple-element.57), calls=%async_computation | async-start | bytes 4194304 | tf_op jit(solution)/shard_map/all_to_all | solution.py:370
  14.9 1.6 collective-permute-start
  17.7 1.6 collective-permute-start.2
  19.9 2.4 %collective-permute-start.4 = (bf16[8,32,256]{2,1,0:T(8,128)(2,1)}, bf16[8,32,256]{2,1,0:T(8,128)(2,1)S(1)}, u32[]{:S(2)}, u32[]{:S(2)}) collective-permute-start(bf16[8,32,256]{2,1,0:T(8,128)(2,1)} %get-tuple-element.53), channel_id=1, source_target_pairs={{0,5},{1,6},{2,7},{3,0},{4,1},{5,2},{6,3},{7,4},{8,13},{9,14},{10,... | collective-permute-start | bytes 393224 | tf_op jit(solution)/shard_map/ppermute | solution.py:384
  24.3 2.0 cut_p.1
  27.1 11.6 %degree.1.refs_17_.refs_28_ = f32[16,256]{1,0:T(8,128)} custom-call(s32[192]{0:T(256)} %refs_0_.3, s32[1]{0:T(128)S(6)} %copy.11.count_ref.refs_2_, bf16[192,256,256]{2,1,0:T(8,128)(2,1)} %refs_4_.1, f32[16,256]{1,0:T(8,128)} %reshape.54.shift_ref), custom_call_target="tpu_custom_call" | custom-call | flops 12000000000 | bytes 12582912 | tf_op jit(solution)/shard_map/degree/pallas_call | solution.py:96
  38.8 6.4 %all-to-all-done.refs_16_.refs_26_ = bf16[128,32,256]{2,1,0:T(8,128)(2,1)S(1)} async-done(((bf16[128,32,256]{2,1,0:T(8,128)(2,1)}), bf16[128,32,256]{2,1,0:T(8,128)(2,1)S(1)}, u32[]{:S(2)}, u32[]{:S(2)}) %all-to-all-start) | async-done | bytes 2097184 | tf_op jit(solution)/shard_map/all_to_all | solution.py:370
  48.6 2.7 %collective-permute-done.3.refs_12_.refs_8_ = bf16[8,32,256]{2,1,0:T(8,128)(2,1)S(1)} collective-permute-done((bf16[8,32,256]{2,1,0:T(8,128)(2,1)}, bf16[8,32,256]{2,1,0:T(8,128)(2,1)S(1)}, u32[]{:S(2)}, u32[]{:S(2)}) %collective-permute-start.3) | collective-permute-done | bytes 131104 | tf_op jit(solution)/shard_map/ppermute | solution.py:384
  52.1 1.5 collective-permute-start.9
  53.8 2.5 %collective-permute-start.11 = (bf16[8,32,256]{2,1,0:T(8,128)(2,1)}, bf16[8,32,256]{2,1,0:T(8,128)(2,1)S(1)}, u32[]{:S(2)}, u32[]{:S(2)}) collective-permute-start(bf16[8,32,256]{2,1,0:T(8,128)(2,1)} %get-tuple-element.74), channel_id=1, source_target_pairs={{0,5},{1,6},{2,7},{3,0},{4,1},{5,2},{6,3},{7,4},{8,13},{9,14},{10,... | collective-permute-start | bytes 393224 | tf_op jit(solution)/shard_map/ppermute | solution.py:384
  59.6 15.6 %op_x.1 = (f32[16,32,256]{2,1,0:T(8,128)}, bf16[16,32,256]{2,1,0:T(8,128)(2,1)}, bf16[128,72,256]{2,1,0:T(8,128)(2,1)}, bf16[8,40,256]{2,1,0:T(8,128)(2,1)}, bf1...) custom-call(s32[192]{0:T(256)} %refs_0_.3, ...), custom_call_target="tpu_custom_call" | custom-call | flops 12000000000 | bytes 12582912 | tf_op jit(solution)/shard_map/op_x/pallas_call | solution.py:213
  76.8 12.7 %all-to-all-start.1 = ((bf16[128,72,256]{2,1,0:T(8,128)(2,1)}), bf16[128,72,256]{2,1,0:T(8,128)(2,1)}, u32[]{:S(2)}, u32[]{:S(2)}) async-start(bf16[128,72,256]{2,1,0:T(8,128)(2,1)} %get-tuple-element.91), calls=%async_computation.1 | async-start | bytes 9437184 | tf_op jit(solution)/shard_map/all_to_all | solution.py:370
  89.5 1.6 collective-permute-start.14
  92.4 1.6 collective-permute-start.16
  94.6 2.5 %collective-permute-start.18 = (bf16[8,40,256]{2,1,0:T(8,128)(2,1)S(1)}, bf16[8,40,256]{2,1,0:T(8,128)(2,1)S(1)}, u32[]{:S(2)}, u32[]{:S(2)}) collective-permute-start(bf16[8,40,256]{2,1,0:T(8,128)(2,1)S(1)} %copy-done.5), channel_id=1, source_target_pairs={{0,5},{1,6},{2,7},{3,0},{4,1},{5,2},{6,3},{7,4},{8,13},{9,14},{10,... | collective-permute-start | bytes 491528 | tf_op jit(solution)/shard_map/ppermute | solution.py:384
  97.1 44.8 %collective-permute-done.14.refs_19_ = bf16[8,40,256]{2,1,0:T(8,128)(2,1)S(1)} collective-permute-done((bf16[8,40,256]{2,1,0:T(8,128)(2,1)S(1)}, bf16[8,40,256]{2,1,0:T(8,128)(2,1)S(1)}, u32[]{:S(2)}, u32[]{:S(2)}) %collective-permute-start.14) | collective-permute-done | bytes 163872 | tf_op jit(solution)/shard_map/ppermute | solution.py:384
  141.9 3.3 %collective-permute-start.19 = (bf16[8,40,256]{2,1,0:T(8,128)(2,1)S(1)}, bf16[8,40,256]{2,1,0:T(8,128)(2,1)S(1)}, u32[]{:S(2)}, u32[]{:S(2)}) collective-permute-start(bf16[8,40,256]{2,1,0:T(8,128)(2,1)S(1)} %copy-done.3), channel_id=1, source_target_pairs={{0,6},{1,7},{2,0},{3,1},{4,2},{5,3},{6,4},{7,5},{8,14},{9,15},{10,... | collective-permute-start | bytes 491528 | tf_op jit(solution)/shard_map/ppermute | solution.py:384
  145.2 3.9 %collective-permute-done.15.refs_20_ = bf16[8,40,256]{2,1,0:T(8,128)(2,1)S(1)} collective-permute-done((bf16[8,40,256]{2,1,0:T(8,128)(2,1)S(1)}, bf16[8,40,256]{2,1,0:T(8,128)(2,1)S(1)}, u32[]{:S(2)}, u32[]{:S(2)}) %collective-permute-start.15) | collective-permute-done | bytes 163872 | tf_op jit(solution)/shard_map/ppermute | solution.py:384
  150.1 6.4 %collective-permute-done.17.refs_22_ = bf16[8,40,256]{2,1,0:T(8,128)(2,1)S(1)} collective-permute-done((bf16[8,40,256]{2,1,0:T(8,128)(2,1)S(1)}, bf16[8,40,256]{2,1,0:T(8,128)(2,1)S(1)}, u32[]{:S(2)}, u32[]{:S(2)}) %collective-permute-start.17) | collective-permute-done | bytes 163872 | tf_op jit(solution)/shard_map/ppermute | solution.py:384
  157.7 17.8 %op_ps.1 = (bf16[16,32,256]{2,1,0:T(8,128)(2,1)}, f32[128,1,144]{2,1,0:T(1,128)}) custom-call(s32[192]{0:T(256)} %refs_0_.3, s32[192]{0:T(256)} %refs_1_.3, s32[1]{0:T(128)S(6)} %copy.11.count_ref.refs_2_, s32[208]{0:T(256)} %pad_add_fusion.refs_3_, bf16[192,256,256]{2,1,0:T(8,128)(2,1)} %refs_4_.1, bf16[8,32,256]{2,1,0:T(8,128)(2,1)} %copy-done.15, ...), custom_call_target="tpu_custom_call" | custom-call | flops 12000000000 | bytes 12582912 | tf_op jit(solution)/shard_map/op_ps/pallas_call | solution.py:298
  175.4 17.5 %all_to_all.20 = f32[128,1,144]{2,1,0:T(1,128)S(1)} all-to-all(f32[128,1,144]{2,1,0:T(1,128)} %get-tuple-element.94), channel_id=1, replica_groups=mesh['comm'=16,'inner'=8] {'comm','inner'}, dimensions={0} | all-to-all | bytes 147456 | tf_op jit(solution)/shard_map/all_to_all | solution.py:370
  193.2 14.3 %all_to_all.21.sums_ref = f32[128,1,144]{2,1,0:T(1,128)} all-to-all(f32[128,1,144]{2,1,0:T(1,128)S(1)} %broadcast_in_dim.30), channel_id=1, replica_groups=mesh['comm'=16,'inner'=8] {'comm','inner'}, dimensions={0} | all-to-all | bytes 147456 | tf_op jit(solution)/shard_map/all_to_all | solution.py:370
  207.5 10.4 %ritz.1 = (f32[32,4096]{1,0:T(8,128)}, f32[32,4096]{1,0:T(8,128)}) custom-call(f32[128,1,144]{2,1,0:T(1,128)} %all_to_all.21.sums_ref, bf16[16,32,256]{2,1,0:T(8,128)(2,1)} %get-tuple-element.56.refs_8_.refs_29_.x_ref, bf16[16,32,256]{2,1,0:T(8,128)(2,1)} %get-tuple-element.68.refs_18_.refs_30_.p_ref, bf16[16,32,256]{2,1,0:T(8,128)(2,1)} %get-tuple-element.95.s_ref), custom_call_target="tpu_custom_call" | custom-call | flops 4000000000 | bytes 2097152 | tf_op jit(solution)/shard_map/ritz/pallas_call | solution.py:363
  (101 shorter events, 17.1 us)
Async XLA Ops:
  3.4 41.8 %all-to-all-start = ((bf16[128,32,256]{2,1,0:T(8,128)(2,1)}), bf16[128,32,256]{2,1,0:T(8,128)(2,1)S(1)}, u32[]{:S(2)}, u32[]{:S(2)}) async-start(bf16[128,32,256]{2,1,0:T(8,128)(2,1)} %get-tuple-element.57), calls=%async_computation | async-start | bytes 4194304 | tf_op jit(solution)/shard_map/all_to_all | solution.py:370
  14.9 30.3 %collective-permute-start = (bf16[8,32,256]{2,1,0:T(8,128)(2,1)}, bf16[8,32,256]{2,1,0:T(8,128)(2,1)S(1)}, u32[]{:S(2)}, u32[]{:S(2)}) collective-permute-start(bf16[8,32,256]{2,1,0:T(8,128)(2,1)} %get-tuple-element.49), channel_id=1, source_target_pairs={{0,1},{1,2},{2,3},{3,4},{4,5},{5,6},{6,7},{7,0},{8,9},{9,10},{10,1... | collective-permute-start | bytes 393224 | tf_op jit(solution)/shard_map/ppermute | solution.py:384
  16.5 29.1 %collective-permute-start.1 = (bf16[8,32,256]{2,1,0:T(8,128)(2,1)}, bf16[8,32,256]{2,1,0:T(8,128)(2,1)S(1)}, u32[]{:S(2)}, u32[]{:S(2)}) collective-permute-start(bf16[8,32,256]{2,1,0:T(8,128)(2,1)} %get-tuple-element.50), channel_id=1, source_target_pairs={{0,2},{1,3},{2,4},{3,5},{4,6},{5,7},{6,0},{7,1},{8,10},{9,11},{10,... | collective-permute-start | bytes 393224 | tf_op jit(solution)/shard_map/ppermute | solution.py:384
  17.7 29.4 %collective-permute-start.2 = (bf16[8,32,256]{2,1,0:T(8,128)(2,1)}, bf16[8,32,256]{2,1,0:T(8,128)(2,1)S(1)}, u32[]{:S(2)}, u32[]{:S(2)}) collective-permute-start(bf16[8,32,256]{2,1,0:T(8,128)(2,1)} %get-tuple-element.51), channel_id=1, source_target_pairs={{0,3},{1,4},{2,5},{3,6},{4,7},{5,0},{6,1},{7,2},{8,11},{9,12},{10,... | collective-permute-start | bytes 393224 | tf_op jit(solution)/shard_map/ppermute | solution.py:384
  19.4 31.9 %collective-permute-start.3 = (bf16[8,32,256]{2,1,0:T(8,128)(2,1)}, bf16[8,32,256]{2,1,0:T(8,128)(2,1)S(1)}, u32[]{:S(2)}, u32[]{:S(2)}) collective-permute-start(bf16[8,32,256]{2,1,0:T(8,128)(2,1)} %get-tuple-element.52), channel_id=1, source_target_pairs={{0,4},{1,5},{2,6},{3,7},{4,0},{5,1},{6,2},{7,3},{8,12},{9,13},{10,... | collective-permute-start | bytes 393224 | tf_op jit(solution)/shard_map/ppermute | solution.py:384
  19.9 32.1 %collective-permute-start.4 = (bf16[8,32,256]{2,1,0:T(8,128)(2,1)}, bf16[8,32,256]{2,1,0:T(8,128)(2,1)S(1)}, u32[]{:S(2)}, u32[]{:S(2)}) collective-permute-start(bf16[8,32,256]{2,1,0:T(8,128)(2,1)} %get-tuple-element.53), channel_id=1, source_target_pairs={{0,5},{1,6},{2,7},{3,0},{4,1},{5,2},{6,3},{7,4},{8,13},{9,14},{10,... | collective-permute-start | bytes 393224 | tf_op jit(solution)/shard_map/ppermute | solution.py:384
  45.2 8.4 %collective-permute-start.5 = (bf16[8,32,256]{2,1,0:T(8,128)(2,1)S(1)}, bf16[8,32,256]{2,1,0:T(8,128)(2,1)S(1)}, u32[]{:S(2)}, u32[]{:S(2)}) collective-permute-start(bf16[8,32,256]{2,1,0:T(8,128)(2,1)S(1)} %copy-done.29), channel_id=1, source_target_pairs={{0,6},{1,7},{2,0},{3,1},{4,2},{5,3},{6,4},{7,5},{8,14},{9,15},{10,... | collective-permute-start | bytes 393224 | tf_op jit(solution)/shard_map/ppermute | solution.py:384
  45.7 8.1 %collective-permute-start.6 = (bf16[8,32,256]{2,1,0:T(8,128)(2,1)}, bf16[8,32,256]{2,1,0:T(8,128)(2,1)S(1)}, u32[]{:S(2)}, u32[]{:S(2)}) collective-permute-start(bf16[8,32,256]{2,1,0:T(8,128)(2,1)} %get-tuple-element.55), channel_id=1, source_target_pairs={{0,7},{1,0},{2,1},{3,2},{4,3},{5,4},{6,5},{7,6},{8,15},{9,8},{10,9... | collective-permute-start | bytes 393224 | tf_op jit(solution)/shard_map/ppermute | solution.py:384
  47.2 9.2 %collective-permute-start.7 = (bf16[8,32,256]{2,1,0:T(8,128)(2,1)}, bf16[8,32,256]{2,1,0:T(8,128)(2,1)S(1)}, u32[]{:S(2)}, u32[]{:S(2)}) collective-permute-start(bf16[8,32,256]{2,1,0:T(8,128)(2,1)} %get-tuple-element.70), channel_id=1, source_target_pairs={{0,1},{1,2},{2,3},{3,4},{4,5},{5,6},{6,7},{7,0},{8,9},{9,10},{10,1... | collective-permute-start | bytes 393224 | tf_op jit(solution)/shard_map/ppermute | solution.py:384
  51.3 7.0 %collective-permute-start.8 = (bf16[8,32,256]{2,1,0:T(8,128)(2,1)}, bf16[8,32,256]{2,1,0:T(8,128)(2,1)S(1)}, u32[]{:S(2)}, u32[]{:S(2)}) collective-permute-start(bf16[8,32,256]{2,1,0:T(8,128)(2,1)} %get-tuple-element.71), channel_id=1, source_target_pairs={{0,2},{1,3},{2,4},{3,5},{4,6},{5,7},{6,0},{7,1},{8,10},{9,11},{10,... | collective-permute-start | bytes 393224 | tf_op jit(solution)/shard_map/ppermute | solution.py:384
  52.1 23.2 %collective-permute-start.9 = (bf16[8,32,256]{2,1,0:T(8,128)(2,1)}, bf16[8,32,256]{2,1,0:T(8,128)(2,1)S(1)}, u32[]{:S(2)}, u32[]{:S(2)}) collective-permute-start(bf16[8,32,256]{2,1,0:T(8,128)(2,1)} %get-tuple-element.72), channel_id=1, source_target_pairs={{0,3},{1,4},{2,5},{3,6},{4,7},{5,0},{6,1},{7,2},{8,11},{9,12},{10,... | collective-permute-start | bytes 393224 | tf_op jit(solution)/shard_map/ppermute | solution.py:384
  53.6 21.7 %collective-permute-start.10 = (bf16[8,32,256]{2,1,0:T(8,128)(2,1)}, bf16[8,32,256]{2,1,0:T(8,128)(2,1)S(1)}, u32[]{:S(2)}, u32[]{:S(2)}) collective-permute-start(bf16[8,32,256]{2,1,0:T(8,128)(2,1)} %get-tuple-element.73), channel_id=1, source_target_pairs={{0,4},{1,5},{2,6},{3,7},{4,0},{5,1},{6,2},{7,3},{8,12},{9,13},{10,... | collective-permute-start | bytes 393224 | tf_op jit(solution)/shard_map/ppermute | solution.py:384
  53.8 21.5 %collective-permute-start.11 = (bf16[8,32,256]{2,1,0:T(8,128)(2,1)}, bf16[8,32,256]{2,1,0:T(8,128)(2,1)S(1)}, u32[]{:S(2)}, u32[]{:S(2)}) collective-permute-start(bf16[8,32,256]{2,1,0:T(8,128)(2,1)} %get-tuple-element.74), channel_id=1, source_target_pairs={{0,5},{1,6},{2,7},{3,0},{4,1},{5,2},{6,3},{7,4},{8,13},{9,14},{10,... | collective-permute-start | bytes 393224 | tf_op jit(solution)/shard_map/ppermute | solution.py:384
  56.3 19.0 %collective-permute-start.12 = (bf16[8,32,256]{2,1,0:T(8,128)(2,1)}, bf16[8,32,256]{2,1,0:T(8,128)(2,1)S(1)}, u32[]{:S(2)}, u32[]{:S(2)}) collective-permute-start(bf16[8,32,256]{2,1,0:T(8,128)(2,1)} %get-tuple-element.75), channel_id=1, source_target_pairs={{0,6},{1,7},{2,0},{3,1},{4,2},{5,3},{6,4},{7,5},{8,14},{9,15},{10,... | collective-permute-start | bytes 393224 | tf_op jit(solution)/shard_map/ppermute | solution.py:384
  58.3 17.1 %collective-permute-start.13 = (bf16[8,32,256]{2,1,0:T(8,128)(2,1)}, bf16[8,32,256]{2,1,0:T(8,128)(2,1)S(1)}, u32[]{:S(2)}, u32[]{:S(2)}) collective-permute-start(bf16[8,32,256]{2,1,0:T(8,128)(2,1)} %get-tuple-element.76), channel_id=1, source_target_pairs={{0,7},{1,0},{2,1},{3,2},{4,3},{5,4},{6,5},{7,6},{8,15},{9,8},{10,9... | collective-permute-start | bytes 393224 | tf_op jit(solution)/shard_map/ppermute | solution.py:384
  76.8 72.3 %copy-start.1 = (bf16[8,40,256]{2,1,0:T(8,128)(2,1)S(1)}, bf16[8,40,256]{2,1,0:T(8,128)(2,1)}, u32[]{:S(2)}) copy-start(bf16[8,40,256]{2,1,0:T(8,128)(2,1)} %get-tuple-element.90) | copy-start | bytes 491524
  76.8 80.1 %all-to-all-start.1 = ((bf16[128,72,256]{2,1,0:T(8,128)(2,1)}), bf16[128,72,256]{2,1,0:T(8,128)(2,1)}, u32[]{:S(2)}, u32[]{:S(2)}) async-start(bf16[128,72,256]{2,1,0:T(8,128)(2,1)} %get-tuple-element.91), calls=%async_computation.1 | async-start | bytes 9437184 | tf_op jit(solution)/shard_map/all_to_all | solution.py:370
  89.5 52.4 %collective-permute-start.14 = (bf16[8,40,256]{2,1,0:T(8,128)(2,1)S(1)}, bf16[8,40,256]{2,1,0:T(8,128)(2,1)S(1)}, u32[]{:S(2)}, u32[]{:S(2)}) collective-permute-start(bf16[8,40,256]{2,1,0:T(8,128)(2,1)S(1)} %copy-done.13), channel_id=1, source_target_pairs={{0,1},{1,2},{2,3},{3,4},{4,5},{5,6},{6,7},{7,0},{8,9},{9,10},{10,1... | collective-permute-start | bytes 491528 | tf_op jit(solution)/shard_map/ppermute | solution.py:384
  91.2 57.9 %collective-permute-start.15 = (bf16[8,40,256]{2,1,0:T(8,128)(2,1)S(1)}, bf16[8,40,256]{2,1,0:T(8,128)(2,1)S(1)}, u32[]{:S(2)}, u32[]{:S(2)}) collective-permute-start(bf16[8,40,256]{2,1,0:T(8,128)(2,1)S(1)} %copy-done.11), channel_id=1, source_target_pairs={{0,2},{1,3},{2,4},{3,5},{4,6},{5,7},{6,0},{7,1},{8,10},{9,11},{10,... | collective-permute-start | bytes 491528 | tf_op jit(solution)/shard_map/ppermute | solution.py:384
  92.4 57.7 %collective-permute-start.16 = (bf16[8,40,256]{2,1,0:T(8,128)(2,1)S(1)}, bf16[8,40,256]{2,1,0:T(8,128)(2,1)S(1)}, u32[]{:S(2)}, u32[]{:S(2)}) collective-permute-start(bf16[8,40,256]{2,1,0:T(8,128)(2,1)S(1)} %copy-done.9), channel_id=1, source_target_pairs={{0,3},{1,4},{2,5},{3,6},{4,7},{5,0},{6,1},{7,2},{8,11},{9,12},{10,... | collective-permute-start | bytes 491528 | tf_op jit(solution)/shard_map/ppermute | solution.py:384
  94.0 62.4 %collective-permute-start.17 = (bf16[8,40,256]{2,1,0:T(8,128)(2,1)S(1)}, bf16[8,40,256]{2,1,0:T(8,128)(2,1)S(1)}, u32[]{:S(2)}, u32[]{:S(2)}) collective-permute-start(bf16[8,40,256]{2,1,0:T(8,128)(2,1)S(1)} %copy-done.7), channel_id=1, source_target_pairs={{0,4},{1,5},{2,6},{3,7},{4,0},{5,1},{6,2},{7,3},{8,12},{9,13},{10,... | collective-permute-start | bytes 491528 | tf_op jit(solution)/shard_map/ppermute | solution.py:384
  94.6 62.3 %collective-permute-start.18 = (bf16[8,40,256]{2,1,0:T(8,128)(2,1)S(1)}, bf16[8,40,256]{2,1,0:T(8,128)(2,1)S(1)}, u32[]{:S(2)}, u32[]{:S(2)}) collective-permute-start(bf16[8,40,256]{2,1,0:T(8,128)(2,1)S(1)} %copy-done.5), channel_id=1, source_target_pairs={{0,5},{1,6},{2,7},{3,0},{4,1},{5,2},{6,3},{7,4},{8,13},{9,14},{10,... | collective-permute-start | bytes 491528 | tf_op jit(solution)/shard_map/ppermute | solution.py:384
  141.9 15.0 %collective-permute-start.19 = (bf16[8,40,256]{2,1,0:T(8,128)(2,1)S(1)}, bf16[8,40,256]{2,1,0:T(8,128)(2,1)S(1)}, u32[]{:S(2)}, u32[]{:S(2)}) collective-permute-start(bf16[8,40,256]{2,1,0:T(8,128)(2,1)S(1)} %copy-done.3), channel_id=1, source_target_pairs={{0,6},{1,7},{2,0},{3,1},{4,2},{5,3},{6,4},{7,5},{8,14},{9,15},{10,... | collective-permute-start | bytes 491528 | tf_op jit(solution)/shard_map/ppermute | solution.py:384
  149.1 7.8 %collective-permute-start.20 = (bf16[8,40,256]{2,1,0:T(8,128)(2,1)S(1)}, bf16[8,40,256]{2,1,0:T(8,128)(2,1)S(1)}, u32[]{:S(2)}, u32[]{:S(2)}) collective-permute-start(bf16[8,40,256]{2,1,0:T(8,128)(2,1)S(1)} %copy-done.1), channel_id=1, source_target_pairs={{0,7},{1,0},{2,1},{3,2},{4,3},{5,4},{6,5},{7,6},{8,15},{9,8},{10,9... | collective-permute-start | bytes 491528 | tf_op jit(solution)/shard_map/ppermute | solution.py:384
  (29 other events, 317.6 us)

commit v3 on v2

--- a/solution.py
+++ b/solution.py
@@ -66,8 +66,8 @@
             use(k * CHUNK + e, held.at[k % slots * CHUNK + e])
 
 
-def stream_start(tile_ref, held, sems):
-    for k in range(AHEAD):
+def stream_start(tile_ref, held, sems, first=0, last=AHEAD):
+    for k in range(first, last):
         pltpu.make_async_copy(
             tile_ref.at[pl.ds(k * CHUNK, CHUNK)], held.at[pl.ds(k * CHUNK, CHUNK)], sems.at[k]).start()
 
@@ -169,11 +169,13 @@
     pairs += [(ref, pool.at[pl.ds(own + k * pick, pick)]) for k, ref in enumerate(near_refs)]
     pairs += [(far_ref, pool.at[pl.ds(own + 7 * pick, far_ref.shape[0])])]
     copies = copy_all(pairs, pool_sems)
-    stream_start(tile_ref, held, sems)
+    stream_start(tile_ref, held, sems, 0, 1)
     acc[...] = jnp.zeros_like(acc)
     for copy in copies:
         copy.wait()
+    stream_start(tile_ref, held, sems, 1)
     tile_sums(plan, tile_ref, pool, acc, held, sems)
+    half = degree_ref.shape[1] // 2
     numer = denom = 0.0
     for b in range(own):
         wide = pool[b].astype(f32)
@@ -181,24 +183,26 @@
         low = image.astype(bf16)
         image_ref[b] = image
         low_ref[b] = low
-        ext[b, 0:width] = p_ref[b]
-        ext[b, width : 2 * width] = low
+        for k, part in enumerate((p_ref[b][:, :half], low[:, :half], p_ref[b][:, half:], low[:, half:])):
+            ext[b, k * width : (k + 1) * width] = part
         numer = numer + wide * image
         denom = denom + wide * wide
     terms = [jnp.concatenate([u, v], axis=1) for u, v in zip(split3(row_sums(numer)), split3(row_sums(denom)))]
-    sums = jnp.concatenate(terms + [jnp.zeros_like(terms[0])], axis=1).astype(f32)
-    at = lax.broadcasted_iota(i32, (8, sums.shape[1]), 0)
+    wide_sums = jnp.concatenate(terms + [jnp.zeros_like(terms[0])], axis=1).astype(f32)
+    at = lax.broadcasted_iota(i32, (8, half), 0)
     for b in range(own):
         degree = degree_ref[b : b + 1, :]
         high = degree.astype(bf16).astype(f32)
-        tail = jnp.where(at == 0, high, jnp.where(at == 1, degree - high, jnp.where(at == 2, sums, 0.0)))
-        ext[b, 2 * width :] = tail.astype(bf16)
+        tail = jnp.zeros((8, half), f32)
+        for k, row in enumerate((high, degree - high, wide_sums)):
+            tail = jnp.where(at == 2 * k, row[:, :half], jnp.where(at == 2 * k + 1, row[:, half:], tail))
+        ext[b, 4 * width :] = tail.astype(bf16)
     for e in range(send_ref.shape[0]):
         send_ref[e] = ext[far_index[e]]
     for d, ref in enumerate(around_refs, 1):
         mate = (place_ref[0] + d) % 8
         for e in range(pick):
-            ref[e] = ext[near_index[mate, e], width:]
+            ref[e] = ext[near_index[mate, e]]
 
 
 def op_x(plan, far_index, near_index, place, tiles, own_x, nears, far, degree, p):
@@ -208,44 +212,42 @@
     out = [
         jax.ShapeDtypeStruct(own_x.shape, f32),
         jax.ShapeDtypeStruct(own_x.shape, bf16),
-        jax.ShapeDtypeStruct((far.shape[0], 2 * width + 8, size), bf16),
-    ] + [jax.ShapeDtypeStruct((pick, width + 8, size), bf16)] * 7
+        jax.ShapeDtypeStruct((far.shape[0], 4 * width + 8, size // 2), bf16),
+    ] + [jax.ShapeDtypeStruct((pick, 4 * width + 8, size // 2), bf16)] * 7
     return call(
         first_kernel, "op_x", [SMEM] * 7 + [HBM] * 10 + [degree, p], out,
         [pltpu.VMEM((blocks, width, size), bf16), pltpu.VMEM((own + 1, width, size), f32)] + stream_scratch(size)
-        + [pltpu.SemaphoreType.DMA((9,)), pltpu.VMEM((own, 2 * width + 8, size), bf16)],
+        + [pltpu.SemaphoreType.DMA((9,)), pltpu.VMEM((own, 4 * width + 8, size // 2), bf16)],
         1.2e10, tiles.size,
     )(*plan, far_index, near_index, place, tiles, own_x, *nears, far, degree, p)
 
 
 def last_kernel(*refs):
     plan, tile_ref = refs[:4], refs[4]
-    near_x, near_p, near_low = refs[5:12], refs[12:19], refs[19:26]
-    far_x_ref, far_ref = refs[26:28]
-    degree_ref, x_ref, p_ref, image_ref, low_x_ref = refs[28:33]
-    search_ref, out_ref = refs[33:35]
-    pool, acc, held, sems, pool_sems, xs, lows, fars = refs[35:]
+    near_x, near_refs, far_x_ref, far_ref = refs[5:12], refs[12:19], refs[19], refs[20]
+    degree_ref, x_ref, p_ref, image_ref, low_x_ref = refs[21:26]
+    search_ref, out_ref = refs[26:28]
+    pool, acc, held, sems, pool_sems, xs, sent = refs[28:]
     own, width, size = x_ref.shape
     pick = near_x[0].shape[0]
     near, far = 7 * pick, far_ref.shape[0]
-    pairs = [(far_ref, fars), (far_x_ref, xs.at[pl.ds(near, far)])]
+    pairs = [(far_ref, sent.at[pl.ds(near, far)]), (far_x_ref, xs.at[pl.ds(near, far)])]
     for k in range(7):
         pairs.append((near_x[k], xs.at[pl.ds(k * pick, pick)]))
-        pairs.append((near_low[k], lows.at[pl.ds(k * pick, pick)]))
-        pairs.append((near_p[k], pool.at[pl.ds(own + k * pick, pick), pl.ds(0, width)]))
+        pairs.append((near_refs[k], sent.at[pl.ds(k * pick, pick)]))
     copies = copy_all(pairs, pool_sems)
-    stream_start(tile_ref, held, sems)
     acc[...] = jnp.zeros_like(acc)
     copies[0].wait()
+    stream_start(tile_ref, held, sems)
 
     def add(k, total):
         for e in range(8):
-            total = total + fars[k * 8 + e, 2 * width :].astype(f32)
+            total = total + sent[near + k * 8 + e, 4 * width :].astype(f32)
         return total
 
-    sums = lax.fori_loop(0, far // 8, add, jnp.zeros((8, size), f32))[2:3, :]
+    sums = lax.fori_loop(0, far // 8, add, jnp.zeros((8, size // 2), f32))
     two = 2 * width
-    sums = sums[:, :two] + sums[:, two : 2 * two] + sums[:, 2 * two : 3 * two]
+    sums = sums[4:5, :two] + sums[4:5, two:] + sums[5:6, :two]
     ratio = sums[:, :width] / (sums[:, width:two] + 1e-06)
     square = (width, width)
     turn = lax.broadcasted_iota(i32, square, 0) == lax.broadcasted_iota(i32, square, 1)
@@ -259,23 +261,21 @@
     for copy in copies[1:]:
         copy.wait()
 
+    def join(left, right):
+        return jnp.concatenate([left, right], axis=1)
+
     def form(image, x, tail):
         tail = tail.astype(f32)
-        inv = 1.0 / (tail[0:1] + tail[1:2])
+        inv = 1.0 / (join(tail[0:1], tail[1:2]) + join(tail[2:3], tail[3:4]))
         return ((image.astype(f32) - ratio * x.astype(f32)) * inv).astype(bf16)
 
-    @pl.loop(0, 7)
-    def _(k):
-        for e in range(pick):
-            m = k * pick + e
-            pool[own + m, width:] = form(lows[m, 0:width], xs[m], lows[m, width:])
-
-    @pl.loop(0, far // 8)
+    @pl.loop(0, (near + far) // 8)
     def _(k):
         for e in range(8):
             m = k * 8 + e
-            pool[own + near + m, 0:width] = fars[m, 0:width]
-            pool[own + near + m, width:] = form(fars[m, width : 2 * width], xs[near + m], fars[m, 2 * width :])
+            part = lambda r: join(sent[m, r * width : (r + 1) * width], sent[m, (r + 2) * width : (r + 3) * width])
+            pool[own + m, 0:width] = part(0)
+            pool[own + m, width:] = form(part(1), xs[m], sent[m, 4 * width :])
 
     tile_sums(plan, tile_ref, pool, acc, held, sems)
     total = 0.0
@@ -289,24 +289,23 @@
     out_ref[:, 0, :] = jnp.concatenate([total[:, : 4 * width], rest], axis=0).T
 
 
-def op_ps(plan, tiles, near_x, near_p, near_low, far_x, far, degree, x, p, image, low_x):
+def op_ps(plan, tiles, near_x, near, far_x, far, degree, x, p, image, low_x):
     own, width, size = x.shape
     pick = near_x[0].shape[0]
-    near, count = 7 * pick, far.shape[0]
+    count = 7 * pick + far.shape[0]
     n = 3 * width
     out = [jax.ShapeDtypeStruct(x.shape, bf16), jax.ShapeDtypeStruct((4 * width, 1, n + n // 2), f32)]
     return call(
-        last_kernel, "op_ps", [SMEM] * 4 + [HBM] * 24 + [degree, x, p, image, low_x], out,
-        [pltpu.VMEM((own + near + count, 2 * width, size), bf16), pltpu.VMEM((own + 1, 2 * width, size), f32)]
+        last_kernel, "op_ps", [SMEM] * 4 + [HBM] * 17 + [degree, x, p, image, low_x], out,
+        [pltpu.VMEM((own + count, 2 * width, size), bf16), pltpu.VMEM((own + 1, 2 * width, size), f32)]
         + stream_scratch(size)
         + [
-            pltpu.SemaphoreType.DMA((23,)),
-            pltpu.VMEM((near + count, width, size), bf16),
-            pltpu.VMEM((near, width + 8, size), bf16),
-            pltpu.VMEM((count, 2 * width + 8, size), bf16),
+            pltpu.SemaphoreType.DMA((16,)),
+            pltpu.VMEM((count, width, size), bf16),
+            pltpu.VMEM((count, 4 * width + 8, size // 2), bf16),
         ],
         1.2e10, tiles.size,
-    )(*plan, tiles, *near_x, *near_p, *near_low, far_x, far, degree, x, p, image, low_x)
+    )(*plan, tiles, *near_x, *near, far_x, far, degree, x, p, image, low_x)
 
 
 def inverse(gram, eye, guess_ref, image_ref):
@@ -314,8 +313,7 @@
     root_col = lax.rsqrt(jnp.sum(gram * eye, axis=1, keepdims=True))
     scaled = gram * root_row * root_col
     bound = jnp.max(jnp.sum(jnp.abs(scaled), axis=1, keepdims=True))
-    guess_ref[...] = eye / bound
-    image_ref[...] = scaled / bound
+    rough = scaled.astype(bf16)
 
     def improve(state):
         count, _ = state
@@ -325,7 +323,22 @@
         image_ref[...] = exact_dot(scaled, guess)
         return count + 1, jnp.max(jnp.abs(eye - image))
 
-    lax.while_loop(lambda state: (state[1] > 3e-4) & (state[0] < 60), improve, (jnp.int32(0), jnp.float32(1.0)))
+    start = (jnp.int32(0), jnp.float32(1.0))
+    guess = eye / bound
+    for _ in range(8):
+        guess = guess.astype(bf16)
+        image = jnp.dot(rough, guess, preferred_element_type=f32)
+        guess = jnp.dot(guess, (2.0 * eye - image).astype(bf16), preferred_element_type=f32)
+    guess_ref[...] = guess
+    image_ref[...] = exact_dot(scaled, guess)
+    away = jnp.max(jnp.sum(jnp.abs(eye - image_ref[...]), axis=1, keepdims=True))
+
+    @pl.when(jnp.logical_not(away < 0.9))
+    def _():
+        guess_ref[...] = eye / bound
+        image_ref[...] = scaled / bound
+
+    lax.while_loop(lambda state: (state[1] > 3e-4) & (state[0] < 60), improve, start)
     return exact_dot(guess_ref[...], 2.0 * eye - image_ref[...]) * root_row * root_col
 
 
@@ -404,24 +417,23 @@
         near_table.reshape(-1),
         own + (inner - 1) * pick + jnp.arange(devices, dtype=i32),
     ])
-    plan = (tile_row, tile_col, tile_count, table)
     spot = place.reshape(1)
 
     x, *rest = cut("cut_x", own, far_index, near_index, spot, vec_x, 1)
     far_x = exchange(rest[7], BOTH)
-    near_x = pass_on(rest[:7], inner)
+    tile_row, table = lax.optimization_barrier((tile_row, table))
+    plan = (tile_row, tile_col, tile_count, table)
     degree = degree_of(tiles, tile_row, tile_count, diag_shift.reshape(own, size))
-    p, *near_p = cut("cut_p", own, far_index, near_index, spot, vec_p, 0)
-    far_x, p, near_p, degree = lax.optimization_barrier((far_x, p, near_p, degree))
-    near_p = pass_on(near_p, inner)
-
-    image, low_x, far, *near_low = op_x(
+    late, degree = lax.optimization_barrier((rest[4:7], degree))
+    near_x = pass_on(rest[:4] + late, inner)
+    p = vec_p.reshape(width, own, size).transpose(1, 0, 2)
+    p, late = lax.optimization_barrier((p, late))
+
+    image, low_x, far, *near = op_x(
         plan, far_index, near_index, spot, tiles, x, near_x, far_x, degree, p)
-    far, near_p = lax.optimization_barrier((far, near_p))
     far = exchange(far, BOTH)
-    near_low = pass_on(near_low, inner)
-    search, sums = op_ps(
-        plan, tiles, near_x, near_p, near_low, far_x, far, degree, x, p, image, low_x)
+    near = pass_on(near, inner)
+    search, sums = op_ps(plan, tiles, near_x, near, far_x, far, degree, x, p, image, low_x)
     return tuple(ritz(total(sums, devices), x, p, search))
 
 

time: 218 us -> 213 us (0.977)
  starting transfers between devices: 51.6 us -> 39.9 us
  waiting for transfers between devices: 67.4 us -> 77.2 us
  Pallas kernels: 60.2 us -> 57.1 us
    ppermute x21 -> x14, waiting for transfers between devices: 61 us -> 77.2 us  [pass_on(): lax.ppermute(part, 'inner', [(k, (k + d) % inner) for k in range(inner)])]
    ppermute x21 -> x14, starting transfers between devices: 27.4 us -> 19.5 us  [pass_on(): lax.ppermute(part, 'inner', [(k, (k + d) % inner) for k in range(inner)])]
    all_to_all x2, waiting for transfers between devices: 6.42 us -> 0.01 us  [exchange(): return lax.all_to_all(a, axes, split_axis=0, concat_axis=0, tiled=True)]
    all_to_all x2, starting transfers between devices: 24.2 us -> 20.4 us  [exchange(): return lax.all_to_all(a, axes, split_axis=0, concat_axis=0, tiled=True)]
    pallas_call x2 -> x1, Pallas kernels: 4.77 us -> 2.74 us  [cut(): call(functools.partial(cut_kernel, own), name, [SMEM] * 3 + [field], out,...]
  transfers between devices with their start and end apart: 23 -> 16, of which waited for: 9 -> 8; matrix products, arithmetic and copies ran while one was open for 1% -> 1% of each run, Pallas kernels for 13% -> 5%
where the time goes in v3:
time: 213 us
  waiting for transfers between devices  77.2 us (36%)
  Pallas kernels  57.1 us (27%)
  starting transfers between devices  39.9 us (19%)
  blocking collectives  31.7 us (15%)
  local copies, waits for them, and re-layouts  4.52 us (2%)
    ppermute x14, waiting for transfers between devices, pass_on(): lax.ppermute(part, 'inner', [(k, (k + d) % inner) for k in range(inner)])  77.2 us
    all_to_all x2, blocking collectives, exchange(): return lax.all_to_all(a, axes, split_axis=0, concat_axis=0, tiled=True)  31.7 us
    all_to_all x2, starting transfers between devices, exchange(): return lax.all_to_all(a, axes, split_axis=0, concat_axis=0, tiled=True)  20.4 us
    ppermute x14, starting transfers between devices, pass_on(): lax.ppermute(part, 'inner', [(k, (k + d) % inner) for k in range(inner)])  19.5 us
    pallas_call x1, Pallas kernels, op_ps(): call(last_kernel, 'op_ps', [SMEM] * 4 + [HBM] * 17 + [degree, x, p, image...  16.8 us
    pallas_call x1, Pallas kernels, op_x(): call(first_kernel, 'op_x', [SMEM] * 7 + [HBM] * 10 + [degree, p], out, [p...  16.1 us
    pallas_call x1, Pallas kernels, degree_of(): call(degree_kernel, 'degree', [SMEM, SMEM, HBM, shift], [jax.ShapeDtypeSt...  11.6 us
    pallas_call x1, Pallas kernels, ritz(): call(ritz_kernel, 'ritz', [sums, x, p, search], [shape, shape], [pltpu.VM...  9.85 us
  transfers between devices with their start and end apart: 16, of which 8 were waited for; matrix products, arithmetic and copies ran while one was open for 1% of the time, Pallas kernels for 5%

profile of v3, /device:TPU:1, one launch (start us, length us, event | category | flops | bytes accessed | tf_op | source)
XLA Modules:
  0.0 213.0 jit_solution(14500886527287610900)
XLA Ops:
  0.6 2.7 %cut_x.1 = (bf16[16,32,256]{2,1,0:T(8,128)(2,1)}, bf16[8,32,256]{2,1,0:T(8,128)(2,1)}, bf16[8,32,256]{2,1,0:T(8,128)(2,1)}, bf16[8,32,256]{2,1,0:T(8,128)(2,1)},...) custom-call(s32[128]{0:T(128)} %bitcast.18, ...), custom_call_target="tpu_custom_call" | custom-call | bytes 1048576 | tf_op jit(solution)/shard_map/cut_x/pallas_call | solution.py:123
  3.4 11.5 %all-to-all-start = ((bf16[128,32,256]{2,1,0:T(8,128)(2,1)}), bf16[128,32,256]{2,1,0:T(8,128)(2,1)S(1)}, u32[]{:S(2)}, u32[]{:S(2)}) async-start(bf16[128,32,256]{2,1,0:T(8,128)(2,1)} %get-tuple-element.43), calls=%async_computation | async-start | bytes 4194304 | tf_op jit(solution)/shard_map/all_to_all | solution.py:383
  17.8 11.6 %degree.1.refs_17_.refs_21_ = f32[16,256]{1,0:T(8,128)} custom-call(s32[192]{0:T(256)} %refs_0_.1, s32[1]{0:T(128)S(6)} %copy.15.count_ref.refs_2_, bf16[192,256,256]{2,1,0:T(8,128)(2,1)} %refs_4_.1, f32[16,256]{1,0:T(8,128)} %reshape.57.shift_ref), custom_call_target="tpu_custom_call" | custom-call | flops 12000000000 | bytes 12582912 | tf_op jit(solution)/shard_map/degree/pallas_call | solution.py:96
  29.4 2.9 %collective-permute-start.4 = (bf16[8,32,256]{2,1,0:T(8,128)(2,1)S(1)}, bf16[8,32,256]{2,1,0:T(8,128)(2,1)S(1)}, u32[]{:S(2)}, u32[]{:S(2)}) collective-permute-start(bf16[8,32,256]{2,1,0:T(8,128)(2,1)S(1)} %copy-done.30), channel_id=1, source_target_pairs={{0,5},{1,6},{2,7},{3,0},{4,1},{5,2},{6,3},{7,4},{8,13},{9,14},{10,... | collective-permute-start | bytes 393224 | tf_op jit(solution)/shard_map/ppermute | solution.py:397
  32.9 1.0 collective-permute-start.6
  34.6 0.9 collective-permute-start.1
  35.5 8.6 %collective-permute-done.4.refs_13_.refs_9_ = bf16[8,32,256]{2,1,0:T(8,128)(2,1)S(1)} collective-permute-done((bf16[8,32,256]{2,1,0:T(8,128)(2,1)S(1)}, bf16[8,32,256]{2,1,0:T(8,128)(2,1)S(1)}, u32[]{:S(2)}, u32[]{:S(2)}) %collective-permute-start.4) | collective-permute-done | bytes 131104 | tf_op jit(solution)/shard_map/ppermute | solution.py:397
  44.5 2.4 %collective-permute-start.3 = (bf16[8,32,256]{2,1,0:T(8,128)(2,1)S(1)}, bf16[8,32,256]{2,1,0:T(8,128)(2,1)S(1)}, u32[]{:S(2)}, u32[]{:S(2)}) collective-permute-start(bf16[8,32,256]{2,1,0:T(8,128)(2,1)S(1)} %copy-done.24), channel_id=1, source_target_pairs={{0,4},{1,5},{2,6},{3,7},{4,0},{5,1},{6,2},{7,3},{8,12},{9,13},{10,... | collective-permute-start | bytes 393224 | tf_op jit(solution)/shard_map/ppermute | solution.py:397
  47.6 4.9 %collective-permute-done.2.refs_11_.refs_7_ = bf16[8,32,256]{2,1,0:T(8,128)(2,1)S(1)} collective-permute-done((bf16[8,32,256]{2,1,0:T(8,128)(2,1)S(1)}, bf16[8,32,256]{2,1,0:T(8,128)(2,1)S(1)}, u32[]{:S(2)}, u32[]{:S(2)}) %collective-permute-start.2) | collective-permute-done | bytes 131104 | tf_op jit(solution)/shard_map/ppermute | solution.py:397
  53.9 16.1 %op_x.1 = (f32[16,32,256]{2,1,0:T(8,128)}, bf16[16,32,256]{2,1,0:T(8,128)(2,1)}, bf16[128,136,128]{2,1,0:T(8,128)(2,1)}, bf16[8,136,128]{2,1,0:T(8,128)(2,1)}, b...) custom-call(s32[192]{0:T(256)} %refs_0_.1, ...), custom_call_target="tpu_custom_call" | custom-call | flops 12000000000 | bytes 12582912 | tf_op jit(solution)/shard_map/op_x/pallas_call | solution.py:217
  70.1 8.9 %all-to-all-start.1 = ((bf16[128,136,128]{2,1,0:T(8,128)(2,1)}), bf16[128,136,128]{2,1,0:T(8,128)(2,1)}, u32[]{:S(2)}, u32[]{:S(2)}) async-start(bf16[128,136,128]{2,1,0:T(8,128)(2,1)} %get-tuple-element.53), calls=%async_computation.1 | async-start | bytes 8912896 | tf_op jit(solution)/shard_map/all_to_all | solution.py:383
  79.0 1.6 collective-permute-start.7
  80.7 1.2 collective-permute-start.8
  81.9 1.6 collective-permute-start.9
  84.1 2.5 %collective-permute-start.11 = (bf16[8,136,128]{2,1,0:T(8,128)(2,1)S(1)}, bf16[8,136,128]{2,1,0:T(8,128)(2,1)S(1)}, u32[]{:S(2)}, u32[]{:S(2)}) collective-permute-start(bf16[8,136,128]{2,1,0:T(8,128)(2,1)S(1)} %copy-done.10), channel_id=1, source_target_pairs={{0,5},{1,6},{2,7},{3,0},{4,1},{5,2},{6,3},{7,4},{8,13},{9,14},{10,... | collective-permute-start | bytes 835592 | tf_op jit(solution)/shard_map/ppermute | solution.py:397
  86.6 44.5 %collective-permute-done.7.refs_12_ = bf16[8,136,128]{2,1,0:T(8,128)(2,1)S(1)} collective-permute-done((bf16[8,136,128]{2,1,0:T(8,128)(2,1)S(1)}, bf16[8,136,128]{2,1,0:T(8,128)(2,1)S(1)}, u32[]{:S(2)}, u32[]{:S(2)}) %collective-permute-start.7) | collective-permute-done | bytes 278560 | tf_op jit(solution)/shard_map/ppermute | solution.py:397
  131.1 3.3 %collective-permute-start.12 = (bf16[8,136,128]{2,1,0:T(8,128)(2,1)S(1)}, bf16[8,136,128]{2,1,0:T(8,128)(2,1)S(1)}, u32[]{:S(2)}, u32[]{:S(2)}) collective-permute-start(bf16[8,136,128]{2,1,0:T(8,128)(2,1)S(1)} %copy-done.9), channel_id=1, source_target_pairs={{0,6},{1,7},{2,0},{3,1},{4,2},{5,3},{6,4},{7,5},{8,14},{9,15},{10,... | collective-permute-start | bytes 835592 | tf_op jit(solution)/shard_map/ppermute | solution.py:397
  134.3 6.4 %collective-permute-done.8.refs_13_ = bf16[8,136,128]{2,1,0:T(8,128)(2,1)S(1)} collective-permute-done((bf16[8,136,128]{2,1,0:T(8,128)(2,1)S(1)}, bf16[8,136,128]{2,1,0:T(8,128)(2,1)S(1)}, u32[]{:S(2)}, u32[]{:S(2)}) %collective-permute-start.8) | collective-permute-done | bytes 278560 | tf_op jit(solution)/shard_map/ppermute | solution.py:397
  140.7 2.3 %collective-permute-done.9.refs_14_ = bf16[8,136,128]{2,1,0:T(8,128)(2,1)S(1)} collective-permute-done((bf16[8,136,128]{2,1,0:T(8,128)(2,1)S(1)}, bf16[8,136,128]{2,1,0:T(8,128)(2,1)S(1)}, u32[]{:S(2)}, u32[]{:S(2)}) %collective-permute-start.9) | collective-permute-done | bytes 278560 | tf_op jit(solution)/shard_map/ppermute | solution.py:397
  143.0 9.9 %collective-permute-done.10.refs_15_ = bf16[8,136,128]{2,1,0:T(8,128)(2,1)S(1)} collective-permute-done((bf16[8,136,128]{2,1,0:T(8,128)(2,1)S(1)}, bf16[8,136,128]{2,1,0:T(8,128)(2,1)S(1)}, u32[]{:S(2)}, u32[]{:S(2)}) %collective-permute-start.10) | collective-permute-done | bytes 278560 | tf_op jit(solution)/shard_map/ppermute | solution.py:397
  154.4 16.8 %op_ps.1 = (bf16[16,32,256]{2,1,0:T(8,128)(2,1)}, f32[128,1,144]{2,1,0:T(1,128)}) custom-call(s32[192]{0:T(256)} %refs_0_.1, s32[192]{0:T(256)} %refs_1_.3, s32[1]{0:T(128)S(6)} %copy.15.count_ref.refs_2_, s32[208]{0:T(256)} %pad_add_fusion.refs_3_, bf16[192,256,256]{2,1,0:T(8,128)(2,1)} %refs_4_.1, bf16[8,32,256]{2,1,0:T(8,128)(2,1)} %copy-done.20, ...), custom_call_target="tpu_custom_call" | custom-call | flops 12000000000 | bytes 12582912 | tf_op jit(solution)/shard_map/op_ps/pallas_call | solution.py:298
  171.2 17.4 %all_to_all.20 = f32[128,1,144]{2,1,0:T(1,128)S(1)} all-to-all(f32[128,1,144]{2,1,0:T(1,128)} %get-tuple-element.56), channel_id=1, replica_groups=mesh['comm'=16,'inner'=8] {'comm','inner'}, dimensions={0} | all-to-all | bytes 147456 | tf_op jit(solution)/shard_map/all_to_all | solution.py:383
  188.9 14.3 %all_to_all.21.sums_ref = f32[128,1,144]{2,1,0:T(1,128)} all-to-all(f32[128,1,144]{2,1,0:T(1,128)S(1)} %broadcast_in_dim.30), channel_id=1, replica_groups=mesh['comm'=16,'inner'=8] {'comm','inner'}, dimensions={0} | all-to-all | bytes 147456 | tf_op jit(solution)/shard_map/all_to_all | solution.py:383
  203.2 9.8 %ritz.1 = (f32[32,4096]{1,0:T(8,128)}, f32[32,4096]{1,0:T(8,128)}) custom-call(f32[128,1,144]{2,1,0:T(1,128)} %all_to_all.21.sums_ref, bf16[16,32,256]{2,1,0:T(8,128)(2,1)} %get-tuple-element.42.refs_8_.refs_22_.x_ref, bf16[16,32,256]{2,1,0:T(8,128)(2,1)} %bitcast.15, bf16[16,32,256]{2,1,0:T(8,128)(2,1)} %get-tuple-element.57.s_ref), custom_call_target="tpu_custom_call" | custom-call | flops 4000000000 | bytes 2097152 | tf_op jit(solution)/shard_map/ritz/pallas_call | solution.py:376
  (89 shorter events, 8.1 us)
Async XLA Ops:
  0.6 16.5 %copy-start.2 = (f32[4096]{0:T(1024)S(1)}, f32[4096]{0:T(1024)}, u32[]{:S(2)}) copy-start(f32[4096]{0:T(1024)} %param.11) | copy-start | bytes 49156
  3.4 49.2 %all-to-all-start = ((bf16[128,32,256]{2,1,0:T(8,128)(2,1)}), bf16[128,32,256]{2,1,0:T(8,128)(2,1)S(1)}, u32[]{:S(2)}, u32[]{:S(2)}) async-start(bf16[128,32,256]{2,1,0:T(8,128)(2,1)} %get-tuple-element.43), calls=%async_computation | async-start | bytes 4194304 | tf_op jit(solution)/shard_map/all_to_all | solution.py:383
  17.7 16.9 %copy-start.26 = (bf16[8,32,256]{2,1,0:T(8,128)(2,1)S(1)}, bf16[8,32,256]{2,1,0:T(8,128)(2,1)}, u32[]{:S(2)}) copy-start(bf16[8,32,256]{2,1,0:T(8,128)(2,1)} %get-tuple-element.33) | copy-start | bytes 393220
  17.7 26.4 %copy-start.25 = (bf16[8,32,256]{2,1,0:T(8,128)(2,1)S(1)}, bf16[8,32,256]{2,1,0:T(8,128)(2,1)}, u32[]{:S(2)}) copy-start(bf16[8,32,256]{2,1,0:T(8,128)(2,1)} %get-tuple-element.34) | copy-start | bytes 393220
  17.7 26.7 %copy-start.24 = (bf16[8,32,256]{2,1,0:T(8,128)(2,1)S(1)}, bf16[8,32,256]{2,1,0:T(8,128)(2,1)}, u32[]{:S(2)}) copy-start(bf16[8,32,256]{2,1,0:T(8,128)(2,1)} %get-tuple-element.35) | copy-start | bytes 393220
  17.7 29.1 %copy-start.1 = (bf16[32,4096]{1,0:T(8,128)(2,1)S(1)}, bf16[32,4096]{1,0:T(8,128)(2,1)}, u32[]{:S(2)}) copy-start(bf16[32,4096]{1,0:T(8,128)(2,1)} %param.10) | copy-start | bytes 786436
  29.4 14.7 %collective-permute-start.4 = (bf16[8,32,256]{2,1,0:T(8,128)(2,1)S(1)}, bf16[8,32,256]{2,1,0:T(8,128)(2,1)S(1)}, u32[]{:S(2)}, u32[]{:S(2)}) collective-permute-start(bf16[8,32,256]{2,1,0:T(8,128)(2,1)S(1)} %copy-done.30), channel_id=1, source_target_pairs={{0,5},{1,6},{2,7},{3,0},{4,1},{5,2},{6,3},{7,4},{8,13},{9,14},{10,... | collective-permute-start | bytes 393224 | tf_op jit(solution)/shard_map/ppermute | solution.py:397
  32.3 12.2 %collective-permute-start.5 = (bf16[8,32,256]{2,1,0:T(8,128)(2,1)S(1)}, bf16[8,32,256]{2,1,0:T(8,128)(2,1)S(1)}, u32[]{:S(2)}, u32[]{:S(2)}) collective-permute-start(bf16[8,32,256]{2,1,0:T(8,128)(2,1)S(1)} %copy-done.29), channel_id=1, source_target_pairs={{0,6},{1,7},{2,0},{3,1},{4,2},{5,3},{6,4},{7,5},{8,14},{9,15},{10,... | collective-permute-start | bytes 393224 | tf_op jit(solution)/shard_map/ppermute | solution.py:397
  32.9 14.7 %collective-permute-start.6 = (bf16[8,32,256]{2,1,0:T(8,128)(2,1)S(1)}, bf16[8,32,256]{2,1,0:T(8,128)(2,1)S(1)}, u32[]{:S(2)}, u32[]{:S(2)}) collective-permute-start(bf16[8,32,256]{2,1,0:T(8,128)(2,1)S(1)} %copy-done.28), channel_id=1, source_target_pairs={{0,7},{1,0},{2,1},{3,2},{4,3},{5,4},{6,5},{7,6},{8,15},{9,8},{10,9... | collective-permute-start | bytes 393224 | tf_op jit(solution)/shard_map/ppermute | solution.py:397
  33.9 13.7 %collective-permute-start = (bf16[8,32,256]{2,1,0:T(8,128)(2,1)S(1)}, bf16[8,32,256]{2,1,0:T(8,128)(2,1)S(1)}, u32[]{:S(2)}, u32[]{:S(2)}) collective-permute-start(bf16[8,32,256]{2,1,0:T(8,128)(2,1)S(1)} %copy-done.27), channel_id=1, source_target_pairs={{0,1},{1,2},{2,3},{3,4},{4,5},{5,6},{6,7},{7,0},{8,9},{9,10},{10,1... | collective-permute-start | bytes 393224 | tf_op jit(solution)/shard_map/ppermute | solution.py:397
  34.6 13.0 %collective-permute-start.1 = (bf16[8,32,256]{2,1,0:T(8,128)(2,1)S(1)}, bf16[8,32,256]{2,1,0:T(8,128)(2,1)S(1)}, u32[]{:S(2)}, u32[]{:S(2)}) collective-permute-start(bf16[8,32,256]{2,1,0:T(8,128)(2,1)S(1)} %copy-done.26), channel_id=1, source_target_pairs={{0,2},{1,3},{2,4},{3,5},{4,6},{5,7},{6,0},{7,1},{8,10},{9,11},{10,... | collective-permute-start | bytes 393224 | tf_op jit(solution)/shard_map/ppermute | solution.py:397
  44.1 8.4 %collective-permute-start.2 = (bf16[8,32,256]{2,1,0:T(8,128)(2,1)S(1)}, bf16[8,32,256]{2,1,0:T(8,128)(2,1)S(1)}, u32[]{:S(2)}, u32[]{:S(2)}) collective-permute-start(bf16[8,32,256]{2,1,0:T(8,128)(2,1)S(1)} %copy-done.25), channel_id=1, source_target_pairs={{0,3},{1,4},{2,5},{3,6},{4,7},{5,0},{6,1},{7,2},{8,11},{9,12},{10,... | collective-permute-start | bytes 393224 | tf_op jit(solution)/shard_map/ppermute | solution.py:397
  44.5 8.1 %collective-permute-start.3 = (bf16[8,32,256]{2,1,0:T(8,128)(2,1)S(1)}, bf16[8,32,256]{2,1,0:T(8,128)(2,1)S(1)}, u32[]{:S(2)}, u32[]{:S(2)}) collective-permute-start(bf16[8,32,256]{2,1,0:T(8,128)(2,1)S(1)} %copy-done.24), channel_id=1, source_target_pairs={{0,4},{1,5},{2,6},{3,7},{4,0},{5,1},{6,2},{7,3},{8,12},{9,13},{10,... | collective-permute-start | bytes 393224 | tf_op jit(solution)/shard_map/ppermute | solution.py:397
  70.1 61.0 %copy-start.9 = (bf16[8,136,128]{2,1,0:T(8,128)(2,1)S(1)}, bf16[8,136,128]{2,1,0:T(8,128)(2,1)}, u32[]{:S(2)}) copy-start(bf16[8,136,128]{2,1,0:T(8,128)(2,1)} %get-tuple-element.51) | copy-start | bytes 835588
  70.1 70.6 %copy-start.8 = (bf16[8,136,128]{2,1,0:T(8,128)(2,1)S(1)}, bf16[8,136,128]{2,1,0:T(8,128)(2,1)}, u32[]{:S(2)}) copy-start(bf16[8,136,128]{2,1,0:T(8,128)(2,1)} %get-tuple-element.52) | copy-start | bytes 835588
  70.1 83.3 %all-to-all-start.1 = ((bf16[128,136,128]{2,1,0:T(8,128)(2,1)}), bf16[128,136,128]{2,1,0:T(8,128)(2,1)}, u32[]{:S(2)}, u32[]{:S(2)}) async-start(bf16[128,136,128]{2,1,0:T(8,128)(2,1)} %get-tuple-element.53), calls=%async_computation.1 | async-start | bytes 8912896 | tf_op jit(solution)/shard_map/all_to_all | solution.py:383
  79.0 52.0 %collective-permute-start.7 = (bf16[8,136,128]{2,1,0:T(8,128)(2,1)S(1)}, bf16[8,136,128]{2,1,0:T(8,128)(2,1)S(1)}, u32[]{:S(2)}, u32[]{:S(2)}) collective-permute-start(bf16[8,136,128]{2,1,0:T(8,128)(2,1)S(1)} %copy-done.16), channel_id=1, source_target_pairs={{0,1},{1,2},{2,3},{3,4},{4,5},{5,6},{6,7},{7,0},{8,9},{9,10},{10,1... | collective-permute-start | bytes 835592 | tf_op jit(solution)/shard_map/ppermute | solution.py:397
  80.7 60.0 %collective-permute-start.8 = (bf16[8,136,128]{2,1,0:T(8,128)(2,1)S(1)}, bf16[8,136,128]{2,1,0:T(8,128)(2,1)S(1)}, u32[]{:S(2)}, u32[]{:S(2)}) collective-permute-start(bf16[8,136,128]{2,1,0:T(8,128)(2,1)S(1)} %copy-done.15), channel_id=1, source_target_pairs={{0,2},{1,3},{2,4},{3,5},{4,6},{5,7},{6,0},{7,1},{8,10},{9,11},{10,... | collective-permute-start | bytes 835592 | tf_op jit(solution)/shard_map/ppermute | solution.py:397
  81.9 61.2 %collective-permute-start.9 = (bf16[8,136,128]{2,1,0:T(8,128)(2,1)S(1)}, bf16[8,136,128]{2,1,0:T(8,128)(2,1)S(1)}, u32[]{:S(2)}, u32[]{:S(2)}) collective-permute-start(bf16[8,136,128]{2,1,0:T(8,128)(2,1)S(1)} %copy-done.13), channel_id=1, source_target_pairs={{0,3},{1,4},{2,5},{3,6},{4,7},{5,0},{6,1},{7,2},{8,11},{9,12},{10,... | collective-permute-start | bytes 835592 | tf_op jit(solution)/shard_map/ppermute | solution.py:397
  83.5 69.4 %collective-permute-start.10 = (bf16[8,136,128]{2,1,0:T(8,128)(2,1)S(1)}, bf16[8,136,128]{2,1,0:T(8,128)(2,1)S(1)}, u32[]{:S(2)}, u32[]{:S(2)}) collective-permute-start(bf16[8,136,128]{2,1,0:T(8,128)(2,1)S(1)} %copy-done.12), channel_id=1, source_target_pairs={{0,4},{1,5},{2,6},{3,7},{4,0},{5,1},{6,2},{7,3},{8,12},{9,13},{10,... | collective-permute-start | bytes 835592 | tf_op jit(solution)/shard_map/ppermute | solution.py:397
  84.1 69.3 %collective-permute-start.11 = (bf16[8,136,128]{2,1,0:T(8,128)(2,1)S(1)}, bf16[8,136,128]{2,1,0:T(8,128)(2,1)S(1)}, u32[]{:S(2)}, u32[]{:S(2)}) collective-permute-start(bf16[8,136,128]{2,1,0:T(8,128)(2,1)S(1)} %copy-done.10), channel_id=1, source_target_pairs={{0,5},{1,6},{2,7},{3,0},{4,1},{5,2},{6,3},{7,4},{8,13},{9,14},{10,... | collective-permute-start | bytes 835592 | tf_op jit(solution)/shard_map/ppermute | solution.py:397
  131.0 22.4 %copy-start.3 = (bf16[8,136,128]{2,1,0:T(8,128)(2,1)}, bf16[8,136,128]{2,1,0:T(8,128)(2,1)S(1)}, u32[]{:S(2)}) copy-start(bf16[8,136,128]{2,1,0:T(8,128)(2,1)S(1)} %collective-permute-done.7.refs_12_) | copy-start | bytes 835588
  131.1 22.4 %collective-permute-start.12 = (bf16[8,136,128]{2,1,0:T(8,128)(2,1)S(1)}, bf16[8,136,128]{2,1,0:T(8,128)(2,1)S(1)}, u32[]{:S(2)}, u32[]{:S(2)}) collective-permute-start(bf16[8,136,128]{2,1,0:T(8,128)(2,1)S(1)} %copy-done.9), channel_id=1, source_target_pairs={{0,6},{1,7},{2,0},{3,1},{4,2},{5,3},{6,4},{7,5},{8,14},{9,15},{10,... | collective-permute-start | bytes 835592 | tf_op jit(solution)/shard_map/ppermute | solution.py:397
  140.7 12.7 %collective-permute-start.13 = (bf16[8,136,128]{2,1,0:T(8,128)(2,1)S(1)}, bf16[8,136,128]{2,1,0:T(8,128)(2,1)S(1)}, u32[]{:S(2)}, u32[]{:S(2)}) collective-permute-start(bf16[8,136,128]{2,1,0:T(8,128)(2,1)S(1)} %copy-done.8), channel_id=1, source_target_pairs={{0,7},{1,0},{2,1},{3,2},{4,3},{5,4},{6,5},{7,6},{8,15},{9,8},{10,9... | collective-permute-start | bytes 835592 | tf_op jit(solution)/shard_map/ppermute | solution.py:397
  (23 other events, 177.2 us)

commit v4 on v3

--- a/solution.py
+++ b/solution.py
@@ -198,7 +198,9 @@
             tail = jnp.where(at == 2 * k, row[:, :half], jnp.where(at == 2 * k + 1, row[:, half:], tail))
         ext[b, 4 * width :] = tail.astype(bf16)
     for e in range(send_ref.shape[0]):
-        send_ref[e] = ext[far_index[e]]
+        block = far_index[e]
+        send_ref[e, 0:width] = ext[block, width : 2 * width]
+        send_ref[e, width:] = ext[block, 3 * width :]
     for d, ref in enumerate(around_refs, 1):
         mate = (place_ref[0] + d) % 8
         for e in range(pick):
@@ -212,7 +214,7 @@
     out = [
         jax.ShapeDtypeStruct(own_x.shape, f32),
         jax.ShapeDtypeStruct(own_x.shape, bf16),
-        jax.ShapeDtypeStruct((far.shape[0], 4 * width + 8, size // 2), bf16),
+        jax.ShapeDtypeStruct((far.shape[0], 2 * width + 8, size // 2), bf16),
     ] + [jax.ShapeDtypeStruct((pick, 4 * width + 8, size // 2), bf16)] * 7
     return call(
         first_kernel, "op_x", [SMEM] * 7 + [HBM] * 10 + [degree, p], out,
@@ -224,17 +226,21 @@
 
 def last_kernel(*refs):
     plan, tile_ref = refs[:4], refs[4]
-    near_x, near_refs, far_x_ref, far_ref = refs[5:12], refs[12:19], refs[19], refs[20]
-    degree_ref, x_ref, p_ref, image_ref, low_x_ref = refs[21:26]
-    search_ref, out_ref = refs[26:28]
-    pool, acc, held, sems, pool_sems, xs, sent = refs[28:]
+    near_x, near_refs, far_x_ref, far_p_ref, far_ref = refs[5:12], refs[12:19], refs[19], refs[20], refs[21]
+    degree_ref, x_ref, p_ref, image_ref, low_x_ref = refs[22:27]
+    search_ref, out_ref = refs[27:29]
+    pool, acc, held, sems, pool_sems, xs, sent, around = refs[29:]
     own, width, size = x_ref.shape
     pick = near_x[0].shape[0]
     near, far = 7 * pick, far_ref.shape[0]
-    pairs = [(far_ref, sent.at[pl.ds(near, far)]), (far_x_ref, xs.at[pl.ds(near, far)])]
+    pairs = [
+        (far_ref, sent),
+        (far_x_ref, xs.at[pl.ds(near, far)]),
+        (far_p_ref, pool.at[pl.ds(own + near, far), pl.ds(0, width)]),
+    ]
     for k in range(7):
         pairs.append((near_x[k], xs.at[pl.ds(k * pick, pick)]))
-        pairs.append((near_refs[k], sent.at[pl.ds(k * pick, pick)]))
+        pairs.append((near_refs[k], around.at[pl.ds(k * pick, pick)]))
     copies = copy_all(pairs, pool_sems)
     acc[...] = jnp.zeros_like(acc)
     copies[0].wait()
@@ -242,7 +248,7 @@
 
     def add(k, total):
         for e in range(8):
-            total = total + sent[near + k * 8 + e, 4 * width :].astype(f32)
+            total = total + sent[k * 8 + e, 2 * width :].astype(f32)
         return total
 
     sums = lax.fori_loop(0, far // 8, add, jnp.zeros((8, size // 2), f32))
@@ -269,13 +275,21 @@
         inv = 1.0 / (join(tail[0:1], tail[1:2]) + join(tail[2:3], tail[3:4]))
         return ((image.astype(f32) - ratio * x.astype(f32)) * inv).astype(bf16)
 
-    @pl.loop(0, (near + far) // 8)
+    @pl.loop(0, 7)
+    def _(k):
+        for e in range(pick):
+            m = k * pick + e
+            part = lambda r: join(
+                around[m, r * width : (r + 1) * width], around[m, (r + 2) * width : (r + 3) * width])
+            pool[own + m, 0:width] = part(0)
+            pool[own + m, width:] = form(part(1), xs[m], around[m, 4 * width :])
+
+    @pl.loop(0, far // 8)
     def _(k):
         for e in range(8):
             m = k * 8 + e
-            part = lambda r: join(sent[m, r * width : (r + 1) * width], sent[m, (r + 2) * width : (r + 3) * width])
-            pool[own + m, 0:width] = part(0)
-            pool[own + m, width:] = form(part(1), xs[m], sent[m, 4 * width :])
+            low = join(sent[m, 0:width], sent[m, width:two])
+            pool[own + near + m, width:] = form(low, xs[near + m], sent[m, two:])
 
     tile_sums(plan, tile_ref, pool, acc, held, sems)
     total = 0.0
@@ -289,23 +303,24 @@
     out_ref[:, 0, :] = jnp.concatenate([total[:, : 4 * width], rest], axis=0).T
 
 
-def op_ps(plan, tiles, near_x, near, far_x, far, degree, x, p, image, low_x):
+def op_ps(plan, tiles, near_x, near, far_x, far_p, far, degree, x, p, image, low_x):
     own, width, size = x.shape
     pick = near_x[0].shape[0]
     count = 7 * pick + far.shape[0]
     n = 3 * width
     out = [jax.ShapeDtypeStruct(x.shape, bf16), jax.ShapeDtypeStruct((4 * width, 1, n + n // 2), f32)]
     return call(
-        last_kernel, "op_ps", [SMEM] * 4 + [HBM] * 17 + [degree, x, p, image, low_x], out,
+        last_kernel, "op_ps", [SMEM] * 4 + [HBM] * 18 + [degree, x, p, image, low_x], out,
         [pltpu.VMEM((own + count, 2 * width, size), bf16), pltpu.VMEM((own + 1, 2 * width, size), f32)]
         + stream_scratch(size)
         + [
-            pltpu.SemaphoreType.DMA((16,)),
+            pltpu.SemaphoreType.DMA((17,)),
             pltpu.VMEM((count, width, size), bf16),
-            pltpu.VMEM((count, 4 * width + 8, size // 2), bf16),
+            pltpu.VMEM((far.shape[0], 2 * width + 8, size // 2), bf16),
+            pltpu.VMEM((7 * pick, 4 * width + 8, size // 2), bf16),
         ],
         1.2e10, tiles.size,
-    )(*plan, tiles, *near_x, *near, far_x, far, degree, x, p, image, low_x)
+    )(*plan, tiles, *near_x, *near, far_x, far_p, far, degree, x, p, image, low_x)
 
 
 def inverse(gram, eye, guess_ref, image_ref):
@@ -426,14 +441,18 @@
     degree = degree_of(tiles, tile_row, tile_count, diag_shift.reshape(own, size))
     late, degree = lax.optimization_barrier((rest[4:7], degree))
     near_x = pass_on(rest[:4] + late, inner)
-    p = vec_p.reshape(width, own, size).transpose(1, 0, 2)
-    p, late = lax.optimization_barrier((p, late))
+    p, *rest = cut("cut_p", own, far_index, near_index, spot, vec_p, 1)
+    far_p = rest[7]
+    p, far_p, late = lax.optimization_barrier((p, far_p, late))
+    far_x, near_x, far_p = lax.optimization_barrier((far_x, near_x, far_p))
+    far_p = exchange(far_p, BOTH)
 
     image, low_x, far, *near = op_x(
         plan, far_index, near_index, spot, tiles, x, near_x, far_x, degree, p)
+    far, far_p, near = lax.optimization_barrier((far, far_p, near))
     far = exchange(far, BOTH)
     near = pass_on(near, inner)
-    search, sums = op_ps(plan, tiles, near_x, near, far_x, far, degree, x, p, image, low_x)
+    search, sums = op_ps(plan, tiles, near_x, near, far_x, far_p, far, degree, x, p, image, low_x)
     return tuple(ritz(total(sums, devices), x, p, search))
 
 

time: 213 us -> 211 us (level)
  waiting for transfers between devices: 77.2 us -> 67.8 us
  starting transfers between devices: 39.9 us -> 44.7 us
    ppermute x14, waiting for transfers between devices: 77.2 us -> 52.9 us  [pass_on(): lax.ppermute(part, 'inner', [(k, (k + d) % inner) for k in range(inner)])]
    all_to_all x2 -> x3, waiting for transfers between devices: 0.01 us -> 14.9 us  [exchange(): return lax.all_to_all(a, axes, split_axis=0, concat_axis=0, tiled=True)]
    all_to_all x2 -> x3, starting transfers between devices: 20.4 us -> 25 us  [exchange(): return lax.all_to_all(a, axes, split_axis=0, concat_axis=0, tiled=True)]
    pallas_call x1 -> x2, Pallas kernels: 2.74 us -> 5.54 us  [cut(): call(functools.partial(cut_kernel, own), name, [SMEM] * 3 + [field], out,...]
    unnamed x62 -> x48, local copies, waits for them, and re-layouts: 2.34 us -> 4.28 us
  transfers between devices with their start and end apart: 16 -> 17, of which waited for: 8 -> 9; matrix products, arithmetic and copies ran while one was open for 1% -> 1% of each run, Pallas kernels for 5% -> 14%
where the time goes in v4:
time: 211 us
  waiting for transfers between devices  67.8 us (32%)
  Pallas kernels  58.6 us (28%)
  starting transfers between devices  44.7 us (21%)
  blocking collectives  31.2 us (15%)
  local copies, waits for them, and re-layouts  5.73 us (3%)
    ppermute x14, waiting for transfers between devices, pass_on(): lax.ppermute(part, 'inner', [(k, (k + d) % inner) for k in range(inner)])  52.9 us
    all_to_all x2, blocking collectives, exchange(): return lax.all_to_all(a, axes, split_axis=0, concat_axis=0, tiled=True)  31.2 us
    all_to_all x3, starting transfers between devices, exchange(): return lax.all_to_all(a, axes, split_axis=0, concat_axis=0, tiled=True)  25 us
    ppermute x14, starting transfers between devices, pass_on(): lax.ppermute(part, 'inner', [(k, (k + d) % inner) for k in range(inner)])  19.8 us
    pallas_call x1, Pallas kernels, op_ps(): call(last_kernel, 'op_ps', [SMEM] * 4 + [HBM] * 18 + [degree, x, p, image...  16.7 us
    pallas_call x1, Pallas kernels, op_x(): call(first_kernel, 'op_x', [SMEM] * 7 + [HBM] * 10 + [degree, p], out, [p...  15.3 us
    all_to_all x3, waiting for transfers between devices, exchange(): return lax.all_to_all(a, axes, split_axis=0, concat_axis=0, tiled=True)  14.9 us
    pallas_call x1, Pallas kernels, degree_of(): call(degree_kernel, 'degree', [SMEM, SMEM, HBM, shift], [jax.ShapeDtypeSt...  11.6 us
  transfers between devices with their start and end apart: 17, of which 9 were waited for; matrix products, arithmetic and copies ran while one was open for 1% of the time, Pallas kernels for 14%

profile of v4, /device:TPU:1, one launch (start us, length us, event | category | flops | bytes accessed | tf_op | source)
XLA Modules:
  0.0 210.6 jit_solution(5791623298744794061)
XLA Ops:
  0.6 2.8 %cut_x.1 = (bf16[16,32,256]{2,1,0:T(8,128)(2,1)}, bf16[8,32,256]{2,1,0:T(8,128)(2,1)}, bf16[8,32,256]{2,1,0:T(8,128)(2,1)}, bf16[8,32,256]{2,1,0:T(8,128)(2,1)},...) custom-call(s32[128]{0:T(128)} %bitcast.8, ...), custom_call_target="tpu_custom_call" | custom-call | bytes 1048576 | tf_op jit(solution)/shard_map/cut_x/pallas_call | solution.py:123
  3.4 11.5 %all-to-all-start = ((bf16[128,32,256]{2,1,0:T(8,128)(2,1)}), bf16[128,32,256]{2,1,0:T(8,128)(2,1)S(1)}, u32[]{:S(2)}, u32[]{:S(2)}) async-start(bf16[128,32,256]{2,1,0:T(8,128)(2,1)} %get-tuple-element.53), calls=%async_computation | async-start | bytes 4194304 | tf_op jit(solution)/shard_map/all_to_all | solution.py:398
  17.7 11.6 %degree.1.refs_17_.refs_22_ = f32[16,256]{1,0:T(8,128)} custom-call(s32[192]{0:T(256)} %refs_0_.1, s32[1]{0:T(128)S(6)} %copy.11.count_ref.refs_2_, bf16[192,256,256]{2,1,0:T(8,128)(2,1)} %refs_4_.1, f32[16,256]{1,0:T(8,128)} %reshape.54.shift_ref), custom_call_target="tpu_custom_call" | custom-call | flops 12000000000 | bytes 12582912 | tf_op jit(solution)/shard_map/degree/pallas_call | solution.py:96
  29.4 2.9 %collective-permute-start.4 = (bf16[8,32,256]{2,1,0:T(8,128)(2,1)S(1)}, bf16[8,32,256]{2,1,0:T(8,128)(2,1)S(1)}, u32[]{:S(2)}, u32[]{:S(2)}) collective-permute-start(bf16[8,32,256]{2,1,0:T(8,128)(2,1)S(1)} %copy-done.23), channel_id=1, source_target_pairs={{0,5},{1,6},{2,7},{3,0},{4,1},{5,2},{6,3},{7,4},{8,13},{9,14},{10,... | collective-permute-start | bytes 393224 | tf_op jit(solution)/shard_map/ppermute | solution.py:412
  35.5 8.6 %collective-permute-done.4.refs_13_.refs_9_ = bf16[8,32,256]{2,1,0:T(8,128)(2,1)S(1)} collective-permute-done((bf16[8,32,256]{2,1,0:T(8,128)(2,1)S(1)}, bf16[8,32,256]{2,1,0:T(8,128)(2,1)S(1)}, u32[]{:S(2)}, u32[]{:S(2)}) %collective-permute-start.4) | collective-permute-done | bytes 131104 | tf_op jit(solution)/shard_map/ppermute | solution.py:412
  44.5 2.4 %collective-permute-start.3 = (bf16[8,32,256]{2,1,0:T(8,128)(2,1)S(1)}, bf16[8,32,256]{2,1,0:T(8,128)(2,1)S(1)}, u32[]{:S(2)}, u32[]{:S(2)}) collective-permute-start(bf16[8,32,256]{2,1,0:T(8,128)(2,1)S(1)} %copy-done.17), channel_id=1, source_target_pairs={{0,4},{1,5},{2,6},{3,7},{4,0},{5,1},{6,2},{7,3},{8,12},{9,13},{10,... | collective-permute-start | bytes 393224 | tf_op jit(solution)/shard_map/ppermute | solution.py:412
  46.9 2.8 %cut_p.1 = (bf16[16,32,256]{2,1,0:T(8,128)(2,1)}, bf16[8,32,256]{2,1,0:T(8,128)(2,1)}, bf16[8,32,256]{2,1,0:T(8,128)(2,1)}, bf16[8,32,256]{2,1,0:T(8,128)(2,1)},...) custom-call(s32[128]{0:T(128)} %bitcast.9, ...), custom_call_target="tpu_custom_call" | custom-call | bytes 1048576 | tf_op jit(solution)/shard_map/cut_p/pallas_call | solution.py:123
  49.7 2.8 %collective-permute-done.2.refs_11_.refs_7_ = bf16[8,32,256]{2,1,0:T(8,128)(2,1)S(1)} collective-permute-done((bf16[8,32,256]{2,1,0:T(8,128)(2,1)S(1)}, bf16[8,32,256]{2,1,0:T(8,128)(2,1)S(1)}, u32[]{:S(2)}, u32[]{:S(2)}) %collective-permute-start.2) | collective-permute-done | bytes 131104 | tf_op jit(solution)/shard_map/ppermute | solution.py:412
  54.0 9.0 %all-to-all-start.1 = ((bf16[128,32,256]{2,1,0:T(8,128)(2,1)}), bf16[128,32,256]{2,1,0:T(8,128)(2,1)}, u32[]{:S(2)}, u32[]{:S(2)}) async-start(bf16[128,32,256]{2,1,0:T(8,128)(2,1)} %get-tuple-element.79), calls=%async_computation.1 | async-start | bytes 4194304 | tf_op jit(solution)/shard_map/all_to_all | solution.py:398
  63.0 15.3 %op_x.1 = (f32[16,32,256]{2,1,0:T(8,128)}, bf16[16,32,256]{2,1,0:T(8,128)(2,1)}, bf16[128,72,128]{2,1,0:T(8,128)(2,1)}, bf16[8,136,128]{2,1,0:T(8,128)(2,1)}, bf...) custom-call(s32[192]{0:T(256)} %refs_0_.1, ...), custom_call_target="tpu_custom_call" | custom-call | flops 12000000000 | bytes 12582912 | tf_op jit(solution)/shard_map/op_x/pallas_call | solution.py:219
  78.2 14.9 %all-to-all-done.1.refs_20_ = bf16[128,32,256]{2,1,0:T(8,128)(2,1)} async-done(((bf16[128,32,256]{2,1,0:T(8,128)(2,1)}), bf16[128,32,256]{2,1,0:T(8,128)(2,1)}, u32[]{:S(2)}, u32[]{:S(2)}) %all-to-all-start.1) | async-done | bytes 2097184 | tf_op jit(solution)/shard_map/all_to_all | solution.py:398
  93.1 4.5 %all-to-all-start.2 = ((bf16[128,72,128]{2,1,0:T(8,128)(2,1)}), bf16[128,72,128]{2,1,0:T(8,128)(2,1)S(1)}, u32[]{:S(2)}, u32[]{:S(2)}) async-start(bf16[128,72,128]{2,1,0:T(8,128)(2,1)} %get-tuple-element.95), calls=%async_computation.2 | async-start | bytes 4718592 | tf_op jit(solution)/shard_map/all_to_all | solution.py:398
  97.6 1.6 collective-permute-start.7
  100.5 1.7 collective-permute-start.9
  102.7 2.5 %collective-permute-start.11 = (bf16[8,136,128]{2,1,0:T(8,128)(2,1)}, bf16[8,136,128]{2,1,0:T(8,128)(2,1)S(1)}, u32[]{:S(2)}, u32[]{:S(2)}) collective-permute-start(bf16[8,136,128]{2,1,0:T(8,128)(2,1)} %get-tuple-element.91), channel_id=1, source_target_pairs={{0,5},{1,6},{2,7},{3,0},{4,1},{5,2},{6,3},{7,4},{8,13},{9,14},{10,... | collective-permute-start | bytes 835592 | tf_op jit(solution)/shard_map/ppermute | solution.py:412
  105.2 22.3 %collective-permute-done.7.refs_12_ = bf16[8,136,128]{2,1,0:T(8,128)(2,1)S(1)} collective-permute-done((bf16[8,136,128]{2,1,0:T(8,128)(2,1)}, bf16[8,136,128]{2,1,0:T(8,128)(2,1)S(1)}, u32[]{:S(2)}, u32[]{:S(2)}) %collective-permute-start.7) | collective-permute-done | bytes 278560 | tf_op jit(solution)/shard_map/ppermute | solution.py:412
  127.6 3.4 %collective-permute-start.12 = (bf16[8,136,128]{2,1,0:T(8,128)(2,1)}, bf16[8,136,128]{2,1,0:T(8,128)(2,1)S(1)}, u32[]{:S(2)}, u32[]{:S(2)}) collective-permute-start(bf16[8,136,128]{2,1,0:T(8,128)(2,1)} %get-tuple-element.92), channel_id=1, source_target_pairs={{0,6},{1,7},{2,0},{3,1},{4,2},{5,3},{6,4},{7,5},{8,14},{9,15},{10,... | collective-permute-start | bytes 835592 | tf_op jit(solution)/shard_map/ppermute | solution.py:412
  131.0 6.3 %collective-permute-done.8.refs_13_ = bf16[8,136,128]{2,1,0:T(8,128)(2,1)S(1)} collective-permute-done((bf16[8,136,128]{2,1,0:T(8,128)(2,1)}, bf16[8,136,128]{2,1,0:T(8,128)(2,1)S(1)}, u32[]{:S(2)}, u32[]{:S(2)}) %collective-permute-start.8) | collective-permute-done | bytes 278560 | tf_op jit(solution)/shard_map/ppermute | solution.py:412
  137.3 2.2 %collective-permute-done.9.refs_14_ = bf16[8,136,128]{2,1,0:T(8,128)(2,1)S(1)} collective-permute-done((bf16[8,136,128]{2,1,0:T(8,128)(2,1)}, bf16[8,136,128]{2,1,0:T(8,128)(2,1)S(1)}, u32[]{:S(2)}, u32[]{:S(2)}) %collective-permute-start.9) | collective-permute-done | bytes 278560 | tf_op jit(solution)/shard_map/ppermute | solution.py:412
  139.5 10.0 %collective-permute-done.10.refs_15_ = bf16[8,136,128]{2,1,0:T(8,128)(2,1)S(1)} collective-permute-done((bf16[8,136,128]{2,1,0:T(8,128)(2,1)}, bf16[8,136,128]{2,1,0:T(8,128)(2,1)S(1)}, u32[]{:S(2)}, u32[]{:S(2)}) %collective-permute-start.10) | collective-permute-done | bytes 278560 | tf_op jit(solution)/shard_map/ppermute | solution.py:412
  152.9 16.7 %op_ps.1 = (bf16[16,32,256]{2,1,0:T(8,128)(2,1)}, f32[128,1,144]{2,1,0:T(1,128)}) custom-call(s32[192]{0:T(256)} %refs_0_.1, s32[192]{0:T(256)} %refs_1_.3, s32[1]{0:T(128)S(6)} %copy.11.count_ref.refs_2_, s32[208]{0:T(256)} %pad_add_fusion.refs_3_, bf16[192,256,256]{2,1,0:T(8,128)(2,1)} %refs_4_.1, bf16[8,32,256]{2,1,0:T(8,128)(2,1)} %copy-done.13, ...), custom_call_target="tpu_custom_call" | custom-call | flops 12000000000 | bytes 12582912 | tf_op jit(solution)/shard_map/op_ps/pallas_call | solution.py:312
  169.6 17.1 %all_to_all.25 = f32[128,1,144]{2,1,0:T(1,128)S(1)} all-to-all(f32[128,1,144]{2,1,0:T(1,128)} %get-tuple-element.98), channel_id=1, replica_groups=mesh['comm'=16,'inner'=8] {'comm','inner'}, dimensions={0} | all-to-all | bytes 147456 | tf_op jit(solution)/shard_map/all_to_all | solution.py:398
  186.9 14.2 %all_to_all.26.sums_ref = f32[128,1,144]{2,1,0:T(1,128)} all-to-all(f32[128,1,144]{2,1,0:T(1,128)S(1)} %broadcast_in_dim.30), channel_id=1, replica_groups=mesh['comm'=16,'inner'=8] {'comm','inner'}, dimensions={0} | all-to-all | bytes 147456 | tf_op jit(solution)/shard_map/all_to_all | solution.py:398
  201.1 9.4 %ritz.1 = (f32[32,4096]{1,0:T(8,128)}, f32[32,4096]{1,0:T(8,128)}) custom-call(f32[128,1,144]{2,1,0:T(1,128)} %all_to_all.26.sums_ref, bf16[16,32,256]{2,1,0:T(8,128)(2,1)} %get-tuple-element.74.refs_8_.refs_23_.x_ref, bf16[16,32,256]{2,1,0:T(8,128)(2,1)} %get-tuple-element.77.refs_18_.refs_24_.p_ref, bf16[16,32,256]{2,1,0:T(8,128)(2,1)} %get-tuple-element.99.s_ref), custom_call_target="tpu_custom_call" | custom-call | flops 4000000000 | bytes 2097152 | tf_op jit(solution)/shard_map/ritz/pallas_call | solution.py:391
  (77 shorter events, 12.4 us)
Async XLA Ops:
  3.4 49.2 %all-to-all-start = ((bf16[128,32,256]{2,1,0:T(8,128)(2,1)}), bf16[128,32,256]{2,1,0:T(8,128)(2,1)S(1)}, u32[]{:S(2)}, u32[]{:S(2)}) async-start(bf16[128,32,256]{2,1,0:T(8,128)(2,1)} %get-tuple-element.53), calls=%async_computation | async-start | bytes 4194304 | tf_op jit(solution)/shard_map/all_to_all | solution.py:398
  17.7 15.1 %copy-start.21 = (bf16[8,32,256]{2,1,0:T(8,128)(2,1)S(1)}, bf16[8,32,256]{2,1,0:T(8,128)(2,1)}, u32[]{:S(2)}) copy-start(bf16[8,32,256]{2,1,0:T(8,128)(2,1)} %get-tuple-element.63) | copy-start | bytes 393220
  17.7 16.2 %copy-start.20 = (bf16[8,32,256]{2,1,0:T(8,128)(2,1)S(1)}, bf16[8,32,256]{2,1,0:T(8,128)(2,1)}, u32[]{:S(2)}) copy-start(bf16[8,32,256]{2,1,0:T(8,128)(2,1)} %get-tuple-element.54) | copy-start | bytes 393220
  17.7 16.9 %copy-start.19 = (bf16[8,32,256]{2,1,0:T(8,128)(2,1)S(1)}, bf16[8,32,256]{2,1,0:T(8,128)(2,1)}, u32[]{:S(2)}) copy-start(bf16[8,32,256]{2,1,0:T(8,128)(2,1)} %get-tuple-element.55) | copy-start | bytes 393220
  17.7 26.4 %copy-start.18 = (bf16[8,32,256]{2,1,0:T(8,128)(2,1)S(1)}, bf16[8,32,256]{2,1,0:T(8,128)(2,1)}, u32[]{:S(2)}) copy-start(bf16[8,32,256]{2,1,0:T(8,128)(2,1)} %get-tuple-element.56) | copy-start | bytes 393220
  17.7 26.7 %copy-start.17 = (bf16[8,32,256]{2,1,0:T(8,128)(2,1)S(1)}, bf16[8,32,256]{2,1,0:T(8,128)(2,1)}, u32[]{:S(2)}) copy-start(bf16[8,32,256]{2,1,0:T(8,128)(2,1)} %get-tuple-element.57) | copy-start | bytes 393220
  29.4 14.7 %collective-permute-start.4 = (bf16[8,32,256]{2,1,0:T(8,128)(2,1)S(1)}, bf16[8,32,256]{2,1,0:T(8,128)(2,1)S(1)}, u32[]{:S(2)}, u32[]{:S(2)}) collective-permute-start(bf16[8,32,256]{2,1,0:T(8,128)(2,1)S(1)} %copy-done.23), channel_id=1, source_target_pairs={{0,5},{1,6},{2,7},{3,0},{4,1},{5,2},{6,3},{7,4},{8,13},{9,14},{10,... | collective-permute-start | bytes 393224 | tf_op jit(solution)/shard_map/ppermute | solution.py:412
  32.3 12.2 %collective-permute-start.5 = (bf16[8,32,256]{2,1,0:T(8,128)(2,1)S(1)}, bf16[8,32,256]{2,1,0:T(8,128)(2,1)S(1)}, u32[]{:S(2)}, u32[]{:S(2)}) collective-permute-start(bf16[8,32,256]{2,1,0:T(8,128)(2,1)S(1)} %copy-done.22), channel_id=1, source_target_pairs={{0,6},{1,7},{2,0},{3,1},{4,2},{5,3},{6,4},{7,5},{8,14},{9,15},{10,... | collective-permute-start | bytes 393224 | tf_op jit(solution)/shard_map/ppermute | solution.py:412
  32.8 16.8 %collective-permute-start.6 = (bf16[8,32,256]{2,1,0:T(8,128)(2,1)S(1)}, bf16[8,32,256]{2,1,0:T(8,128)(2,1)S(1)}, u32[]{:S(2)}, u32[]{:S(2)}) collective-permute-start(bf16[8,32,256]{2,1,0:T(8,128)(2,1)S(1)} %copy-done.21), channel_id=1, source_target_pairs={{0,7},{1,0},{2,1},{3,2},{4,3},{5,4},{6,5},{7,6},{8,15},{9,8},{10,9... | collective-permute-start | bytes 393224 | tf_op jit(solution)/shard_map/ppermute | solution.py:412
  33.9 15.8 %collective-permute-start = (bf16[8,32,256]{2,1,0:T(8,128)(2,1)S(1)}, bf16[8,32,256]{2,1,0:T(8,128)(2,1)S(1)}, u32[]{:S(2)}, u32[]{:S(2)}) collective-permute-start(bf16[8,32,256]{2,1,0:T(8,128)(2,1)S(1)} %copy-done.20), channel_id=1, source_target_pairs={{0,1},{1,2},{2,3},{3,4},{4,5},{5,6},{6,7},{7,0},{8,9},{9,10},{10,1... | collective-permute-start | bytes 393224 | tf_op jit(solution)/shard_map/ppermute | solution.py:412
  34.6 15.1 %collective-permute-start.1 = (bf16[8,32,256]{2,1,0:T(8,128)(2,1)S(1)}, bf16[8,32,256]{2,1,0:T(8,128)(2,1)S(1)}, u32[]{:S(2)}, u32[]{:S(2)}) collective-permute-start(bf16[8,32,256]{2,1,0:T(8,128)(2,1)S(1)} %copy-done.19), channel_id=1, source_target_pairs={{0,2},{1,3},{2,4},{3,5},{4,6},{5,7},{6,0},{7,1},{8,10},{9,11},{10,... | collective-permute-start | bytes 393224 | tf_op jit(solution)/shard_map/ppermute | solution.py:412
  44.1 8.4 %collective-permute-start.2 = (bf16[8,32,256]{2,1,0:T(8,128)(2,1)S(1)}, bf16[8,32,256]{2,1,0:T(8,128)(2,1)S(1)}, u32[]{:S(2)}, u32[]{:S(2)}) collective-permute-start(bf16[8,32,256]{2,1,0:T(8,128)(2,1)S(1)} %copy-done.18), channel_id=1, source_target_pairs={{0,3},{1,4},{2,5},{3,6},{4,7},{5,0},{6,1},{7,2},{8,11},{9,12},{10,... | collective-permute-start | bytes 393224 | tf_op jit(solution)/shard_map/ppermute | solution.py:412
  44.5 8.1 %collective-permute-start.3 = (bf16[8,32,256]{2,1,0:T(8,128)(2,1)S(1)}, bf16[8,32,256]{2,1,0:T(8,128)(2,1)S(1)}, u32[]{:S(2)}, u32[]{:S(2)}) collective-permute-start(bf16[8,32,256]{2,1,0:T(8,128)(2,1)S(1)} %copy-done.17), channel_id=1, source_target_pairs={{0,4},{1,5},{2,6},{3,7},{4,0},{5,1},{6,2},{7,3},{8,12},{9,13},{10,... | collective-permute-start | bytes 393224 | tf_op jit(solution)/shard_map/ppermute | solution.py:412
  54.0 39.2 %all-to-all-start.1 = ((bf16[128,32,256]{2,1,0:T(8,128)(2,1)}), bf16[128,32,256]{2,1,0:T(8,128)(2,1)}, u32[]{:S(2)}, u32[]{:S(2)}) async-start(bf16[128,32,256]{2,1,0:T(8,128)(2,1)} %get-tuple-element.79), calls=%async_computation.1 | async-start | bytes 4194304 | tf_op jit(solution)/shard_map/all_to_all | solution.py:398
  93.1 44.2 %copy-start.6 = (bf16[8,136,128]{2,1,0:T(8,128)(2,1)S(1)}, bf16[8,136,128]{2,1,0:T(8,128)(2,1)}, u32[]{:S(2)}) copy-start(bf16[8,136,128]{2,1,0:T(8,128)(2,1)} %get-tuple-element.93) | copy-start | bytes 835588
  93.1 58.3 %all-to-all-start.2 = ((bf16[128,72,128]{2,1,0:T(8,128)(2,1)}), bf16[128,72,128]{2,1,0:T(8,128)(2,1)S(1)}, u32[]{:S(2)}, u32[]{:S(2)}) async-start(bf16[128,72,128]{2,1,0:T(8,128)(2,1)} %get-tuple-element.95), calls=%async_computation.2 | async-start | bytes 4718592 | tf_op jit(solution)/shard_map/all_to_all | solution.py:398
  97.6 29.9 %collective-permute-start.7 = (bf16[8,136,128]{2,1,0:T(8,128)(2,1)}, bf16[8,136,128]{2,1,0:T(8,128)(2,1)S(1)}, u32[]{:S(2)}, u32[]{:S(2)}) collective-permute-start(bf16[8,136,128]{2,1,0:T(8,128)(2,1)} %get-tuple-element.87), channel_id=1, source_target_pairs={{0,1},{1,2},{2,3},{3,4},{4,5},{5,6},{6,7},{7,0},{8,9},{9,10},{10,1... | collective-permute-start | bytes 835592 | tf_op jit(solution)/shard_map/ppermute | solution.py:412
  99.3 38.0 %collective-permute-start.8 = (bf16[8,136,128]{2,1,0:T(8,128)(2,1)}, bf16[8,136,128]{2,1,0:T(8,128)(2,1)S(1)}, u32[]{:S(2)}, u32[]{:S(2)}) collective-permute-start(bf16[8,136,128]{2,1,0:T(8,128)(2,1)} %get-tuple-element.88), channel_id=1, source_target_pairs={{0,2},{1,3},{2,4},{3,5},{4,6},{5,7},{6,0},{7,1},{8,10},{9,11},{10,... | collective-permute-start | bytes 835592 | tf_op jit(solution)/shard_map/ppermute | solution.py:412
  100.5 39.0 %collective-permute-start.9 = (bf16[8,136,128]{2,1,0:T(8,128)(2,1)}, bf16[8,136,128]{2,1,0:T(8,128)(2,1)S(1)}, u32[]{:S(2)}, u32[]{:S(2)}) collective-permute-start(bf16[8,136,128]{2,1,0:T(8,128)(2,1)} %get-tuple-element.89), channel_id=1, source_target_pairs={{0,3},{1,4},{2,5},{3,6},{4,7},{5,0},{6,1},{7,2},{8,11},{9,12},{10,... | collective-permute-start | bytes 835592 | tf_op jit(solution)/shard_map/ppermute | solution.py:412
  102.2 47.4 %collective-permute-start.10 = (bf16[8,136,128]{2,1,0:T(8,128)(2,1)}, bf16[8,136,128]{2,1,0:T(8,128)(2,1)S(1)}, u32[]{:S(2)}, u32[]{:S(2)}) collective-permute-start(bf16[8,136,128]{2,1,0:T(8,128)(2,1)} %get-tuple-element.90), channel_id=1, source_target_pairs={{0,4},{1,5},{2,6},{3,7},{4,0},{5,1},{6,2},{7,3},{8,12},{9,13},{10,... | collective-permute-start | bytes 835592 | tf_op jit(solution)/shard_map/ppermute | solution.py:412
  102.7 47.3 %collective-permute-start.11 = (bf16[8,136,128]{2,1,0:T(8,128)(2,1)}, bf16[8,136,128]{2,1,0:T(8,128)(2,1)S(1)}, u32[]{:S(2)}, u32[]{:S(2)}) collective-permute-start(bf16[8,136,128]{2,1,0:T(8,128)(2,1)} %get-tuple-element.91), channel_id=1, source_target_pairs={{0,5},{1,6},{2,7},{3,0},{4,1},{5,2},{6,3},{7,4},{8,13},{9,14},{10,... | collective-permute-start | bytes 835592 | tf_op jit(solution)/shard_map/ppermute | solution.py:412
  127.6 23.9 %copy-start.3 = (bf16[8,136,128]{2,1,0:T(8,128)(2,1)}, bf16[8,136,128]{2,1,0:T(8,128)(2,1)S(1)}, u32[]{:S(2)}) copy-start(bf16[8,136,128]{2,1,0:T(8,128)(2,1)S(1)} %collective-permute-done.7.refs_12_) | copy-start | bytes 835588
  127.6 22.4 %collective-permute-start.12 = (bf16[8,136,128]{2,1,0:T(8,128)(2,1)}, bf16[8,136,128]{2,1,0:T(8,128)(2,1)S(1)}, u32[]{:S(2)}, u32[]{:S(2)}) collective-permute-start(bf16[8,136,128]{2,1,0:T(8,128)(2,1)} %get-tuple-element.92), channel_id=1, source_target_pairs={{0,6},{1,7},{2,0},{3,1},{4,2},{5,3},{6,4},{7,5},{8,14},{9,15},{10,... | collective-permute-start | bytes 835592 | tf_op jit(solution)/shard_map/ppermute | solution.py:412
  137.3 14.1 %collective-permute-start.13 = (bf16[8,136,128]{2,1,0:T(8,128)(2,1)S(1)}, bf16[8,136,128]{2,1,0:T(8,128)(2,1)}, u32[]{:S(2)}, u32[]{:S(2)}) collective-permute-start(bf16[8,136,128]{2,1,0:T(8,128)(2,1)S(1)} %copy-done.6), channel_id=1, source_target_pairs={{0,7},{1,0},{2,1},{3,2},{4,3},{5,4},{6,5},{7,6},{8,15},{9,8},{10,9... | collective-permute-start | bytes 835592 | tf_op jit(solution)/shard_map/ppermute | solution.py:412
  (17 other events, 97.7 us)

commit v5 on v4

--- a/solution.py
+++ b/solution.py
@@ -99,29 +99,39 @@
     )(tile_row, tile_count, tiles, shift)[0]
 
 
-def cut_kernel(own, far_index, near_index, place_ref, field_ref, *outs):
-    blocks_ref = outs[0]
+def cut_kernel(own, far_index, near_index, place_ref, field_ref, blocks_ref, *outs):
+    step = pl.program_id(0)
     size = blocks_ref.shape[2]
-    for b in range(own):
-        blocks_ref[b] = field_ref[:, b * size : (b + 1) * size]
-    nears = outs[1:8]
-    pick = nears[0].shape[0]
-    for d, near_ref in enumerate(nears, 1):
-        mate = (place_ref[0] + d) % (len(nears) + 1)
-        for e in range(pick):
-            near_ref[e] = blocks_ref[near_index[mate, e]]
-    for far_ref in outs[8:]:
-        for e in range(far_ref.shape[0]):
-            far_ref[e] = blocks_ref[far_index[e]]
-
-
-def cut(name, own, far_index, near_index, place, field, far):
+    nears, far_ref = outs[:7], outs[7]
+    pick, count = nears[0].shape[0], far_ref.shape[0]
+
+    @pl.when(step == 0)
+    def _():
+        for b in range(own):
+            blocks_ref[b] = field_ref[:, b * size : (b + 1) * size]
+        for d, near_ref in enumerate(nears, 1):
+            mate = (place_ref[0] + d) % (len(nears) + 1)
+            for e in range(pick):
+                near_ref[e] = blocks_ref[near_index[mate, e]]
+
+    for e in range(count):
+        far_ref[e] = blocks_ref[far_index[step * count + e]]
+
+
+def cut(name, own, far_index, near_index, place, field, steps=4):
     width, size = field.shape[0], field.shape[1] // own
-    pick = near_index.shape[1]
+    pick, count = near_index.shape[1], far_index.shape[0]
     shape = lambda n: jax.ShapeDtypeStruct((n, width, size), bf16)
-    out = [shape(own)] + [shape(pick)] * 7 + [shape(far_index.shape[0])] * far
-    return call(
-        functools.partial(cut_kernel, own), name, [SMEM] * 3 + [field], out, [], 0, 8 * field.size,
+    held = lambda n: pl.BlockSpec((n, width, size), lambda g: (0, 0, 0))
+    return pl.pallas_call(
+        functools.partial(cut_kernel, own),
+        grid=(steps,),
+        in_specs=[SMEM] * 3 + [pl.BlockSpec(field.shape, lambda g: (0, 0))],
+        out_specs=[held(own)] + [held(pick)] * 7 + [pl.BlockSpec((count // steps, width, size), lambda g: (g, 0, 0))],
+        out_shape=[shape(own)] + [shape(pick)] * 7 + [shape(count)],
+        compiler_params=pltpu.CompilerParams(vmem_limit_bytes=LIMIT * MIB),
+        cost_estimate=cost(0, 8 * field.size),
+        name=name,
     )(far_index, near_index, place, field)
 
 
@@ -330,6 +340,13 @@
     bound = jnp.max(jnp.sum(jnp.abs(scaled), axis=1, keepdims=True))
     rough = scaled.astype(bf16)
 
+    def improve_roughly(state):
+        count, _ = state
+        guess = guess_ref[...].astype(bf16)
+        image = jnp.dot(rough, guess, preferred_element_type=f32)
+        guess_ref[...] = jnp.dot(guess, (2.0 * eye - image).astype(bf16), preferred_element_type=f32)
+        return count + 1, jnp.max(jnp.abs(eye - image))
+
     def improve(state):
         count, _ = state
         image = image_ref[...]
@@ -339,13 +356,9 @@
         return count + 1, jnp.max(jnp.abs(eye - image))
 
     start = (jnp.int32(0), jnp.float32(1.0))
-    guess = eye / bound
-    for _ in range(8):
-        guess = guess.astype(bf16)
-        image = jnp.dot(rough, guess, preferred_element_type=f32)
-        guess = jnp.dot(guess, (2.0 * eye - image).astype(bf16), preferred_element_type=f32)
-    guess_ref[...] = guess
-    image_ref[...] = exact_dot(scaled, guess)
+    guess_ref[...] = eye / bound
+    lax.while_loop(lambda state: (state[1] > 0.1) & (state[0] < 12), improve_roughly, start)
+    image_ref[...] = exact_dot(scaled, guess_ref[...])
     away = jnp.max(jnp.sum(jnp.abs(eye - image_ref[...]), axis=1, keepdims=True))
 
     @pl.when(jnp.logical_not(away < 0.9))
@@ -357,7 +370,8 @@
     return exact_dot(guess_ref[...], 2.0 * eye - image_ref[...]) * root_row * root_col
 
 
-def ritz_kernel(sums_ref, x_ref, p_ref, s_ref, out_x_ref, out_p_ref, guess_ref, image_ref):
+def ritz_kernel(sums_ref, x_hbm, p_hbm, s_hbm, out_x_ref, out_p_ref, guess_ref, image_ref, x_ref, p_ref, s_ref, sems):
+    copies = copy_all([(x_hbm, x_ref), (p_hbm, p_ref), (s_hbm, s_ref)], sems)
     width = x_ref.shape[1]
     n = 3 * width
     eye = (lax.broadcasted_iota(i32, (n, n), 0) == lax.broadcasted_iota(i32, (n, n), 1)).astype(f32)
@@ -378,6 +392,8 @@
     lanes = lax.broadcasted_iota(i32, coeff.shape, 1)
     both = jnp.concatenate([coeff, jnp.where(lanes < width, 0.0, coeff)], axis=0).astype(bf16)
     size = x_ref.shape[2]
+    for copy in copies:
+        copy.wait()
     for b in range(out_x_ref.shape[1] // size):
         basis = jnp.concatenate([x_ref[b], p_ref[b], s_ref[b]], axis=0)
         out = jnp.dot(both, basis, preferred_element_type=f32)
@@ -389,8 +405,9 @@
     own, width, size = p.shape
     shape = jax.ShapeDtypeStruct((width, own * size), f32)
     return call(
-        ritz_kernel, "ritz", [sums, x, p, search], [shape, shape],
-        [pltpu.VMEM((3 * width, 3 * width), f32)] * 2, 4e9, 2 * MIB,
+        ritz_kernel, "ritz", [sums, HBM, HBM, HBM], [shape, shape],
+        [pltpu.VMEM((3 * width, 3 * width), f32)] * 2
+        + [pltpu.VMEM(p.shape, bf16)] * 3 + [pltpu.SemaphoreType.DMA((3,))], 4e9, 2 * MIB,
     )(sums, x, p, search)
 
 
@@ -434,14 +451,14 @@
     ])
     spot = place.reshape(1)
 
-    x, *rest = cut("cut_x", own, far_index, near_index, spot, vec_x, 1)
+    x, *rest = cut("cut_x", own, far_index, near_index, spot, vec_x)
     far_x = exchange(rest[7], BOTH)
     tile_row, table = lax.optimization_barrier((tile_row, table))
     plan = (tile_row, tile_col, tile_count, table)
     degree = degree_of(tiles, tile_row, tile_count, diag_shift.reshape(own, size))
     late, degree = lax.optimization_barrier((rest[4:7], degree))
     near_x = pass_on(rest[:4] + late, inner)
-    p, *rest = cut("cut_p", own, far_index, near_index, spot, vec_p, 1)
+    p, *rest = cut("cut_p", own, far_index, near_index, spot, vec_p)
     far_p = rest[7]
     p, far_p, late = lax.optimization_barrier((p, far_p, late))
     far_x, near_x, far_p = lax.optimization_barrier((far_x, near_x, far_p))

time: 211 us -> 212 us (level)
  no operation moved by 1% of the time
where the time goes in v5:
time: 212 us; the launch traced here: 211 us
  waiting for transfers between devices  67.2 us (32%)
  Pallas kernels  59.7 us (28%)
  starting transfers between devices  44.8 us (21%)
  blocking collectives  31.2 us (15%)
  local copies, waits for them, and re-layouts  5.73 us (3%)
    ppermute x14, waiting for transfers between devices, pass_on(): lax.ppermute(part, 'inner', [(k, (k + d) % inner) for k in range(inner)])  52.3 us
    all_to_all x2, blocking collectives, exchange(): return lax.all_to_all(a, axes, split_axis=0, concat_axis=0, tiled=True)  31.2 us
    all_to_all x3, starting transfers between devices, exchange(): return lax.all_to_all(a, axes, split_axis=0, concat_axis=0, tiled=True)  25 us
    ppermute x14, starting transfers between devices, pass_on(): lax.ppermute(part, 'inner', [(k, (k + d) % inner) for k in range(inner)])  19.8 us
    pallas_call x1, Pallas kernels, op_ps(): call(last_kernel, 'op_ps', [SMEM] * 4 + [HBM] * 18 + [degree, x, p, image...  16.7 us
    pallas_call x1, Pallas kernels, op_x(): call(first_kernel, 'op_x', [SMEM] * 7 + [HBM] * 10 + [degree, p], out, [p...  15.3 us
    all_to_all x3, waiting for transfers between devices, exchange(): return lax.all_to_all(a, axes, split_axis=0, concat_axis=0, tiled=True)  14.9 us
    pallas_call x1, Pallas kernels, degree_of(): call(degree_kernel, 'degree', [SMEM, SMEM, HBM, shift], [jax.ShapeDtypeSt...  11.6 us
  transfers between devices with their start and end apart: 17, of which 9 were waited for; matrix products, arithmetic and copies ran while one was open for 1% of the time, Pallas kernels for 14%

profile of v5, /device:TPU:1, one launch (start us, length us, event | category | flops | bytes accessed | tf_op | source)
XLA Modules:
  0.0 211.1 jit_solution(1953774739969140966)
XLA Ops:
  0.6 3.4 %cut_x.1 = (bf16[16,32,256]{2,1,0:T(8,128)(2,1)}, bf16[8,32,256]{2,1,0:T(8,128)(2,1)}, bf16[8,32,256]{2,1,0:T(8,128)(2,1)}, bf16[8,32,256]{2,1,0:T(8,128)(2,1)},...) custom-call(s32[128]{0:T(128)} %bitcast.8, ...), custom_call_target="tpu_custom_call" | custom-call | bytes 1048576 | tf_op jit(solution)/shard_map/cut_x/pallas_call | solution.py:126
  4.0 11.5 %all-to-all-start = ((bf16[128,32,256]{2,1,0:T(8,128)(2,1)}), bf16[128,32,256]{2,1,0:T(8,128)(2,1)S(1)}, u32[]{:S(2)}, u32[]{:S(2)}) async-start(bf16[128,32,256]{2,1,0:T(8,128)(2,1)} %get-tuple-element.53), calls=%async_computation | async-start | bytes 4194304 | tf_op jit(solution)/shard_map/all_to_all | solution.py:415
  18.4 11.6 %degree.1.refs_17_.refs_22_ = f32[16,256]{1,0:T(8,128)} custom-call(s32[192]{0:T(256)} %refs_0_.1, s32[1]{0:T(128)S(6)} %copy.11.count_ref.refs_2_, bf16[192,256,256]{2,1,0:T(8,128)(2,1)} %refs_4_.1, f32[16,256]{1,0:T(8,128)} %reshape.54.shift_ref), custom_call_target="tpu_custom_call" | custom-call | flops 12000000000 | bytes 12582912 | tf_op jit(solution)/shard_map/degree/pallas_call | solution.py:96
  30.0 2.9 %collective-permute-start.4 = (bf16[8,32,256]{2,1,0:T(8,128)(2,1)S(1)}, bf16[8,32,256]{2,1,0:T(8,128)(2,1)S(1)}, u32[]{:S(2)}, u32[]{:S(2)}) collective-permute-start(bf16[8,32,256]{2,1,0:T(8,128)(2,1)S(1)} %copy-done.23), channel_id=1, source_target_pairs={{0,5},{1,6},{2,7},{3,0},{4,1},{5,2},{6,3},{7,4},{8,13},{9,14},{10,... | collective-permute-start | bytes 393224 | tf_op jit(solution)/shard_map/ppermute | solution.py:429
  36.1 8.6 %collective-permute-done.4.refs_13_.refs_9_ = bf16[8,32,256]{2,1,0:T(8,128)(2,1)S(1)} collective-permute-done((bf16[8,32,256]{2,1,0:T(8,128)(2,1)S(1)}, bf16[8,32,256]{2,1,0:T(8,128)(2,1)S(1)}, u32[]{:S(2)}, u32[]{:S(2)}) %collective-permute-start.4) | collective-permute-done | bytes 131104 | tf_op jit(solution)/shard_map/ppermute | solution.py:429
  45.1 2.4 %collective-permute-start.3 = (bf16[8,32,256]{2,1,0:T(8,128)(2,1)S(1)}, bf16[8,32,256]{2,1,0:T(8,128)(2,1)S(1)}, u32[]{:S(2)}, u32[]{:S(2)}) collective-permute-start(bf16[8,32,256]{2,1,0:T(8,128)(2,1)S(1)} %copy-done.17), channel_id=1, source_target_pairs={{0,4},{1,5},{2,6},{3,7},{4,0},{5,1},{6,2},{7,3},{8,12},{9,13},{10,... | collective-permute-start | bytes 393224 | tf_op jit(solution)/shard_map/ppermute | solution.py:429
  47.5 3.4 %cut_p.1 = (bf16[16,32,256]{2,1,0:T(8,128)(2,1)}, bf16[8,32,256]{2,1,0:T(8,128)(2,1)}, bf16[8,32,256]{2,1,0:T(8,128)(2,1)}, bf16[8,32,256]{2,1,0:T(8,128)(2,1)},...) custom-call(s32[128]{0:T(128)} %bitcast.9, ...), custom_call_target="tpu_custom_call" | custom-call | bytes 1048576 | tf_op jit(solution)/shard_map/cut_p/pallas_call | solution.py:126
  50.9 2.2 %collective-permute-done.2.refs_11_.refs_7_ = bf16[8,32,256]{2,1,0:T(8,128)(2,1)S(1)} collective-permute-done((bf16[8,32,256]{2,1,0:T(8,128)(2,1)S(1)}, bf16[8,32,256]{2,1,0:T(8,128)(2,1)S(1)}, u32[]{:S(2)}, u32[]{:S(2)}) %collective-permute-start.2) | collective-permute-done | bytes 131104 | tf_op jit(solution)/shard_map/ppermute | solution.py:429
  54.6 9.0 %all-to-all-start.1 = ((bf16[128,32,256]{2,1,0:T(8,128)(2,1)}), bf16[128,32,256]{2,1,0:T(8,128)(2,1)}, u32[]{:S(2)}, u32[]{:S(2)}) async-start(bf16[128,32,256]{2,1,0:T(8,128)(2,1)} %get-tuple-element.79), calls=%async_computation.1 | async-start | bytes 4194304 | tf_op jit(solution)/shard_map/all_to_all | solution.py:415
  63.6 15.3 %op_x.1 = (f32[16,32,256]{2,1,0:T(8,128)}, bf16[16,32,256]{2,1,0:T(8,128)(2,1)}, bf16[128,72,128]{2,1,0:T(8,128)(2,1)}, bf16[8,136,128]{2,1,0:T(8,128)(2,1)}, bf...) custom-call(s32[192]{0:T(256)} %refs_0_.1, ...), custom_call_target="tpu_custom_call" | custom-call | flops 12000000000 | bytes 12582912 | tf_op jit(solution)/shard_map/op_x/pallas_call | solution.py:229
  78.8 14.9 %all-to-all-done.1.refs_20_ = bf16[128,32,256]{2,1,0:T(8,128)(2,1)} async-done(((bf16[128,32,256]{2,1,0:T(8,128)(2,1)}), bf16[128,32,256]{2,1,0:T(8,128)(2,1)}, u32[]{:S(2)}, u32[]{:S(2)}) %all-to-all-start.1) | async-done | bytes 2097184 | tf_op jit(solution)/shard_map/all_to_all | solution.py:415
  93.8 4.5 %all-to-all-start.2 = ((bf16[128,72,128]{2,1,0:T(8,128)(2,1)}), bf16[128,72,128]{2,1,0:T(8,128)(2,1)S(1)}, u32[]{:S(2)}, u32[]{:S(2)}) async-start(bf16[128,72,128]{2,1,0:T(8,128)(2,1)} %get-tuple-element.95), calls=%async_computation.2 | async-start | bytes 4718592 | tf_op jit(solution)/shard_map/all_to_all | solution.py:415
  98.3 1.6 collective-permute-start.7
  101.1 1.7 collective-permute-start.9
  103.3 2.5 %collective-permute-start.11 = (bf16[8,136,128]{2,1,0:T(8,128)(2,1)}, bf16[8,136,128]{2,1,0:T(8,128)(2,1)S(1)}, u32[]{:S(2)}, u32[]{:S(2)}) collective-permute-start(bf16[8,136,128]{2,1,0:T(8,128)(2,1)} %get-tuple-element.91), channel_id=1, source_target_pairs={{0,5},{1,6},{2,7},{3,0},{4,1},{5,2},{6,3},{7,4},{8,13},{9,14},{10,... | collective-permute-start | bytes 835592 | tf_op jit(solution)/shard_map/ppermute | solution.py:429
  105.9 22.3 %collective-permute-done.7.refs_12_ = bf16[8,136,128]{2,1,0:T(8,128)(2,1)S(1)} collective-permute-done((bf16[8,136,128]{2,1,0:T(8,128)(2,1)}, bf16[8,136,128]{2,1,0:T(8,128)(2,1)S(1)}, u32[]{:S(2)}, u32[]{:S(2)}) %collective-permute-start.7) | collective-permute-done | bytes 278560 | tf_op jit(solution)/shard_map/ppermute | solution.py:429
  128.2 3.4 %collective-permute-start.12 = (bf16[8,136,128]{2,1,0:T(8,128)(2,1)}, bf16[8,136,128]{2,1,0:T(8,128)(2,1)S(1)}, u32[]{:S(2)}, u32[]{:S(2)}) collective-permute-start(bf16[8,136,128]{2,1,0:T(8,128)(2,1)} %get-tuple-element.92), channel_id=1, source_target_pairs={{0,6},{1,7},{2,0},{3,1},{4,2},{5,3},{6,4},{7,5},{8,14},{9,15},{10,... | collective-permute-start | bytes 835592 | tf_op jit(solution)/shard_map/ppermute | solution.py:429
  131.6 6.3 %collective-permute-done.8.refs_13_ = bf16[8,136,128]{2,1,0:T(8,128)(2,1)S(1)} collective-permute-done((bf16[8,136,128]{2,1,0:T(8,128)(2,1)}, bf16[8,136,128]{2,1,0:T(8,128)(2,1)S(1)}, u32[]{:S(2)}, u32[]{:S(2)}) %collective-permute-start.8) | collective-permute-done | bytes 278560 | tf_op jit(solution)/shard_map/ppermute | solution.py:429
  137.9 2.2 %collective-permute-done.9.refs_14_ = bf16[8,136,128]{2,1,0:T(8,128)(2,1)S(1)} collective-permute-done((bf16[8,136,128]{2,1,0:T(8,128)(2,1)}, bf16[8,136,128]{2,1,0:T(8,128)(2,1)S(1)}, u32[]{:S(2)}, u32[]{:S(2)}) %collective-permute-start.9) | collective-permute-done | bytes 278560 | tf_op jit(solution)/shard_map/ppermute | solution.py:429
  140.2 10.0 %collective-permute-done.10.refs_15_ = bf16[8,136,128]{2,1,0:T(8,128)(2,1)S(1)} collective-permute-done((bf16[8,136,128]{2,1,0:T(8,128)(2,1)}, bf16[8,136,128]{2,1,0:T(8,128)(2,1)S(1)}, u32[]{:S(2)}, u32[]{:S(2)}) %collective-permute-start.10) | collective-permute-done | bytes 278560 | tf_op jit(solution)/shard_map/ppermute | solution.py:429
  153.5 16.7 %op_ps.1 = (bf16[16,32,256]{2,1,0:T(8,128)(2,1)}, f32[128,1,144]{2,1,0:T(1,128)}) custom-call(s32[192]{0:T(256)} %refs_0_.1, s32[192]{0:T(256)} %refs_1_.3, s32[1]{0:T(128)S(6)} %copy.11.count_ref.refs_2_, s32[208]{0:T(256)} %pad_add_fusion.refs_3_, bf16[192,256,256]{2,1,0:T(8,128)(2,1)} %refs_4_.1, bf16[8,32,256]{2,1,0:T(8,128)(2,1)} %copy-done.13, ...), custom_call_target="tpu_custom_call" | custom-call | flops 12000000000 | bytes 12582912 | tf_op jit(solution)/shard_map/op_ps/pallas_call | solution.py:322
  170.3 17.1 %all_to_all.25 = f32[128,1,144]{2,1,0:T(1,128)S(1)} all-to-all(f32[128,1,144]{2,1,0:T(1,128)} %get-tuple-element.98), channel_id=1, replica_groups=mesh['comm'=16,'inner'=8] {'comm','inner'}, dimensions={0} | all-to-all | bytes 147456 | tf_op jit(solution)/shard_map/all_to_all | solution.py:415
  187.6 14.2 %all_to_all.26.sums_ref = f32[128,1,144]{2,1,0:T(1,128)} all-to-all(f32[128,1,144]{2,1,0:T(1,128)S(1)} %broadcast_in_dim.30), channel_id=1, replica_groups=mesh['comm'=16,'inner'=8] {'comm','inner'}, dimensions={0} | all-to-all | bytes 147456 | tf_op jit(solution)/shard_map/all_to_all | solution.py:415
  201.7 9.4 %ritz.1 = (f32[32,4096]{1,0:T(8,128)}, f32[32,4096]{1,0:T(8,128)}) custom-call(f32[128,1,144]{2,1,0:T(1,128)} %all_to_all.26.sums_ref, bf16[16,32,256]{2,1,0:T(8,128)(2,1)} %get-tuple-element.74.refs_8_.refs_23_.x_hbm, bf16[16,32,256]{2,1,0:T(8,128)(2,1)} %get-tuple-element.77.refs_18_.refs_24_.p_hbm, bf16[16,32,256]{2,1,0:T(8,128)(2,1)} %get-tuple-element.99.s_hbm), custom_call_target="tpu_custom_call" | custom-call | flops 4000000000 | bytes 2097152 | tf_op jit(solution)/shard_map/ritz/pallas_call | solution.py:407
  (77 shorter events, 12.4 us)
Async XLA Ops:
  4.0 49.2 %all-to-all-start = ((bf16[128,32,256]{2,1,0:T(8,128)(2,1)}), bf16[128,32,256]{2,1,0:T(8,128)(2,1)S(1)}, u32[]{:S(2)}, u32[]{:S(2)}) async-start(bf16[128,32,256]{2,1,0:T(8,128)(2,1)} %get-tuple-element.53), calls=%async_computation | async-start | bytes 4194304 | tf_op jit(solution)/shard_map/all_to_all | solution.py:415
  18.3 15.1 %copy-start.21 = (bf16[8,32,256]{2,1,0:T(8,128)(2,1)S(1)}, bf16[8,32,256]{2,1,0:T(8,128)(2,1)}, u32[]{:S(2)}) copy-start(bf16[8,32,256]{2,1,0:T(8,128)(2,1)} %get-tuple-element.63) | copy-start | bytes 393220
  18.3 16.2 %copy-start.20 = (bf16[8,32,256]{2,1,0:T(8,128)(2,1)S(1)}, bf16[8,32,256]{2,1,0:T(8,128)(2,1)}, u32[]{:S(2)}) copy-start(bf16[8,32,256]{2,1,0:T(8,128)(2,1)} %get-tuple-element.54) | copy-start | bytes 393220
  18.3 16.9 %copy-start.19 = (bf16[8,32,256]{2,1,0:T(8,128)(2,1)S(1)}, bf16[8,32,256]{2,1,0:T(8,128)(2,1)}, u32[]{:S(2)}) copy-start(bf16[8,32,256]{2,1,0:T(8,128)(2,1)} %get-tuple-element.55) | copy-start | bytes 393220
  18.3 26.4 %copy-start.18 = (bf16[8,32,256]{2,1,0:T(8,128)(2,1)S(1)}, bf16[8,32,256]{2,1,0:T(8,128)(2,1)}, u32[]{:S(2)}) copy-start(bf16[8,32,256]{2,1,0:T(8,128)(2,1)} %get-tuple-element.56) | copy-start | bytes 393220
  18.4 26.7 %copy-start.17 = (bf16[8,32,256]{2,1,0:T(8,128)(2,1)S(1)}, bf16[8,32,256]{2,1,0:T(8,128)(2,1)}, u32[]{:S(2)}) copy-start(bf16[8,32,256]{2,1,0:T(8,128)(2,1)} %get-tuple-element.57) | copy-start | bytes 393220
  30.0 14.8 %collective-permute-start.4 = (bf16[8,32,256]{2,1,0:T(8,128)(2,1)S(1)}, bf16[8,32,256]{2,1,0:T(8,128)(2,1)S(1)}, u32[]{:S(2)}, u32[]{:S(2)}) collective-permute-start(bf16[8,32,256]{2,1,0:T(8,128)(2,1)S(1)} %copy-done.23), channel_id=1, source_target_pairs={{0,5},{1,6},{2,7},{3,0},{4,1},{5,2},{6,3},{7,4},{8,13},{9,14},{10,... | collective-permute-start | bytes 393224 | tf_op jit(solution)/shard_map/ppermute | solution.py:429
  32.9 12.2 %collective-permute-start.5 = (bf16[8,32,256]{2,1,0:T(8,128)(2,1)S(1)}, bf16[8,32,256]{2,1,0:T(8,128)(2,1)S(1)}, u32[]{:S(2)}, u32[]{:S(2)}) collective-permute-start(bf16[8,32,256]{2,1,0:T(8,128)(2,1)S(1)} %copy-done.22), channel_id=1, source_target_pairs={{0,6},{1,7},{2,0},{3,1},{4,2},{5,3},{6,4},{7,5},{8,14},{9,15},{10,... | collective-permute-start | bytes 393224 | tf_op jit(solution)/shard_map/ppermute | solution.py:429
  33.4 17.4 %collective-permute-start.6 = (bf16[8,32,256]{2,1,0:T(8,128)(2,1)S(1)}, bf16[8,32,256]{2,1,0:T(8,128)(2,1)S(1)}, u32[]{:S(2)}, u32[]{:S(2)}) collective-permute-start(bf16[8,32,256]{2,1,0:T(8,128)(2,1)S(1)} %copy-done.21), channel_id=1, source_target_pairs={{0,7},{1,0},{2,1},{3,2},{4,3},{5,4},{6,5},{7,6},{8,15},{9,8},{10,9... | collective-permute-start | bytes 393224 | tf_op jit(solution)/shard_map/ppermute | solution.py:429
  34.5 16.4 %collective-permute-start = (bf16[8,32,256]{2,1,0:T(8,128)(2,1)S(1)}, bf16[8,32,256]{2,1,0:T(8,128)(2,1)S(1)}, u32[]{:S(2)}, u32[]{:S(2)}) collective-permute-start(bf16[8,32,256]{2,1,0:T(8,128)(2,1)S(1)} %copy-done.20), channel_id=1, source_target_pairs={{0,1},{1,2},{2,3},{3,4},{4,5},{5,6},{6,7},{7,0},{8,9},{9,10},{10,1... | collective-permute-start | bytes 393224 | tf_op jit(solution)/shard_map/ppermute | solution.py:429
  35.2 15.7 %collective-permute-start.1 = (bf16[8,32,256]{2,1,0:T(8,128)(2,1)S(1)}, bf16[8,32,256]{2,1,0:T(8,128)(2,1)S(1)}, u32[]{:S(2)}, u32[]{:S(2)}) collective-permute-start(bf16[8,32,256]{2,1,0:T(8,128)(2,1)S(1)} %copy-done.19), channel_id=1, source_target_pairs={{0,2},{1,3},{2,4},{3,5},{4,6},{5,7},{6,0},{7,1},{8,10},{9,11},{10,... | collective-permute-start | bytes 393224 | tf_op jit(solution)/shard_map/ppermute | solution.py:429
  44.7 8.4 %collective-permute-start.2 = (bf16[8,32,256]{2,1,0:T(8,128)(2,1)S(1)}, bf16[8,32,256]{2,1,0:T(8,128)(2,1)S(1)}, u32[]{:S(2)}, u32[]{:S(2)}) collective-permute-start(bf16[8,32,256]{2,1,0:T(8,128)(2,1)S(1)} %copy-done.18), channel_id=1, source_target_pairs={{0,3},{1,4},{2,5},{3,6},{4,7},{5,0},{6,1},{7,2},{8,11},{9,12},{10,... | collective-permute-start | bytes 393224 | tf_op jit(solution)/shard_map/ppermute | solution.py:429
  45.1 8.1 %collective-permute-start.3 = (bf16[8,32,256]{2,1,0:T(8,128)(2,1)S(1)}, bf16[8,32,256]{2,1,0:T(8,128)(2,1)S(1)}, u32[]{:S(2)}, u32[]{:S(2)}) collective-permute-start(bf16[8,32,256]{2,1,0:T(8,128)(2,1)S(1)} %copy-done.17), channel_id=1, source_target_pairs={{0,4},{1,5},{2,6},{3,7},{4,0},{5,1},{6,2},{7,3},{8,12},{9,13},{10,... | collective-permute-start | bytes 393224 | tf_op jit(solution)/shard_map/ppermute | solution.py:429
  54.6 39.2 %all-to-all-start.1 = ((bf16[128,32,256]{2,1,0:T(8,128)(2,1)}), bf16[128,32,256]{2,1,0:T(8,128)(2,1)}, u32[]{:S(2)}, u32[]{:S(2)}) async-start(bf16[128,32,256]{2,1,0:T(8,128)(2,1)} %get-tuple-element.79), calls=%async_computation.1 | async-start | bytes 4194304 | tf_op jit(solution)/shard_map/all_to_all | solution.py:415
  93.7 44.2 %copy-start.6 = (bf16[8,136,128]{2,1,0:T(8,128)(2,1)S(1)}, bf16[8,136,128]{2,1,0:T(8,128)(2,1)}, u32[]{:S(2)}) copy-start(bf16[8,136,128]{2,1,0:T(8,128)(2,1)} %get-tuple-element.93) | copy-start | bytes 835588
  93.8 58.3 %all-to-all-start.2 = ((bf16[128,72,128]{2,1,0:T(8,128)(2,1)}), bf16[128,72,128]{2,1,0:T(8,128)(2,1)S(1)}, u32[]{:S(2)}, u32[]{:S(2)}) async-start(bf16[128,72,128]{2,1,0:T(8,128)(2,1)} %get-tuple-element.95), calls=%async_computation.2 | async-start | bytes 4718592 | tf_op jit(solution)/shard_map/all_to_all | solution.py:415
  98.3 29.9 %collective-permute-start.7 = (bf16[8,136,128]{2,1,0:T(8,128)(2,1)}, bf16[8,136,128]{2,1,0:T(8,128)(2,1)S(1)}, u32[]{:S(2)}, u32[]{:S(2)}) collective-permute-start(bf16[8,136,128]{2,1,0:T(8,128)(2,1)} %get-tuple-element.87), channel_id=1, source_target_pairs={{0,1},{1,2},{2,3},{3,4},{4,5},{5,6},{6,7},{7,0},{8,9},{9,10},{10,1... | collective-permute-start | bytes 835592 | tf_op jit(solution)/shard_map/ppermute | solution.py:429
  99.9 38.0 %collective-permute-start.8 = (bf16[8,136,128]{2,1,0:T(8,128)(2,1)}, bf16[8,136,128]{2,1,0:T(8,128)(2,1)S(1)}, u32[]{:S(2)}, u32[]{:S(2)}) collective-permute-start(bf16[8,136,128]{2,1,0:T(8,128)(2,1)} %get-tuple-element.88), channel_id=1, source_target_pairs={{0,2},{1,3},{2,4},{3,5},{4,6},{5,7},{6,0},{7,1},{8,10},{9,11},{10,... | collective-permute-start | bytes 835592 | tf_op jit(solution)/shard_map/ppermute | solution.py:429
  101.1 39.0 %collective-permute-start.9 = (bf16[8,136,128]{2,1,0:T(8,128)(2,1)}, bf16[8,136,128]{2,1,0:T(8,128)(2,1)S(1)}, u32[]{:S(2)}, u32[]{:S(2)}) collective-permute-start(bf16[8,136,128]{2,1,0:T(8,128)(2,1)} %get-tuple-element.89), channel_id=1, source_target_pairs={{0,3},{1,4},{2,5},{3,6},{4,7},{5,0},{6,1},{7,2},{8,11},{9,12},{10,... | collective-permute-start | bytes 835592 | tf_op jit(solution)/shard_map/ppermute | solution.py:429
  102.8 47.4 %collective-permute-start.10 = (bf16[8,136,128]{2,1,0:T(8,128)(2,1)}, bf16[8,136,128]{2,1,0:T(8,128)(2,1)S(1)}, u32[]{:S(2)}, u32[]{:S(2)}) collective-permute-start(bf16[8,136,128]{2,1,0:T(8,128)(2,1)} %get-tuple-element.90), channel_id=1, source_target_pairs={{0,4},{1,5},{2,6},{3,7},{4,0},{5,1},{6,2},{7,3},{8,12},{9,13},{10,... | collective-permute-start | bytes 835592 | tf_op jit(solution)/shard_map/ppermute | solution.py:429
  103.3 47.3 %collective-permute-start.11 = (bf16[8,136,128]{2,1,0:T(8,128)(2,1)}, bf16[8,136,128]{2,1,0:T(8,128)(2,1)S(1)}, u32[]{:S(2)}, u32[]{:S(2)}) collective-permute-start(bf16[8,136,128]{2,1,0:T(8,128)(2,1)} %get-tuple-element.91), channel_id=1, source_target_pairs={{0,5},{1,6},{2,7},{3,0},{4,1},{5,2},{6,3},{7,4},{8,13},{9,14},{10,... | collective-permute-start | bytes 835592 | tf_op jit(solution)/shard_map/ppermute | solution.py:429
  128.2 23.9 %copy-start.3 = (bf16[8,136,128]{2,1,0:T(8,128)(2,1)}, bf16[8,136,128]{2,1,0:T(8,128)(2,1)S(1)}, u32[]{:S(2)}) copy-start(bf16[8,136,128]{2,1,0:T(8,128)(2,1)S(1)} %collective-permute-done.7.refs_12_) | copy-start | bytes 835588
  128.2 22.4 %collective-permute-start.12 = (bf16[8,136,128]{2,1,0:T(8,128)(2,1)}, bf16[8,136,128]{2,1,0:T(8,128)(2,1)S(1)}, u32[]{:S(2)}, u32[]{:S(2)}) collective-permute-start(bf16[8,136,128]{2,1,0:T(8,128)(2,1)} %get-tuple-element.92), channel_id=1, source_target_pairs={{0,6},{1,7},{2,0},{3,1},{4,2},{5,3},{6,4},{7,5},{8,14},{9,15},{10,... | collective-permute-start | bytes 835592 | tf_op jit(solution)/shard_map/ppermute | solution.py:429
  137.9 14.1 %collective-permute-start.13 = (bf16[8,136,128]{2,1,0:T(8,128)(2,1)S(1)}, bf16[8,136,128]{2,1,0:T(8,128)(2,1)}, u32[]{:S(2)}, u32[]{:S(2)}) collective-permute-start(bf16[8,136,128]{2,1,0:T(8,128)(2,1)S(1)} %copy-done.6), channel_id=1, source_target_pairs={{0,7},{1,0},{2,1},{3,2},{4,3},{5,4},{6,5},{7,6},{8,15},{9,8},{10,9... | collective-permute-start | bytes 835592 | tf_op jit(solution)/shard_map/ppermute | solution.py:429
  (17 other events, 95.8 us)
